TPU v7x, 256 devices: a whole 4x4x8 slice. The times are simulated.
256 devices in a mesh: dp: 8 (over z_hi, core), row: 4 (over y), col: 8 (over z_lo, x).
Axes of the slice: x: 4, y: 4, z: 8 (z_hi: 4, z_lo: 2; z = z_hi * 2 + z_lo), core: 2. Of those that a mesh axis runs over, the one named last changes fastest.
Arguments:
- tokens: bfloat16 [2048, 8192], P(('dp', 'col'), 'row'), may hold values from -6 to 6
- cotangent: bfloat16 [2048, 8192], P(('dp', 'col'), 'row'), may hold values from -6 to 6
- weight: bfloat16 [8192, 16384], P('row', 'col'), may hold values from -0.125 to 0.125
- block_mask: int32 [32, 64], P('row', 'col'), may hold values 0 or 1
Outputs:
- output: bfloat16 [2048, 8192], P(('dp', 'col'), 'row')
- input_grad: bfloat16 [2048, 8192], P(('dp', 'col'), 'row')
- weight_grad: float32 [8192, 8, 2048], P('row', 'dp', 'col')
Inputs may be any that keep to these rules, and one draw needn't show every extreme that they name: block_mask holds only 0 and 1.
All inputs are finite; a program needn't handle non-finite values. No bound on the sum of `block_mask` on one device may be relied on, other than what follows from the above.
Results may differ from a plain program's by a relative error of at most 0.0032.
Values may be sent and summed in bfloat16 or wider, within the bound.
No kernel may reach another device: no remote copies, remote signals or barrier semaphores. Data moves between devices by JAX's collectives and lax.ppermute only.
A program may use at most 128 MiB of HBM per device.

v0:
```python
import math

import jax
import jax.numpy as jnp
from jax import lax
from jax.sharding import PartitionSpec as P

BLOCK = 256


def expand_mask(block_mask):
    kept_blocks = block_mask.astype(jnp.bfloat16)
    return jnp.repeat(jnp.repeat(kept_blocks, BLOCK, axis=0), BLOCK, axis=1)


def slope_times(grad_hidden, pre):
    sigmoid_pre = jax.nn.sigmoid(pre)
    return (grad_hidden * sigmoid_pre * (1.0 + pre * (1.0 - sigmoid_pre))).astype(jnp.bfloat16)


def times_transpose(left, masked):
    return lax.dot_general(
        left, masked, (((1,), (1,)), ((), ())), preferred_element_type=jnp.float32
    )


def on_device(tokens, cotangent, weight, block_mask):
    kept = expand_mask(block_mask)
    masked = weight * kept
    tok_count = tokens.shape[0]
    tok_rows, cot_rows = (
        lax.all_gather(tokens, "col", axis=0, tiled=True),
        lax.all_gather(cotangent, "col", axis=0, tiled=True),
    )
    pre_part = jnp.dot(tok_rows, masked, preferred_element_type=jnp.float32)
    pre = lax.psum(pre_part, "row")
    hidden = jax.nn.silu(pre).astype(jnp.bfloat16)
    grad_part = jnp.dot(cot_rows, masked, preferred_element_type=jnp.float32)
    grad_hidden = lax.psum(grad_part, "row")
    grad_pre = slope_times(grad_hidden, pre)
    projected = lax.psum_scatter(
        times_transpose(hidden, masked), "col", scatter_dimension=0, tiled=True
    )
    output = (tokens.astype(jnp.float32) + projected).astype(jnp.bfloat16)
    back = lax.psum_scatter(
        times_transpose(grad_pre, masked), "col", scatter_dimension=0, tiled=True
    )
    input_grad = (cotangent.astype(jnp.float32) + back).astype(jnp.bfloat16)
    tok_total = tok_count * lax.axis_size("col") * lax.axis_size("dp")
    norm_scale = 1.0 / math.sqrt(tok_total)
    feat_rows = masked.shape[0]
    share_cols = masked.shape[1] // lax.axis_size("dp")
    hid_share = hidden.reshape(hidden.shape[0], 1 * lax.axis_size("dp"), share_cols)
    pre_grad_share = grad_pre.reshape(grad_pre.shape[0], 1 * lax.axis_size("dp"), share_cols)
    kept_share = kept.reshape(feat_rows, 1 * lax.axis_size("dp"), share_cols)
    partial_value = jnp.einsum(
        "td,tcj->cdj", cot_rows, hid_share, preferred_element_type=jnp.float32
    )
    partial_value = partial_value + jnp.einsum(
        "td,tcj->cdj", tok_rows, pre_grad_share, preferred_element_type=jnp.float32
    )
    summed = lax.psum_scatter(
        partial_value * jnp.moveaxis(kept_share, 1, 0).astype(jnp.float32) * norm_scale,
        "dp",
        scatter_dimension=0,
        tiled=True,
    )
    weight_grad = summed.reshape(feat_rows, 1, share_cols)
    return (output, input_grad, weight_grad)


def solution(mesh):
    in_specs = (P(("dp", "col"), "row"), P(("dp", "col"), "row"), P("row", "col"), P("row", "col"))
    out_specs = (P(("dp", "col"), "row"), P(("dp", "col"), "row"), P("row", "dp", "col"))
    return jax.shard_map(
        on_device, mesh=mesh, in_specs=in_specs, out_specs=out_specs, check_vma=False
    )
```

profile of v0, /device:TPU:1, one launch (start us, length us, event | category | flops | bytes accessed | tf_op | source)
XLA Modules:
  0.0 498.7 jit_solution(5643806620404390744)
XLA Ops:
  7.2 0.0 all-gather.3.cloned.1.call-start
  7.2 0.7 all-gather.3.cloned.1.call-update
  7.9 0.0 all-gather.5.cloned.1.call-start
  7.9 0.7 all-gather.5.cloned.1.call-update
  8.6 0.0 all-reduce.3.cloned.1.call-start
  8.7 0.7 convert_element_type.29
  9.4 0.1 broadcast_in_dim.8
  9.5 0.3 copy.7
  9.7 4.5 broadcast_in_dim.9
  14.3 10.3 %copy.9 = bf16[256,8,8,256]{3,1,2,0:T(8,128)(2,1)} copy(bf16[256,8,8,256]{3,2,1,0:T(8,128)(2,1)} %bitcast.33) | data formatting | bytes 16777216
  24.6 10.5 %mul.25 = bf16[2048,2048]{1,0:T(8,128)(2,1)} multiply(bf16[2048,2048]{1,0:T(8,128)(2,1)} %param.6, bf16[2048,2048]{1,0:T(8,128)(2,1)} %bitcast.32) | non-fusion elementwise | flops 4194304 | bytes 25165824 | tf_op jit(solution)/shard_map/mul | solution.py:29
  35.1 15.0 %all-gather.3.cloned.1.call-done = bf16[256,2048]{1,0:T(8,128)(2,1)} async-done(((bf16[32,2048]{1,0:T(8,128)(2,1)}), bf16[256,2048]{1,0:T(8,128)(2,1)}) %all-gather.3.cloned.1.call-update) | async-done | bytes 1048592 | tf_op jit(solution)/shard_map/all_gather | solution.py:32
  50.1 7.4 %convolution_bitcast_fusion.1 = f32[256,2048]{0,1:T(8,128)} fusion(bf16[2048,2048]{1,0:T(8,128)(2,1)} %mul.25, bf16[256,2048]{1,0:T(8,128)(2,1)} %all-gather.3.cloned.1.call-done), kind=kOutput, calls=%fused_computation.3 | convolution fusion | flops 2147483648 | bytes 11534336 | tf_op jit(solution)/shard_map/dot_general | solution.py:35
  57.5 35.0 %all-gather.5.cloned.1.call-done = bf16[256,2048]{1,0:T(8,128)(2,1)} async-done(((bf16[32,2048]{1,0:T(8,128)(2,1)}), bf16[256,2048]{1,0:T(8,128)(2,1)}) %all-gather.5.cloned.1.call-update) | async-done | bytes 1048592 | tf_op jit(solution)/shard_map/all_gather | solution.py:33
  92.5 7.4 %convolution_bitcast_fusion = f32[256,2048]{0,1:T(8,128)} fusion(bf16[2048,2048]{1,0:T(8,128)(2,1)} %mul.25, bf16[256,2048]{1,0:T(8,128)(2,1)} %all-gather.5.cloned.1.call-done), kind=kOutput, calls=%fused_computation.2 | convolution fusion | flops 2147483648 | bytes 11534336 | tf_op jit(solution)/shard_map/dot_general | solution.py:38
  99.9 0.0 all-reduce.3.cloned.1.call-update
  99.9 0.2 reduce-scatter.4.cloned.1.call-start
  100.2 102.2 %all-reduce.3.cloned.1.call-done = (f32[256,2048]{0,1:T(8,128)}, f32[256,2048]{0,1:T(8,128)}) async-done(((f32[256,2048]{0,1:T(8,128)}, f32[256,2048]{0,1:T(8,128)}), (f32[256,2048]{0,1:T(8,128)}, f32[256,2048]{0,1:T(8,128)})) %all-reduce.3.cloned.1.call-update) | async-done | bytes 4194320 | tf_op jit(solution)/shard_map/psum | solution.py:36
  202.4 3.1 multiply_convert_fusion
  205.4 7.2 %fusion.4 = f32[256,2048]{1,0:T(8,128)} fusion(bf16[256,2048]{0,1:T(8,128)(2,1)S(1)} %get-tuple-element.9, bf16[2048,2048]{1,0:T(8,128)(2,1)} %mul.25), kind=kOutput, calls=%fused_computation.12 | convolution fusion | flops 2147483648 | bytes 11534336 | tf_op jit(solution)/shard_map/dot_general | solution.py:22
  212.6 0.0 reduce-scatter.4.cloned.1.call-update
  212.7 0.0 reduce-scatter.6.cloned.1.call-start
  212.7 7.2 %fusion.5 = f32[256,2048]{1,0:T(8,128)} fusion(bf16[256,2048]{0,1:T(8,128)(2,1)S(1)} %get-tuple-element.8, bf16[2048,2048]{1,0:T(8,128)(2,1)} %mul.25), kind=kOutput, calls=%fused_computation.13 | convolution fusion | flops 2147483648 | bytes 11534336 | tf_op jit(solution)/shard_map/dot_general | solution.py:22
  219.9 0.0 reduce-scatter.6.cloned.1.call-update
  219.9 0.0 reduce-scatter.8.cloned.1.call-start
  220.0 3.6 fusion.2
  223.6 8.4 %fusion = f32[8,2048,256]{1,2,0:T(8,128)} fusion(f32[8,256,2048]{2,1,0:T(8,128)S(1)} %fusion.2, f32[2048,8]{0,1:T(8,128)S(1)} %convert_element_type.35, bf16[256,8,256]{0,2,1:T(8,128)(2,1)S(1)} %bitcast.35, bf16[256,2048]{1,0:T(8,128)(2,1)} %all-gather.3.cloned.1.call-done), kind=kOutput, calls=%fused_computation.1 | convolution fusion | flops 2160066560 | bytes 35717120 | tf_op jit(solution)/shard_map/td,tcj->cdj/dot_general | solution.py:59
  232.0 0.0 copy-start
  232.0 0.0 copy-start.1
  232.0 0.0 reduce-scatter.8.cloned.1.call-update
  232.0 20.6 %reduce-scatter.4.cloned.1.call-done = f32[32,2048]{1,0:T(8,128)} async-done(((f32[256,2048]{1,0:T(8,128)}), f32[32,2048]{1,0:T(8,128)}) %reduce-scatter.4.cloned.1.call-update) | async-done | bytes 262160 | tf_op jit(solution)/shard_map/reduce_scatter | solution.py:41
  252.6 0.0 copy-done
  252.6 1.6 add_convert_fusion.1
  254.2 45.1 %reduce-scatter.6.cloned.1.call-done = f32[32,2048]{1,0:T(8,128)} async-done(((f32[256,2048]{1,0:T(8,128)}), f32[32,2048]{1,0:T(8,128)}) %reduce-scatter.6.cloned.1.call-update) | async-done | bytes 262160 | tf_op jit(solution)/shard_map/reduce_scatter | solution.py:45
  299.4 0.0 copy-done.1
  299.4 1.6 add_convert_fusion
  301.0 184.8 %reduce-scatter.8.cloned.1.call-done = f32[1,2048,256]{1,2,0:T(8,128)} async-done(((f32[8,2048,256]{1,2,0:T(8,128)}), f32[1,2048,256]{1,2,0:T(8,128)}) %reduce-scatter.8.cloned.1.call-update) | async-done | bytes 2097168 | tf_op jit(solution)/shard_map/reduce_scatter | solution.py:62
  485.8 6.0 %copy.8 = f32[2048,1,256]{2,1,0:T(1,128)} copy(f32[2048,1,256]{0,2,1:T(8,128)} %bitcast.36) | data formatting | bytes 4194304
  (1 shorter events, 0.0 us)
Async XLA Ops:
  7.2 42.9 %all-gather.3.cloned.1.call-start = ((), (), s32[]{:S(2)}) async-start(), calls=%async_computation.3 | async-start | bytes 1179648 | tf_op jit(solution)/shard_map/all_gather | solution.py:32
  7.9 84.6 %all-gather.5.cloned.1.call-start = ((), (), s32[]{:S(2)}) async-start(), calls=%async_computation.5 | async-start | bytes 1179648 | tf_op jit(solution)/shard_map/all_gather | solution.py:33
  8.6 193.7 %all-reduce.3.cloned.1.call-start = ((), (), s32[]{:S(2)}) async-start(), calls=%async_computation.8 | async-start | bytes 8388608 | tf_op jit(solution)/shard_map/psum | solution.py:36
  99.9 152.7 %reduce-scatter.4.cloned.1.call-start = ((), (), s32[]{:S(2)}) async-start(), calls=%async_computation.4 | async-start | bytes 2359296 | tf_op jit(solution)/shard_map/reduce_scatter | solution.py:41
  212.7 86.7 %reduce-scatter.6.cloned.1.call-start = ((), (), s32[]{:S(2)}) async-start(), calls=%async_computation.6 | async-start | bytes 2359296 | tf_op jit(solution)/shard_map/reduce_scatter | solution.py:45
  219.9 265.9 %reduce-scatter.8.cloned.1.call-start = ((), (), s32[]{:S(2)}) async-start(), calls=%async_computation.7 | async-start | bytes 18874368 | tf_op jit(solution)/shard_map/reduce_scatter | solution.py:62
  232.0 20.6 %copy-start = (bf16[32,2048]{1,0:T(8,128)(2,1)S(1)}, bf16[32,2048]{1,0:T(8,128)(2,1)}, u32[]{:S(2)}) copy-start(bf16[32,2048]{1,0:T(8,128)(2,1)} %param.4) | copy-start | bytes 393220
  232.0 67.4 %copy-start.1 = (bf16[32,2048]{1,0:T(8,128)(2,1)S(1)}, bf16[32,2048]{1,0:T(8,128)(2,1)}, u32[]{:S(2)}) copy-start(bf16[32,2048]{1,0:T(8,128)(2,1)} %param.5) | copy-start | bytes 393220
Sparse Core Ops, SparseCore 0:
  9.8 40.2 all-gather.2
  51.9 40.5 all-gather.4
  100.1 102.2 all-reduce.2
  212.8 39.7 reduce-scatter.3
  255.2 44.1 reduce-scatter.5
  302.0 183.7 reduce-scatter.7
where the time goes:
time: 501 us; the launch traced here: 499 us
  waiting for transfers between devices  404 us (81%)
  matrix products  41.3 us (8%)
  local copies, waits for them, and re-layouts  21.2 us (4%)
  other arithmetic  17.5 us (3%)
  between operations  14.1 us (3%)
    reduce_scatter x1, waiting for transfers between devices, on_device(): lax.psum_scatter(partial_value * jnp.moveaxis(kept_share, 1, 0).astype(jn...  185 us
    psum x1, waiting for transfers between devices, on_device(): pre = lax.psum(pre_part, 'row')  102 us
    reduce_scatter x1, waiting for transfers between devices, on_device(): lax.psum_scatter(times_transpose(grad_pre, masked), 'col', scatter_dimens...  45.1 us
    all_gather x1, waiting for transfers between devices, on_device(): lax.all_gather(cotangent, 'col', axis=0, tiled=True)  35 us
    reduce_scatter x1, waiting for transfers between devices, on_device(): lax.psum_scatter(times_transpose(hidden, masked), 'col', scatter_dimensio...  20.6 us
    unnamed x6, local copies, waits for them, and re-layouts  16.3 us
    all_gather x1, waiting for transfers between devices, on_device(): lax.all_gather(tokens, 'col', axis=0, tiled=True)  15 us
    dot_general x2, matrix products, times_transpose(): lax.dot_general(left, masked, (((1,), (1,)), ((), ())), preferred_element...  14.4 us
  transfers between devices with their start and end apart: 6, of which 6 were waited for; matrix products, arithmetic and copies ran while one was open for 11% of the time, Pallas kernels for 0%

commit v1 on v0

v1 whole, which is shorter than its diff:
```python
import functools
import math

import jax
import jax.numpy as jnp
from jax import lax
from jax.experimental import pallas as pl
from jax.experimental.pallas import tpu as pltpu
from jax.sharding import PartitionSpec as P

BLOCK = 256
VMEM_LIMIT = 56 * 1024 * 1024
SMEM_SPEC = pl.BlockSpec(memory_space=pltpu.SMEM)
BF16, F32 = jnp.bfloat16, jnp.float32


def shift(value, axis, by):
    size = lax.axis_size(axis)
    return lax.ppermute(value, axis, [(i, (i + by) % size) for i in range(size)])


def params(steps=1):
    return pltpu.CompilerParams(
        vmem_limit_bytes=VMEM_LIMIT, dimension_semantics=("arbitrary",) * steps
    )


def masked_copy(mask_ref, w_ref, out_ref, row0, col0):
    for i in range(w_ref.shape[0] // BLOCK):
        for j in range(w_ref.shape[1] // BLOCK):
            part = (pl.ds(i * BLOCK, BLOCK), pl.ds(j * BLOCK, BLOCK))
            kept = mask_ref[row0 + i, col0 + j] != 0
            out_ref[part] = jnp.where(kept, w_ref[part], jnp.zeros((BLOCK, BLOCK), BF16))


def up_kernel(n_col, n_row, pos_ref, mask_ref, *refs):
    parts, w_ref = refs[:n_col], refs[n_col]
    own_ref, sends = refs[n_col + 1], refs[n_col + 2 : n_col + 1 + n_row]
    x_ref, wm_ref, acc_ref = refs[-3:]
    rows = parts[0].shape[1]
    tok = rows * n_col
    step = pl.program_id(0)

    @pl.when(step == 0)
    def _():
        for t in range(2):
            for j in range(n_col):
                x_ref[pl.ds(t * tok + j * rows, rows), :] = parts[j][t]

    masked_copy(mask_ref, w_ref, wm_ref, 0, step * (w_ref.shape[1] // BLOCK))
    acc_ref[...] = jnp.dot(x_ref[...], wm_ref[...], preferred_element_type=F32)
    share = tok // n_row
    me = pos_ref[0]
    for t in range(2):
        for k in range(n_row):
            first = pl.multiple_of(t * tok + lax.rem(me + k, n_row) * share, share)
            value = acc_ref[pl.ds(first, share), :]
            if k == 0:
                own_ref[t] = value
            else:
                sends[k - 1][t] = value.astype(BF16)


def up(pos, mask, parts, weight, n_row, width=512):
    n_col, (_, rows, depth) = len(parts), parts[0].shape
    cols = weight.shape[1]
    tok = rows * n_col
    share = tok // n_row
    return pl.pallas_call(
        functools.partial(up_kernel, n_col, n_row),
        grid=(cols // width,),
        in_specs=[SMEM_SPEC, SMEM_SPEC]
        + [pl.BlockSpec((2, rows, depth), lambda n: (0, 0, 0))] * n_col
        + [pl.BlockSpec((depth, width), lambda n: (0, n))],
        out_specs=[pl.BlockSpec((2, share, width), lambda n: (0, 0, n))] * n_row,
        out_shape=[jax.ShapeDtypeStruct((2, share, cols), F32)]
        + [jax.ShapeDtypeStruct((2, share, cols), BF16)] * (n_row - 1),
        scratch_shapes=[
            pltpu.VMEM((2 * tok, depth), BF16),
            pltpu.VMEM((depth, width), BF16),
            pltpu.VMEM((2 * tok, width), F32),
        ],
        compiler_params=params(),
        name="up",
    )(pos, mask, *parts, weight)


def act_kernel(n_row, n_z, pos_ref, *refs):
    own_ref, recv = refs[0], refs[1:n_row]
    both_ref, pieces = refs[n_row], refs[n_row + 1 :]
    pre = own_ref[0]
    grad_hidden = own_ref[1]
    for ref in recv:
        pre = pre + ref[0].astype(F32)
        grad_hidden = grad_hidden + ref[1].astype(F32)
    sig = jax.nn.sigmoid(pre)
    both_ref[0] = (pre * sig).astype(BF16)
    both_ref[1] = (grad_hidden * sig * (1.0 + pre * (1.0 - sig))).astype(BF16)
    width = both_ref.shape[2] // n_z
    for k in range(n_z):
        first = pl.multiple_of(lax.rem(pos_ref[1] + k, n_z) * width, width)
        for t in range(2):
            pieces[k][t] = both_ref[t, :, pl.ds(first, width)]


def act(pos, own, recv, n_z):
    _, share, cols = own.shape
    return pl.pallas_call(
        functools.partial(act_kernel, len(recv) + 1, n_z),
        in_specs=[SMEM_SPEC] + [pl.BlockSpec(memory_space=pltpu.VMEM)] * (len(recv) + 1),
        out_specs=[pl.BlockSpec(memory_space=pltpu.VMEM)] * (n_z + 1),
        out_shape=[jax.ShapeDtypeStruct((2, share, cols), BF16)]
        + [jax.ShapeDtypeStruct((2, share, cols // n_z), BF16)] * n_z,
        compiler_params=params(0),
        name="act",
    )(pos, own, *recv)


def down_kernel(n_col, n_row, pos_ref, mask_ref, *refs):
    parts, w_ref = refs[:n_row], refs[n_row]
    own_ref, sends = refs[n_row + 1], refs[n_row + 2 : n_row + 1 + n_col]
    x_ref, wm_ref, acc_ref = refs[-3:]
    share = parts[0].shape[1]
    tok = share * n_row
    step = pl.program_id(0)

    @pl.when(step == 0)
    def _():
        for t in range(2):
            for k in range(n_row):
                owner = lax.rem(pos_ref[0] + n_row - k, n_row)
                first = pl.multiple_of(t * tok + owner * share, share)
                x_ref[pl.ds(first, share), :] = parts[k][t]

    masked_copy(mask_ref, w_ref, wm_ref, step * (w_ref.shape[0] // BLOCK), 0)
    acc_ref[...] = lax.dot_general(
        x_ref[...], wm_ref[...], (((1,), (1,)), ((), ())), preferred_element_type=F32
    )
    rows = tok // n_col
    for t in range(2):
        own_ref[t] = acc_ref[pl.ds(t * tok, rows), :]
        for j in range(1, n_col):
            sends[j - 1][t] = acc_ref[pl.ds(t * tok + j * rows, rows), :].astype(BF16)


def down(pos, mask, parts, weight, n_col, width=512):
    n_row, (_, share, depth) = len(parts), parts[0].shape
    feats = weight.shape[0]
    tok = share * n_row
    rows = tok // n_col
    return pl.pallas_call(
        functools.partial(down_kernel, n_col, n_row),
        grid=(feats // width,),
        in_specs=[SMEM_SPEC, SMEM_SPEC]
        + [pl.BlockSpec((2, share, depth), lambda n: (0, 0, 0))] * n_row
        + [pl.BlockSpec((width, depth), lambda n: (n, 0))],
        out_specs=[pl.BlockSpec((2, rows, width), lambda n: (0, 0, n))] * n_col,
        out_shape=[jax.ShapeDtypeStruct((2, rows, feats), F32)]
        + [jax.ShapeDtypeStruct((2, rows, feats), BF16)] * (n_col - 1),
        scratch_shapes=[
            pltpu.VMEM((2 * tok, depth), BF16),
            pltpu.VMEM((width, depth), BF16),
            pltpu.VMEM((2 * tok, width), F32),
        ],
        compiler_params=params(),
        name="down",
    )(pos, mask, *parts, weight)


def grad_kernel(n_col, n_row, n_z, half, pos_ref, *refs):
    near, far = refs[:n_col], refs[n_col : 2 * n_col]
    hidden = refs[2 * n_col : 2 * n_col + n_row]
    out_ref, x_ref, h_ref = refs[-3:]
    rows = near[0].shape[1]
    share = hidden[0].shape[2]
    tok = rows * n_col

    @pl.when(pl.program_id(0) == 0)
    def _():
        side = pos_ref[2] if half == 0 else 1 - pos_ref[2]
        first_col = pl.multiple_of(side * BLOCK, BLOCK)
        for k in range(n_row):
            owner = lax.rem(pos_ref[0] + n_row - k, n_row)
            for z in range(n_z):
                first = pl.multiple_of(z * tok + owner * share, share)
                for t in range(2):
                    h_ref[t, pl.ds(first, share), :] = hidden[k][z, t, :, pl.ds(first_col, BLOCK)]

    for t in range(2):
        for j in range(n_col):
            x_ref[t, pl.ds(j * rows, rows), :] = near[j][t]
            for z in range(1, n_z):
                x_ref[t, pl.ds(z * tok + j * rows, rows), :] = far[j][z - 1, t]
    over_tokens = (((0,), (0,)), ((), ()))
    total = lax.dot_general(x_ref[1], h_ref[0], over_tokens, preferred_element_type=F32)
    total += lax.dot_general(x_ref[0], h_ref[1], over_tokens, preferred_element_type=F32)
    out_ref[...] = total


def grad(pos, near, far, hidden, half, width=512):
    n_col, n_row = len(near), len(hidden)
    _, rows, feats = near[0].shape
    n_z, _, share, cols = hidden[0].shape
    tok = n_z * rows * n_col
    return pl.pallas_call(
        functools.partial(grad_kernel, n_col, n_row, n_z, half),
        grid=(feats // width,),
        in_specs=[SMEM_SPEC]
        + [pl.BlockSpec((2, rows, width), lambda n: (0, 0, n))] * n_col
        + [pl.BlockSpec((n_z - 1, 2, rows, width), lambda n: (0, 0, 0, n))] * n_col
        + [pl.BlockSpec((n_z, 2, share, cols), lambda n: (0, 0, 0, 0))] * n_row,
        out_specs=pl.BlockSpec((width, BLOCK), lambda n: (n, 0)),
        out_shape=jax.ShapeDtypeStruct((feats, BLOCK), F32),
        scratch_shapes=[pltpu.VMEM((2, tok, width), BF16), pltpu.VMEM((2, tok, BLOCK), BF16)],
        compiler_params=params(),
        name="grad",
    )(pos, *near, *far, *hidden)


def finish_kernel(norm_scale, pos_ref, mask_ref, a_ref, b_ref, out_ref):
    rows = a_ref.shape[0]
    kept = mask_ref[pl.program_id(0), pos_ref[3]] != 0
    total = (a_ref[...] + b_ref[...]) * norm_scale
    total = jnp.where(kept, total, jnp.zeros_like(total))
    out_ref[pl.ds(0, rows, 2), :] = total[:, :128]
    out_ref[pl.ds(1, rows, 2), :] = total[:, 128:]


def finish(pos, mask, mine, theirs, norm_scale):
    feats = mine.shape[0]
    block = pl.BlockSpec((BLOCK, BLOCK), lambda n: (n, 0))
    return pl.pallas_call(
        functools.partial(finish_kernel, norm_scale),
        grid=(feats // BLOCK,),
        in_specs=[SMEM_SPEC, SMEM_SPEC, block, block],
        out_specs=pl.BlockSpec((2 * BLOCK, 128), lambda n: (n, 0)),
        out_shape=jax.ShapeDtypeStruct((2 * feats, 128), F32),
        compiler_params=params(),
        name="finish",
    )(pos, mask, mine, theirs)


def on_device(tokens, cotangent, weight, block_mask):
    n_dp, n_row, n_col = (lax.axis_size(a) for a in ("dp", "row", "col"))
    n_z = n_dp // 2
    dp_at = lax.axis_index("dp")
    pos = jnp.stack([lax.axis_index("row"), dp_at // 2, dp_at % 2, dp_at]).astype(jnp.int32)
    both = jnp.stack([tokens, cotangent])

    near = [both] + [shift(both, "col", j) for j in range(1, n_col)]
    far0 = jnp.stack([shift(both, "dp", 2 * k) for k in range(1, n_z)])

    own, *sends = up(pos, block_mask, near, weight, n_row)
    recv = [shift(s, "row", k + 1) for k, s in enumerate(sends)]
    far = [far0] + [shift(far0, "col", j) for j in range(1, n_col)]
    acts, *pieces = act(pos, own, recv, n_z)
    acts_all = [acts] + [shift(acts, "row", k) for k in range(1, n_row)]
    pieces = jnp.stack([pieces[0]] + [shift(pieces[k], "dp", 2 * k) for k in range(1, n_z)])
    pieces_all = [pieces] + [shift(pieces, "row", k) for k in range(1, n_row)]

    own, *sends = down(pos, block_mask, acts_all, weight, n_col)
    total = own + both.astype(F32)
    for j, s in enumerate(sends):
        total = total + shift(s, "col", -(j + 1)).astype(F32)
    output, input_grad = total[0].astype(BF16), total[1].astype(BF16)

    given = grad(pos, near, far, pieces_all, 1)
    theirs = lax.ppermute(given, "dp", [(i, i ^ 1) for i in range(n_dp)])
    mine = grad(pos, near, far, pieces_all, 0)
    tok_total = tokens.shape[0] * n_col * n_dp
    weight_grad = finish(pos, block_mask, mine, theirs, 1.0 / math.sqrt(tok_total))
    return output, input_grad, weight_grad.reshape(weight.shape[0], 1, BLOCK)


def solution(mesh):
    in_specs = (P(("dp", "col"), "row"), P(("dp", "col"), "row"), P("row", "col"), P("row", "col"))
    out_specs = (P(("dp", "col"), "row"), P(("dp", "col"), "row"), P("row", "dp", "col"))
    return jax.shard_map(
        on_device, mesh=mesh, in_specs=in_specs, out_specs=out_specs, check_vma=False
    )
```

time: 501 us -> 288 us (0.57)
  waiting for transfers between devices: 404 us -> 87.7 us
  starting transfers between devices: 0.42 us -> 143 us
  Pallas kernels: 0 us -> 42.7 us
  matrix products: 41.3 us -> 0 us
  other arithmetic: 17.5 us -> 3.21 us
  local copies, waits for them, and re-layouts: 21.2 us -> 7.03 us
  between operations: 14.1 us -> 0.94 us
    reduce_scatter x3 -> x0, waiting for transfers between devices: 251 us -> none  [the longest x1 185 us: on_device(): lax.psum_scatter(partial_value * jnp.moveaxis(kept_share, 1, 0).astype(jn...]
    ppermute x0 -> x37, starting transfers between devices: none -> 143 us  [the longest x36 134 us: shift(): lax.ppermute(value, axis, [(i, (i + by) % size) for i in range(size)])]
    psum x1 -> x0, waiting for transfers between devices: 102 us -> none  [on_device(): pre = lax.psum(pre_part, 'row')]
    ppermute x0 -> x37, waiting for transfers between devices: none -> 87.7 us  [the longest x36 87.7 us: shift(): lax.ppermute(value, axis, [(i, (i + by) % size) for i in range(size)])]
    all_gather x2 -> x0, waiting for transfers between devices: 50 us -> none  [the longest x1 35 us: on_device(): lax.all_gather(cotangent, 'col', axis=0, tiled=True)]
    pallas_call x0 -> x6, Pallas kernels: none -> 42.7 us  [the longest x2 15.2 us: grad(): pl.pallas_call(functools.partial(grad_kernel, n_col, n_row, n_z, half), g...]
    dot_general x6 -> x0, matrix products: 41.3 us -> none  [the longest x2 14.4 us: times_transpose(): lax.dot_general(left, masked, (((1,), (1,)), ((), ())), preferred_element...]
    mul x1 -> x0, other arithmetic: 10.5 us -> none  [on_device(): masked = weight * kept]
  transfers between devices with their start and end apart: 6 -> 37, of which waited for: 6 -> 13; matrix products, arithmetic and copies ran while one was open for 11% -> 1% of each run, Pallas kernels for 0% -> 10%
where the time goes in v1:
time: 288 us; the launch traced here: 284 us
  starting transfers between devices  143 us (50%)
  waiting for transfers between devices  87.7 us (30%)
  Pallas kernels  42.7 us (15%)
  local copies, waits for them, and re-layouts  7.03 us (2%)
  other arithmetic  3.21 us (1%)
    ppermute x36, starting transfers between devices, shift(): lax.ppermute(value, axis, [(i, (i + by) % size) for i in range(size)])  134 us
    ppermute x36, waiting for transfers between devices, shift(): lax.ppermute(value, axis, [(i, (i + by) % size) for i in range(size)])  87.7 us
    pallas_call x2, Pallas kernels, grad(): pl.pallas_call(functools.partial(grad_kernel, n_col, n_row, n_z, half), g...  15.2 us
    pallas_call x1, Pallas kernels, up(): pl.pallas_call(functools.partial(up_kernel, n_col, n_row), grid=(cols //...  9.24 us
    pallas_call x1, Pallas kernels, down(): pl.pallas_call(functools.partial(down_kernel, n_col, n_row), grid=(feats...  8.9 us
    ppermute x1, starting transfers between devices, on_device(): theirs = lax.ppermute(given, 'dp', [(i, i ^ 1) for i in range(n_dp)])  8.21 us
    unnamed x58, local copies, waits for them, and re-layouts  6.31 us
    pallas_call x1, Pallas kernels, finish(): pl.pallas_call(functools.partial(finish_kernel, norm_scale), grid=(feats...  6.15 us
  transfers between devices with their start and end apart: 37, of which 13 were waited for; matrix products, arithmetic and copies ran while one was open for 1% of the time, Pallas kernels for 10%

profile of v1, /device:TPU:1, one launch (start us, length us, event | category | flops | bytes accessed | tf_op | source)
XLA Modules:
  0.0 284.2 jit_solution(8099873393940802495)
XLA Ops:
  0.6 1.0 pad_maximum_fusion.2.refs_0_
  1.6 2.1 collective-permute-start
  3.8 2.5 collective-permute-start.1
  6.2 2.5 collective-permute-start.2
  8.7 1.5 collective-permute-start.4
  10.2 2.3 collective-permute-done.refs_1_
  12.5 3.9 %collective-permute-start.5 = (bf16[2,32,2048]{2,1,0:T(8,128)(2,1)S(1)}, bf16[2,32,2048]{2,1,0:T(8,128)(2,1)S(1)}, u32[]{:S(2)}, u32[]{:S(2)}) collective-permute-start(bf16[2,32,2048]{2,1,0:T(8,128)(2,1)S(1)} %pad_maximum_fusion.2.refs_0_), channel_id=1, source_target_pairs={{0,6},{1,7},{2,0},{3,1},{4,2},{5,3},{6,4},{7,5},{8,14},{9,15},{10,... | collective-permute-start | bytes 786440 | tf_op jit(solution)/shard_map/ppermute | solution.py:19
  16.4 1.7 collective-permute-start.6
  18.1 8.4 %collective-permute-start.22 = (bf16[2,32,2048]{2,1,0:T(8,128)(2,1)S(1)}, bf16[2,32,2048]{2,1,0:T(8,128)(2,1)S(1)}, u32[]{:S(2)}, u32[]{:S(2)}) collective-permute-start(bf16[2,32,2048]{2,1,0:T(8,128)(2,1)S(1)} %pad_maximum_fusion.2.refs_0_), channel_id=1, source_target_pairs={{0,192},{32,224},{64,0},{96,32},{128,64},{160,96},{192,128},{224,1... | collective-permute-start | bytes 786440 | tf_op jit(solution)/shard_map/ppermute | solution.py:19
  26.5 2.2 collective-permute-start.21
  28.6 1.4 collective-permute-done.4.refs_5_
  30.0 3.0 %collective-permute-start.20 = (bf16[2,32,2048]{2,1,0:T(8,128)(2,1)S(1)}, bf16[2,32,2048]{2,1,0:T(8,128)(2,1)S(1)}, u32[]{:S(2)}, u32[]{:S(2)}) collective-permute-start(bf16[2,32,2048]{2,1,0:T(8,128)(2,1)S(1)} %pad_maximum_fusion.2.refs_0_), channel_id=1, source_target_pairs={{0,64},{32,96},{64,128},{96,160},{128,192},{160,224},{192,0},{224,... | collective-permute-start | bytes 786440 | tf_op jit(solution)/shard_map/ppermute | solution.py:19
  35.1 9.2 %up.1 = (f32[2,64,2048]{2,1,0:T(8,128)}, bf16[2,64,2048]{2,1,0:T(8,128)(2,1)}, bf16[2,64,2048]{2,1,0:T(8,128)(2,1)}, bf16[2,64,2048]{2,1,0:T(8,128)(2,1)}) custom-call(s32[4]{0:T(128)} %pad_add_fusion.pos_ref, s32[8,8]{1,0:T(8,128)} %mask_ref.5, bf16[2,32,2048]{2,1,0:T(8,128)(2,1)} %copy-done.2, bf16[2,32,2048]{2,1,0:T(8,128)(2,1)} %copy-done.10, ...), custom_call_target="tpu_custom_call" | custom-call | tf_op jit(solution)/shard_map/up/pallas_call | solution.py:69
  44.3 1.4 collective-permute-start.7
  45.7 2.6 collective-permute-start.8
  48.3 1.1 collective-permute-start.9
  49.4 1.9 collective-permute-done.21
  51.3 8.3 %collective-permute-done.20 = bf16[2,32,2048]{2,1,0:T(8,128)(2,1)S(1)} collective-permute-done((bf16[2,32,2048]{2,1,0:T(8,128)(2,1)S(1)}, bf16[2,32,2048]{2,1,0:T(8,128)(2,1)S(1)}, u32[]{:S(2)}, u32[]{:S(2)}) %collective-permute-start.20) | collective-permute-done | bytes 262176 | tf_op jit(solution)/shard_map/ppermute | solution.py:19
  59.8 9.5 %collective-permute-start.24 = (bf16[3,2,32,2048]{3,2,1,0:T(8,128)(2,1)S(1)}, bf16[3,2,32,2048]{3,2,1,0:T(8,128)(2,1)S(1)}, u32[]{:S(2)}, u32[]{:S(2)}) collective-permute-start(bf16[3,2,32,2048]{3,2,1,0:T(8,128)(2,1)S(1)} %pad_maximum_fusion.refs_8_), channel_id=1, source_target_pairs={{0,2},{1,3},{2,4},{3,5},{4,6},{5,7},{6,0},{7,1},{8,10},{9,11},{10,... | collective-permute-start | bytes 2359304 | tf_op jit(solution)/shard_map/ppermute | solution.py:19
  69.5 1.1 collective-permute-done.9.refs_3_
  71.5 3.3 %act.1 = (bf16[2,64,2048]{2,1,0:T(8,128)(2,1)}, bf16[2,64,512]{2,1,0:T(8,128)(2,1)}, bf16[2,64,512]{2,1,0:T(8,128)(2,1)}, bf16[2,64,512]{2,1,0:T(8,128)(2,1)}, bf16[2,64,512]{2,1,0:T(8,128)(2,1)}) custom-call(s32[4]{0:T(128)} %pad_add_fusion.pos_ref, f32[2,64,2048]{2,1,0:T(8,128)} %get-tuple-element.20.refs_0_, bf16[2,64,2048]{2,1,0:T(8,128)(2,1)} %copy-done.26, ...), custom_call_target="tpu_custom_call" | custom-call | tf_op jit(solution)/shard_map/act/pallas_call | solution.py:108
  74.7 5.3 %collective-permute-start.31 = (bf16[2,64,512]{2,1,0:T(8,128)(2,1)}, bf16[2,64,512]{2,1,0:T(8,128)(2,1)S(1)}, u32[]{:S(2)}, u32[]{:S(2)}) collective-permute-start(bf16[2,64,512]{2,1,0:T(8,128)(2,1)} %get-tuple-element.35), channel_id=1, source_target_pairs={{0,128},{32,160},{64,192},{96,224},{128,0},{160,32},{192,64},{224,... | collective-permute-start | bytes 393224 | tf_op jit(solution)/shard_map/ppermute | solution.py:19
  80.0 13.7 %collective-permute-start.25 = (bf16[3,2,32,2048]{3,2,1,0:T(8,128)(2,1)S(1)}, bf16[3,2,32,2048]{3,2,1,0:T(8,128)(2,1)S(1)}, u32[]{:S(2)}, u32[]{:S(2)}) collective-permute-start(bf16[3,2,32,2048]{3,2,1,0:T(8,128)(2,1)S(1)} %pad_maximum_fusion.refs_8_), channel_id=1, source_target_pairs={{0,3},{1,4},{2,5},{3,6},{4,7},{5,0},{6,1},{7,2},{8,11},{9,12},{10,... | collective-permute-start | bytes 2359304 | tf_op jit(solution)/shard_map/ppermute | solution.py:19
  93.7 29.2 %collective-permute-start.26 = (bf16[3,2,32,2048]{3,2,1,0:T(8,128)(2,1)S(1)}, bf16[3,2,32,2048]{3,2,1,0:T(8,128)(2,1)S(1)}, u32[]{:S(2)}, u32[]{:S(2)}) collective-permute-start(bf16[3,2,32,2048]{3,2,1,0:T(8,128)(2,1)S(1)} %pad_maximum_fusion.refs_8_), channel_id=1, source_target_pairs={{0,4},{1,5},{2,6},{3,7},{4,0},{5,1},{6,2},{7,3},{8,12},{9,13},{10,... | collective-permute-start | bytes 2359304 | tf_op jit(solution)/shard_map/ppermute | solution.py:19
  122.9 11.9 %collective-permute-start.28 = (bf16[3,2,32,2048]{3,2,1,0:T(8,128)(2,1)S(1)}, bf16[3,2,32,2048]{3,2,1,0:T(8,128)(2,1)S(1)}, u32[]{:S(2)}, u32[]{:S(2)}) collective-permute-start(bf16[3,2,32,2048]{3,2,1,0:T(8,128)(2,1)S(1)} %pad_maximum_fusion.refs_8_), channel_id=1, source_target_pairs={{0,6},{1,7},{2,0},{3,1},{4,2},{5,3},{6,4},{7,5},{8,14},{9,15},{10,... | collective-permute-start | bytes 2359304 | tf_op jit(solution)/shard_map/ppermute | solution.py:19
  134.8 1.1 pad_maximum_fusion.1.refs_16_
  136.0 1.7 collective-permute-start.33
  137.7 2.5 collective-permute-start.34
  140.2 23.7 %collective-permute-done.27.refs_13_ = bf16[3,2,32,2048]{3,2,1,0:T(8,128)(2,1)S(1)} collective-permute-done((bf16[3,2,32,2048]{3,2,1,0:T(8,128)(2,1)S(1)}, bf16[3,2,32,2048]{3,2,1,0:T(8,128)(2,1)S(1)}, u32[]{:S(2)}, u32[]{:S(2)}) %collective-permute-start.27) | collective-permute-done | bytes 786464 | tf_op jit(solution)/shard_map/ppermute | solution.py:19
  163.8 3.5 %collective-permute-start.35 = (bf16[4,2,64,512]{3,2,1,0:T(8,128)(2,1)S(1)}, bf16[4,2,64,512]{3,2,1,0:T(8,128)(2,1)}, u32[]{:S(2)}, u32[]{:S(2)}) collective-permute-start(bf16[4,2,64,512]{3,2,1,0:T(8,128)(2,1)S(1)} %pad_maximum_fusion.1.refs_16_), channel_id=1, source_target_pairs={{0,24},{8,0},{16,8},{24,16},{1,25},{9,1},{17,9},{25,17},{2,26},{10... | collective-permute-start | bytes 1572872 | tf_op jit(solution)/shard_map/ppermute | solution.py:19
  167.3 15.7 %collective-permute-done.29.refs_15_ = bf16[3,2,32,2048]{3,2,1,0:T(8,128)(2,1)S(1)} collective-permute-done((bf16[3,2,32,2048]{3,2,1,0:T(8,128)(2,1)S(1)}, bf16[3,2,32,2048]{3,2,1,0:T(8,128)(2,1)S(1)}, u32[]{:S(2)}, u32[]{:S(2)}) %collective-permute-start.29) | collective-permute-done | bytes 786464 | tf_op jit(solution)/shard_map/ppermute | solution.py:19
  183.2 0.8 copy-done.9
  184.4 7.6 %grad.3 = f32[2048,256]{1,0:T(8,128)} custom-call(s32[4]{0:T(128)} %pad_add_fusion.pos_ref, bf16[2,32,2048]{2,1,0:T(8,128)(2,1)} %copy-done.2, bf16[2,32,2048]{2,1,0:T(8,128)(2,1)} %copy-done.10, bf16[2,32,2048]{2,1,0:T(8,128)(2,1)} %copy-done.11, bf16[2,32,2048]{2,1,0:T(8,128)(2,1)} %copy-done.12, bf16[2,32,2048]{2,1,0:T(8,128)(2,1)} %copy-done.13, ...), custom_call_target="tpu_custom_call" | custom-call | tf_op jit(solution)/shard_map/grad/pallas_call | solution.py:205
  192.0 8.2 %collective-permute-start.36 = (f32[2048,256]{1,0:T(8,128)}, f32[2048,256]{1,0:T(8,128)S(1)}, u32[]{:S(2)}, u32[]{:S(2)}) collective-permute-start(f32[2048,256]{1,0:T(8,128)} %grad.3), channel_id=1, source_target_pairs={{0,32},{32,0},{64,96},{96,64},{128,160},{160,128},{192,224},{224,1... | collective-permute-start | bytes 6291464 | tf_op jit(solution)/shard_map/ppermute | solution.py:268
  200.2 1.8 collective-permute-start.10
  202.0 5.1 %collective-permute-start.11 = (bf16[2,64,2048]{2,1,0:T(8,128)(2,1)}, bf16[2,64,2048]{2,1,0:T(8,128)(2,1)S(1)}, u32[]{:S(2)}, u32[]{:S(2)}) collective-permute-start(bf16[2,64,2048]{2,1,0:T(8,128)(2,1)} %get-tuple-element.24.refs_0_), channel_id=1, source_target_pairs={{0,16},{8,24},{16,0},{24,8},{1,17},{9,25},{17,1},{25,9},{2,18},{10... | collective-permute-start | bytes 1572872 | tf_op jit(solution)/shard_map/ppermute | solution.py:19
  207.1 11.2 %collective-permute-done.10.refs_1_ = bf16[2,64,2048]{2,1,0:T(8,128)(2,1)S(1)} collective-permute-done((bf16[2,64,2048]{2,1,0:T(8,128)(2,1)}, bf16[2,64,2048]{2,1,0:T(8,128)(2,1)S(1)}, u32[]{:S(2)}, u32[]{:S(2)}) %collective-permute-start.10) | collective-permute-done | bytes 524320 | tf_op jit(solution)/shard_map/ppermute | solution.py:19
  218.3 12.2 %collective-permute-done.11.refs_2_ = bf16[2,64,2048]{2,1,0:T(8,128)(2,1)S(1)} collective-permute-done((bf16[2,64,2048]{2,1,0:T(8,128)(2,1)}, bf16[2,64,2048]{2,1,0:T(8,128)(2,1)S(1)}, u32[]{:S(2)}, u32[]{:S(2)}) %collective-permute-start.11) | collective-permute-done | bytes 524320 | tf_op jit(solution)/shard_map/ppermute | solution.py:19
  231.4 0.8 copy-done.22
  232.2 8.9 %down.1 = (f32[2,32,2048]{2,1,0:T(8,128)}, bf16[2,32,2048]{2,1,0:T(8,128)(2,1)}, bf16[2,32,2048]{2,1,0:T(8,128)(2,1)}, bf16[2,32,2048]{2,1,0:T(8,128)(2,1)}, bf1...) custom-call(s32[4]{0:T(128)} %pad_add_fusion.pos_ref, ...), custom_call_target="tpu_custom_call" | custom-call | tf_op jit(solution)/shard_map/down/pallas_call | solution.py:151
  241.1 4.3 %collective-permute-start.18 = (bf16[2,32,2048]{2,1,0:T(8,128)(2,1)}, bf16[2,32,2048]{2,1,0:T(8,128)(2,1)S(1)}, u32[]{:S(2)}, u32[]{:S(2)}) collective-permute-start(bf16[2,32,2048]{2,1,0:T(8,128)(2,1)} %get-tuple-element.31), channel_id=1, source_target_pairs={{0,2},{1,3},{2,4},{3,5},{4,6},{5,7},{6,0},{7,1},{8,10},{9,11},{10,... | collective-permute-start | bytes 786440 | tf_op jit(solution)/shard_map/ppermute | solution.py:19
  245.5 1.5 collective-permute-start.16
  246.9 8.2 %collective-permute-done.19 = bf16[2,32,2048]{2,1,0:T(8,128)(2,1)S(1)} collective-permute-done((bf16[2,32,2048]{2,1,0:T(8,128)(2,1)}, bf16[2,32,2048]{2,1,0:T(8,128)(2,1)S(1)}, u32[]{:S(2)}, u32[]{:S(2)}) %collective-permute-start.19) | collective-permute-done | bytes 262176 | tf_op jit(solution)/shard_map/ppermute | solution.py:19
  255.8 2.4 collective-permute-start.14
  258.2 9.1 %collective-permute-start.13 = (bf16[2,32,2048]{2,1,0:T(8,128)(2,1)}, bf16[2,32,2048]{2,1,0:T(8,128)(2,1)S(1)}, u32[]{:S(2)}, u32[]{:S(2)}) collective-permute-start(bf16[2,32,2048]{2,1,0:T(8,128)(2,1)} %get-tuple-element.26), channel_id=1, source_target_pairs={{0,7},{1,0},{2,1},{3,2},{4,3},{5,4},{6,5},{7,6},{8,15},{9,8},{10,9... | collective-permute-start | bytes 786440 | tf_op jit(solution)/shard_map/ppermute | solution.py:19
  267.3 7.6 %grad.2.a_ref = f32[2048,256]{1,0:T(8,128)} custom-call(s32[4]{0:T(128)} %pad_add_fusion.pos_ref, bf16[2,32,2048]{2,1,0:T(8,128)(2,1)} %copy-done.2, bf16[2,32,2048]{2,1,0:T(8,128)(2,1)} %copy-done.10, bf16[2,32,2048]{2,1,0:T(8,128)(2,1)} %copy-done.11, bf16[2,32,2048]{2,1,0:T(8,128)(2,1)} %copy-done.12, bf16[2,32,2048]{2,1,0:T(8,128)(2,1)} %copy-done.13, ...), custom_call_target="tpu_custom_call" | custom-call | tf_op jit(solution)/shard_map/grad/pallas_call | solution.py:205
  276.7 1.3 copy-done.19
  278.0 6.2 %finish.1 = f32[4096,128]{1,0:T(8,128)} custom-call(s32[4]{0:T(128)} %pad_add_fusion.pos_ref, s32[8,8]{1,0:T(8,128)} %mask_ref.5, f32[2048,256]{1,0:T(8,128)} %grad.2.a_ref, f32[2048,256]{1,0:T(8,128)} %copy-done.19), custom_call_target="tpu_custom_call" | custom-call | tf_op jit(solution)/shard_map/finish/pallas_call | solution.py:232
  (96 shorter events, 7.0 us)
Async XLA Ops:
  1.6 32.0 %copy-start.2 = (bf16[2,32,2048]{2,1,0:T(8,128)(2,1)}, bf16[2,32,2048]{2,1,0:T(8,128)(2,1)S(1)}, u32[]{:S(2)}) copy-start(bf16[2,32,2048]{2,1,0:T(8,128)(2,1)S(1)} %pad_maximum_fusion.2.refs_0_) | copy-start | bytes 786436
  1.6 10.9 %collective-permute-start = (bf16[2,32,2048]{2,1,0:T(8,128)(2,1)S(1)}, bf16[2,32,2048]{2,1,0:T(8,128)(2,1)S(1)}, u32[]{:S(2)}, u32[]{:S(2)}) collective-permute-start(bf16[2,32,2048]{2,1,0:T(8,128)(2,1)S(1)} %pad_maximum_fusion.2.refs_0_), channel_id=1, source_target_pairs={{0,1},{1,2},{2,3},{3,4},{4,5},{5,6},{6,7},{7,0},{8,9},{9,10},{10,1... | collective-permute-start | bytes 786440 | tf_op jit(solution)/shard_map/ppermute | solution.py:19
  3.8 12.6 %collective-permute-start.1 = (bf16[2,32,2048]{2,1,0:T(8,128)(2,1)S(1)}, bf16[2,32,2048]{2,1,0:T(8,128)(2,1)S(1)}, u32[]{:S(2)}, u32[]{:S(2)}) collective-permute-start(bf16[2,32,2048]{2,1,0:T(8,128)(2,1)S(1)} %pad_maximum_fusion.2.refs_0_), channel_id=1, source_target_pairs={{0,2},{1,3},{2,4},{3,5},{4,6},{5,7},{6,0},{7,1},{8,10},{9,11},{10,... | collective-permute-start | bytes 786440 | tf_op jit(solution)/shard_map/ppermute | solution.py:19
  6.2 11.9 %collective-permute-start.2 = (bf16[2,32,2048]{2,1,0:T(8,128)(2,1)S(1)}, bf16[2,32,2048]{2,1,0:T(8,128)(2,1)S(1)}, u32[]{:S(2)}, u32[]{:S(2)}) collective-permute-start(bf16[2,32,2048]{2,1,0:T(8,128)(2,1)S(1)} %pad_maximum_fusion.2.refs_0_), channel_id=1, source_target_pairs={{0,3},{1,4},{2,5},{3,6},{4,7},{5,0},{6,1},{7,2},{8,11},{9,12},{10,... | collective-permute-start | bytes 786440 | tf_op jit(solution)/shard_map/ppermute | solution.py:19
  8.7 17.8 %collective-permute-start.3 = (bf16[2,32,2048]{2,1,0:T(8,128)(2,1)S(1)}, bf16[2,32,2048]{2,1,0:T(8,128)(2,1)S(1)}, u32[]{:S(2)}, u32[]{:S(2)}) collective-permute-start(bf16[2,32,2048]{2,1,0:T(8,128)(2,1)S(1)} %pad_maximum_fusion.2.refs_0_), channel_id=1, source_target_pairs={{0,4},{1,5},{2,6},{3,7},{4,0},{5,1},{6,2},{7,3},{8,12},{9,13},{10,... | collective-permute-start | bytes 786440 | tf_op jit(solution)/shard_map/ppermute | solution.py:19
  8.7 21.3 %collective-permute-start.4 = (bf16[2,32,2048]{2,1,0:T(8,128)(2,1)S(1)}, bf16[2,32,2048]{2,1,0:T(8,128)(2,1)S(1)}, u32[]{:S(2)}, u32[]{:S(2)}) collective-permute-start(bf16[2,32,2048]{2,1,0:T(8,128)(2,1)S(1)} %pad_maximum_fusion.2.refs_0_), channel_id=1, source_target_pairs={{0,5},{1,6},{2,7},{3,0},{4,1},{5,2},{6,3},{7,4},{8,13},{9,14},{10,... | collective-permute-start | bytes 786440 | tf_op jit(solution)/shard_map/ppermute | solution.py:19
  12.5 21.2 %copy-start.10 = (bf16[2,32,2048]{2,1,0:T(8,128)(2,1)}, bf16[2,32,2048]{2,1,0:T(8,128)(2,1)S(1)}, u32[]{:S(2)}) copy-start(bf16[2,32,2048]{2,1,0:T(8,128)(2,1)S(1)} %collective-permute-done.refs_1_) | copy-start | bytes 786436
  12.5 21.2 %collective-permute-start.5 = (bf16[2,32,2048]{2,1,0:T(8,128)(2,1)S(1)}, bf16[2,32,2048]{2,1,0:T(8,128)(2,1)S(1)}, u32[]{:S(2)}, u32[]{:S(2)}) collective-permute-start(bf16[2,32,2048]{2,1,0:T(8,128)(2,1)S(1)} %pad_maximum_fusion.2.refs_0_), channel_id=1, source_target_pairs={{0,6},{1,7},{2,0},{3,1},{4,2},{5,3},{6,4},{7,5},{8,14},{9,15},{10,... | collective-permute-start | bytes 786440 | tf_op jit(solution)/shard_map/ppermute | solution.py:19
  16.4 17.3 %collective-permute-start.6 = (bf16[2,32,2048]{2,1,0:T(8,128)(2,1)S(1)}, bf16[2,32,2048]{2,1,0:T(8,128)(2,1)S(1)}, u32[]{:S(2)}, u32[]{:S(2)}) collective-permute-start(bf16[2,32,2048]{2,1,0:T(8,128)(2,1)S(1)} %pad_maximum_fusion.2.refs_0_), channel_id=1, source_target_pairs={{0,7},{1,0},{2,1},{3,2},{4,3},{5,4},{6,5},{7,6},{8,15},{9,8},{10,9... | collective-permute-start | bytes 786440 | tf_op jit(solution)/shard_map/ppermute | solution.py:19
  18.1 30.2 %collective-permute-start.22 = (bf16[2,32,2048]{2,1,0:T(8,128)(2,1)S(1)}, bf16[2,32,2048]{2,1,0:T(8,128)(2,1)S(1)}, u32[]{:S(2)}, u32[]{:S(2)}) collective-permute-start(bf16[2,32,2048]{2,1,0:T(8,128)(2,1)S(1)} %pad_maximum_fusion.2.refs_0_), channel_id=1, source_target_pairs={{0,192},{32,224},{64,0},{96,32},{128,64},{160,96},{192,128},{224,1... | collective-permute-start | bytes 786440 | tf_op jit(solution)/shard_map/ppermute | solution.py:19
  26.5 24.8 %collective-permute-start.21 = (bf16[2,32,2048]{2,1,0:T(8,128)(2,1)S(1)}, bf16[2,32,2048]{2,1,0:T(8,128)(2,1)S(1)}, u32[]{:S(2)}, u32[]{:S(2)}) collective-permute-start(bf16[2,32,2048]{2,1,0:T(8,128)(2,1)S(1)} %pad_maximum_fusion.2.refs_0_), channel_id=1, source_target_pairs={{0,128},{32,160},{64,192},{96,224},{128,0},{160,32},{192,64},{224,... | collective-permute-start | bytes 786440 | tf_op jit(solution)/shard_map/ppermute | solution.py:19
  30.0 29.6 %collective-permute-start.20 = (bf16[2,32,2048]{2,1,0:T(8,128)(2,1)S(1)}, bf16[2,32,2048]{2,1,0:T(8,128)(2,1)S(1)}, u32[]{:S(2)}, u32[]{:S(2)}) collective-permute-start(bf16[2,32,2048]{2,1,0:T(8,128)(2,1)S(1)} %pad_maximum_fusion.2.refs_0_), channel_id=1, source_target_pairs={{0,64},{32,96},{64,128},{96,160},{128,192},{160,224},{192,0},{224,... | collective-permute-start | bytes 786440 | tf_op jit(solution)/shard_map/ppermute | solution.py:19
  44.3 24.9 %collective-permute-start.7 = (bf16[2,64,2048]{2,1,0:T(8,128)(2,1)}, bf16[2,64,2048]{2,1,0:T(8,128)(2,1)S(1)}, u32[]{:S(2)}, u32[]{:S(2)}) collective-permute-start(bf16[2,64,2048]{2,1,0:T(8,128)(2,1)} %get-tuple-element.21), channel_id=1, source_target_pairs={{0,8},{8,16},{16,24},{24,0},{1,9},{9,17},{17,25},{25,1},{2,10},{10... | collective-permute-start | bytes 1572872 | tf_op jit(solution)/shard_map/ppermute | solution.py:19
  45.7 23.9 %collective-permute-start.8 = (bf16[2,64,2048]{2,1,0:T(8,128)(2,1)}, bf16[2,64,2048]{2,1,0:T(8,128)(2,1)S(1)}, u32[]{:S(2)}, u32[]{:S(2)}) collective-permute-start(bf16[2,64,2048]{2,1,0:T(8,128)(2,1)} %get-tuple-element.22), channel_id=1, source_target_pairs={{0,16},{8,24},{16,0},{24,8},{1,17},{9,25},{17,1},{25,9},{2,18},{10... | collective-permute-start | bytes 1572872 | tf_op jit(solution)/shard_map/ppermute | solution.py:19
  48.3 22.4 %collective-permute-start.9 = (bf16[2,64,2048]{2,1,0:T(8,128)(2,1)}, bf16[2,64,2048]{2,1,0:T(8,128)(2,1)S(1)}, u32[]{:S(2)}, u32[]{:S(2)}) collective-permute-start(bf16[2,64,2048]{2,1,0:T(8,128)(2,1)} %get-tuple-element.23), channel_id=1, source_target_pairs={{0,24},{8,0},{16,8},{24,16},{1,25},{9,1},{17,9},{25,17},{2,26},{10... | collective-permute-start | bytes 1572872 | tf_op jit(solution)/shard_map/ppermute | solution.py:19
  59.7 123.4 %copy-start = (bf16[3,2,32,2048]{3,2,1,0:T(8,128)(2,1)}, bf16[3,2,32,2048]{3,2,1,0:T(8,128)(2,1)S(1)}, u32[]{:S(2)}) copy-start(bf16[3,2,32,2048]{3,2,1,0:T(8,128)(2,1)S(1)} %pad_maximum_fusion.refs_8_) | copy-start | bytes 2359300
  59.7 63.2 %collective-permute-start.23 = (bf16[3,2,32,2048]{3,2,1,0:T(8,128)(2,1)S(1)}, bf16[3,2,32,2048]{3,2,1,0:T(8,128)(2,1)S(1)}, u32[]{:S(2)}, u32[]{:S(2)}) collective-permute-start(bf16[3,2,32,2048]{3,2,1,0:T(8,128)(2,1)S(1)} %pad_maximum_fusion.refs_8_), channel_id=1, source_target_pairs={{0,1},{1,2},{2,3},{3,4},{4,5},{5,6},{6,7},{7,0},{8,9},{9,10},{10,1... | collective-permute-start | bytes 2359304 | tf_op jit(solution)/shard_map/ppermute | solution.py:19
  59.8 75.0 %collective-permute-start.24 = (bf16[3,2,32,2048]{3,2,1,0:T(8,128)(2,1)S(1)}, bf16[3,2,32,2048]{3,2,1,0:T(8,128)(2,1)S(1)}, u32[]{:S(2)}, u32[]{:S(2)}) collective-permute-start(bf16[3,2,32,2048]{3,2,1,0:T(8,128)(2,1)S(1)} %pad_maximum_fusion.refs_8_), channel_id=1, source_target_pairs={{0,2},{1,3},{2,4},{3,5},{4,6},{5,7},{6,0},{7,1},{8,10},{9,11},{10,... | collective-permute-start | bytes 2359304 | tf_op jit(solution)/shard_map/ppermute | solution.py:19
  74.7 5.3 %collective-permute-start.32 = (bf16[2,64,512]{2,1,0:T(8,128)(2,1)}, bf16[2,64,512]{2,1,0:T(8,128)(2,1)S(1)}, u32[]{:S(2)}, u32[]{:S(2)}) collective-permute-start(bf16[2,64,512]{2,1,0:T(8,128)(2,1)} %get-tuple-element.36), channel_id=1, source_target_pairs={{0,192},{32,224},{64,0},{96,32},{128,64},{160,96},{192,128},{224,1... | collective-permute-start | bytes 393224 | tf_op jit(solution)/shard_map/ppermute | solution.py:19
  74.7 19.0 %collective-permute-start.31 = (bf16[2,64,512]{2,1,0:T(8,128)(2,1)}, bf16[2,64,512]{2,1,0:T(8,128)(2,1)S(1)}, u32[]{:S(2)}, u32[]{:S(2)}) collective-permute-start(bf16[2,64,512]{2,1,0:T(8,128)(2,1)} %get-tuple-element.35), channel_id=1, source_target_pairs={{0,128},{32,160},{64,192},{96,224},{128,0},{160,32},{192,64},{224,... | collective-permute-start | bytes 393224 | tf_op jit(solution)/shard_map/ppermute | solution.py:19
  80.0 42.9 %collective-permute-start.30 = (bf16[2,64,512]{2,1,0:T(8,128)(2,1)}, bf16[2,64,512]{2,1,0:T(8,128)(2,1)S(1)}, u32[]{:S(2)}, u32[]{:S(2)}) collective-permute-start(bf16[2,64,512]{2,1,0:T(8,128)(2,1)} %get-tuple-element.34), channel_id=1, source_target_pairs={{0,64},{32,96},{64,128},{96,160},{128,192},{160,224},{192,0},{224,... | collective-permute-start | bytes 393224 | tf_op jit(solution)/shard_map/ppermute | solution.py:19
  80.0 55.9 %collective-permute-start.25 = (bf16[3,2,32,2048]{3,2,1,0:T(8,128)(2,1)S(1)}, bf16[3,2,32,2048]{3,2,1,0:T(8,128)(2,1)S(1)}, u32[]{:S(2)}, u32[]{:S(2)}) collective-permute-start(bf16[3,2,32,2048]{3,2,1,0:T(8,128)(2,1)S(1)} %pad_maximum_fusion.refs_8_), channel_id=1, source_target_pairs={{0,3},{1,4},{2,5},{3,6},{4,7},{5,0},{6,1},{7,2},{8,11},{9,12},{10,... | collective-permute-start | bytes 2359304 | tf_op jit(solution)/shard_map/ppermute | solution.py:19
  93.7 44.0 %collective-permute-start.26 = (bf16[3,2,32,2048]{3,2,1,0:T(8,128)(2,1)S(1)}, bf16[3,2,32,2048]{3,2,1,0:T(8,128)(2,1)S(1)}, u32[]{:S(2)}, u32[]{:S(2)}) collective-permute-start(bf16[3,2,32,2048]{3,2,1,0:T(8,128)(2,1)S(1)} %pad_maximum_fusion.refs_8_), channel_id=1, source_target_pairs={{0,4},{1,5},{2,6},{3,7},{4,0},{5,1},{6,2},{7,3},{8,12},{9,13},{10,... | collective-permute-start | bytes 2359304 | tf_op jit(solution)/shard_map/ppermute | solution.py:19
  122.9 40.9 %collective-permute-start.27 = (bf16[3,2,32,2048]{3,2,1,0:T(8,128)(2,1)S(1)}, bf16[3,2,32,2048]{3,2,1,0:T(8,128)(2,1)S(1)}, u32[]{:S(2)}, u32[]{:S(2)}) collective-permute-start(bf16[3,2,32,2048]{3,2,1,0:T(8,128)(2,1)S(1)} %pad_maximum_fusion.refs_8_), channel_id=1, source_target_pairs={{0,5},{1,6},{2,7},{3,0},{4,1},{5,2},{6,3},{7,4},{8,13},{9,14},{10,... | collective-permute-start | bytes 2359304 | tf_op jit(solution)/shard_map/ppermute | solution.py:19
  122.9 60.2 %copy-start.3 = (bf16[3,2,32,2048]{3,2,1,0:T(8,128)(2,1)}, bf16[3,2,32,2048]{3,2,1,0:T(8,128)(2,1)S(1)}, u32[]{:S(2)}) copy-start(bf16[3,2,32,2048]{3,2,1,0:T(8,128)(2,1)S(1)} %collective-permute-done.23.refs_9_) | copy-start | bytes 2359300
  122.9 44.4 %collective-permute-start.28 = (bf16[3,2,32,2048]{3,2,1,0:T(8,128)(2,1)S(1)}, bf16[3,2,32,2048]{3,2,1,0:T(8,128)(2,1)S(1)}, u32[]{:S(2)}, u32[]{:S(2)}) collective-permute-start(bf16[3,2,32,2048]{3,2,1,0:T(8,128)(2,1)S(1)} %pad_maximum_fusion.refs_8_), channel_id=1, source_target_pairs={{0,6},{1,7},{2,0},{3,1},{4,2},{5,3},{6,4},{7,5},{8,14},{9,15},{10,... | collective-permute-start | bytes 2359304 | tf_op jit(solution)/shard_map/ppermute | solution.py:19
  134.8 48.3 %copy-start.4 = (bf16[3,2,32,2048]{3,2,1,0:T(8,128)(2,1)}, bf16[3,2,32,2048]{3,2,1,0:T(8,128)(2,1)S(1)}, u32[]{:S(2)}) copy-start(bf16[3,2,32,2048]{3,2,1,0:T(8,128)(2,1)S(1)} %collective-permute-done.24.refs_10_) | copy-start | bytes 2359300
  134.8 48.3 %collective-permute-start.29 = (bf16[3,2,32,2048]{3,2,1,0:T(8,128)(2,1)S(1)}, bf16[3,2,32,2048]{3,2,1,0:T(8,128)(2,1)S(1)}, u32[]{:S(2)}, u32[]{:S(2)}) collective-permute-start(bf16[3,2,32,2048]{3,2,1,0:T(8,128)(2,1)S(1)} %pad_maximum_fusion.refs_8_), channel_id=1, source_target_pairs={{0,7},{1,0},{2,1},{3,2},{4,3},{5,4},{6,5},{7,6},{8,15},{9,8},{10,9... | collective-permute-start | bytes 2359304 | tf_op jit(solution)/shard_map/ppermute | solution.py:19
  135.9 47.2 %copy-start.1 = (bf16[4,2,64,512]{3,2,1,0:T(8,128)(2,1)}, bf16[4,2,64,512]{3,2,1,0:T(8,128)(2,1)S(1)}, u32[]{:S(2)}) copy-start(bf16[4,2,64,512]{3,2,1,0:T(8,128)(2,1)S(1)} %pad_maximum_fusion.1.refs_16_) | copy-start | bytes 1572868
  136.0 47.2 %copy-start.5 = (bf16[3,2,32,2048]{3,2,1,0:T(8,128)(2,1)}, bf16[3,2,32,2048]{3,2,1,0:T(8,128)(2,1)S(1)}, u32[]{:S(2)}) copy-start(bf16[3,2,32,2048]{3,2,1,0:T(8,128)(2,1)S(1)} %collective-permute-done.25.refs_11_) | copy-start | bytes 2359300
  136.0 47.1 %collective-permute-start.33 = (bf16[4,2,64,512]{3,2,1,0:T(8,128)(2,1)S(1)}, bf16[4,2,64,512]{3,2,1,0:T(8,128)(2,1)S(1)}, u32[]{:S(2)}, u32[]{:S(2)}) collective-permute-start(bf16[4,2,64,512]{3,2,1,0:T(8,128)(2,1)S(1)} %pad_maximum_fusion.1.refs_16_), channel_id=1, source_target_pairs={{0,8},{8,16},{16,24},{24,0},{1,9},{9,17},{17,25},{25,1},{2,10},{10... | collective-permute-start | bytes 1572872 | tf_op jit(solution)/shard_map/ppermute | solution.py:19
  137.7 45.5 %copy-start.6 = (bf16[3,2,32,2048]{3,2,1,0:T(8,128)(2,1)}, bf16[3,2,32,2048]{3,2,1,0:T(8,128)(2,1)S(1)}, u32[]{:S(2)}) copy-start(bf16[3,2,32,2048]{3,2,1,0:T(8,128)(2,1)S(1)} %collective-permute-done.26.refs_12_) | copy-start | bytes 2359300
  137.7 45.4 %collective-permute-start.34 = (bf16[4,2,64,512]{3,2,1,0:T(8,128)(2,1)S(1)}, bf16[4,2,64,512]{3,2,1,0:T(8,128)(2,1)S(1)}, u32[]{:S(2)}, u32[]{:S(2)}) collective-permute-start(bf16[4,2,64,512]{3,2,1,0:T(8,128)(2,1)S(1)} %pad_maximum_fusion.1.refs_16_), channel_id=1, source_target_pairs={{0,16},{8,24},{16,0},{24,8},{1,17},{9,25},{17,1},{25,9},{2,18},{10... | collective-permute-start | bytes 1572872 | tf_op jit(solution)/shard_map/ppermute | solution.py:19
  163.8 19.4 %copy-start.7 = (bf16[3,2,32,2048]{3,2,1,0:T(8,128)(2,1)}, bf16[3,2,32,2048]{3,2,1,0:T(8,128)(2,1)S(1)}, u32[]{:S(2)}) copy-start(bf16[3,2,32,2048]{3,2,1,0:T(8,128)(2,1)S(1)} %collective-permute-done.27.refs_13_) | copy-start | bytes 2359300
  163.8 19.3 %collective-permute-start.35 = (bf16[4,2,64,512]{3,2,1,0:T(8,128)(2,1)S(1)}, bf16[4,2,64,512]{3,2,1,0:T(8,128)(2,1)}, u32[]{:S(2)}, u32[]{:S(2)}) collective-permute-start(bf16[4,2,64,512]{3,2,1,0:T(8,128)(2,1)S(1)} %pad_maximum_fusion.1.refs_16_), channel_id=1, source_target_pairs={{0,24},{8,0},{16,8},{24,16},{1,25},{9,1},{17,9},{25,17},{2,26},{10... | collective-permute-start | bytes 1572872 | tf_op jit(solution)/shard_map/ppermute | solution.py:19
  192.0 84.7 %collective-permute-start.36 = (f32[2048,256]{1,0:T(8,128)}, f32[2048,256]{1,0:T(8,128)S(1)}, u32[]{:S(2)}, u32[]{:S(2)}) collective-permute-start(f32[2048,256]{1,0:T(8,128)} %grad.3), channel_id=1, source_target_pairs={{0,32},{32,0},{64,96},{96,64},{128,160},{160,128},{192,224},{224,1... | collective-permute-start | bytes 6291464 | tf_op jit(solution)/shard_map/ppermute | solution.py:268
  200.2 18.1 %collective-permute-start.10 = (bf16[2,64,2048]{2,1,0:T(8,128)(2,1)}, bf16[2,64,2048]{2,1,0:T(8,128)(2,1)S(1)}, u32[]{:S(2)}, u32[]{:S(2)}) collective-permute-start(bf16[2,64,2048]{2,1,0:T(8,128)(2,1)} %get-tuple-element.24.refs_0_), channel_id=1, source_target_pairs={{0,8},{8,16},{16,24},{24,0},{1,9},{9,17},{17,25},{25,1},{2,10},{10... | collective-permute-start | bytes 1572872 | tf_op jit(solution)/shard_map/ppermute | solution.py:19
  202.0 28.6 %collective-permute-start.11 = (bf16[2,64,2048]{2,1,0:T(8,128)(2,1)}, bf16[2,64,2048]{2,1,0:T(8,128)(2,1)S(1)}, u32[]{:S(2)}, u32[]{:S(2)}) collective-permute-start(bf16[2,64,2048]{2,1,0:T(8,128)(2,1)} %get-tuple-element.24.refs_0_), channel_id=1, source_target_pairs={{0,16},{8,24},{16,0},{24,8},{1,17},{9,25},{17,1},{25,9},{2,18},{10... | collective-permute-start | bytes 1572872 | tf_op jit(solution)/shard_map/ppermute | solution.py:19
  207.1 23.5 %collective-permute-start.12 = (bf16[2,64,2048]{2,1,0:T(8,128)(2,1)}, bf16[2,64,2048]{2,1,0:T(8,128)(2,1)S(1)}, u32[]{:S(2)}, u32[]{:S(2)}) collective-permute-start(bf16[2,64,2048]{2,1,0:T(8,128)(2,1)} %get-tuple-element.24.refs_0_), channel_id=1, source_target_pairs={{0,24},{8,0},{16,8},{24,16},{1,25},{9,1},{17,9},{25,17},{2,26},{10... | collective-permute-start | bytes 1572872 | tf_op jit(solution)/shard_map/ppermute | solution.py:19
  241.1 14.1 %collective-permute-start.19 = (bf16[2,32,2048]{2,1,0:T(8,128)(2,1)}, bf16[2,32,2048]{2,1,0:T(8,128)(2,1)S(1)}, u32[]{:S(2)}, u32[]{:S(2)}) collective-permute-start(bf16[2,32,2048]{2,1,0:T(8,128)(2,1)} %get-tuple-element.32), channel_id=1, source_target_pairs={{0,1},{1,2},{2,3},{3,4},{4,5},{5,6},{6,7},{7,0},{8,9},{9,10},{10,1... | collective-permute-start | bytes 786440 | tf_op jit(solution)/shard_map/ppermute | solution.py:19
  241.1 14.6 %collective-permute-start.18 = (bf16[2,32,2048]{2,1,0:T(8,128)(2,1)}, bf16[2,32,2048]{2,1,0:T(8,128)(2,1)S(1)}, u32[]{:S(2)}, u32[]{:S(2)}) collective-permute-start(bf16[2,32,2048]{2,1,0:T(8,128)(2,1)} %get-tuple-element.31), channel_id=1, source_target_pairs={{0,2},{1,3},{2,4},{3,5},{4,6},{5,7},{6,0},{7,1},{8,10},{9,11},{10,... | collective-permute-start | bytes 786440 | tf_op jit(solution)/shard_map/ppermute | solution.py:19
  245.5 12.7 %collective-permute-start.17 = (bf16[2,32,2048]{2,1,0:T(8,128)(2,1)}, bf16[2,32,2048]{2,1,0:T(8,128)(2,1)S(1)}, u32[]{:S(2)}, u32[]{:S(2)}) collective-permute-start(bf16[2,32,2048]{2,1,0:T(8,128)(2,1)} %get-tuple-element.30), channel_id=1, source_target_pairs={{0,3},{1,4},{2,5},{3,6},{4,7},{5,0},{6,1},{7,2},{8,11},{9,12},{10,... | collective-permute-start | bytes 786440 | tf_op jit(solution)/shard_map/ppermute | solution.py:19
  245.5 29.4 %collective-permute-start.16 = (bf16[2,32,2048]{2,1,0:T(8,128)(2,1)}, bf16[2,32,2048]{2,1,0:T(8,128)(2,1)S(1)}, u32[]{:S(2)}, u32[]{:S(2)}) collective-permute-start(bf16[2,32,2048]{2,1,0:T(8,128)(2,1)} %get-tuple-element.29), channel_id=1, source_target_pairs={{0,4},{1,5},{2,6},{3,7},{4,0},{5,1},{6,2},{7,3},{8,12},{9,13},{10,... | collective-permute-start | bytes 786440 | tf_op jit(solution)/shard_map/ppermute | solution.py:19
  255.1 19.8 %collective-permute-start.15 = (bf16[2,32,2048]{2,1,0:T(8,128)(2,1)}, bf16[2,32,2048]{2,1,0:T(8,128)(2,1)S(1)}, u32[]{:S(2)}, u32[]{:S(2)}) collective-permute-start(bf16[2,32,2048]{2,1,0:T(8,128)(2,1)} %get-tuple-element.28), channel_id=1, source_target_pairs={{0,5},{1,6},{2,7},{3,0},{4,1},{5,2},{6,3},{7,4},{8,13},{9,14},{10,... | collective-permute-start | bytes 786440 | tf_op jit(solution)/shard_map/ppermute | solution.py:19
  255.8 19.2 %collective-permute-start.14 = (bf16[2,32,2048]{2,1,0:T(8,128)(2,1)}, bf16[2,32,2048]{2,1,0:T(8,128)(2,1)S(1)}, u32[]{:S(2)}, u32[]{:S(2)}) collective-permute-start(bf16[2,32,2048]{2,1,0:T(8,128)(2,1)} %get-tuple-element.27), channel_id=1, source_target_pairs={{0,6},{1,7},{2,0},{3,1},{4,2},{5,3},{6,4},{7,5},{8,14},{9,15},{10,... | collective-permute-start | bytes 786440 | tf_op jit(solution)/shard_map/ppermute | solution.py:19
  258.2 17.4 %copy-start.24 = (bf16[32,2048]{1,0:T(8,128)(2,1)S(1)}, bf16[32,2048]{1,0:T(8,128)(2,1)}, u32[]{:S(2)}) copy-start(bf16[32,2048]{1,0:T(8,128)(2,1)} %param.4) | copy-start | bytes 393220
  258.2 17.4 %copy-start.25 = (f32[2,32,2048]{2,1,0:T(8,128)S(1)}, f32[2,32,2048]{2,1,0:T(8,128)}, u32[]{:S(2)}) copy-start(f32[2,32,2048]{2,1,0:T(8,128)} %get-tuple-element.25) | copy-start | bytes 1572868
  258.2 17.4 %collective-permute-start.13 = (bf16[2,32,2048]{2,1,0:T(8,128)(2,1)}, bf16[2,32,2048]{2,1,0:T(8,128)(2,1)S(1)}, u32[]{:S(2)}, u32[]{:S(2)}) collective-permute-start(bf16[2,32,2048]{2,1,0:T(8,128)(2,1)} %get-tuple-element.26), channel_id=1, source_target_pairs={{0,7},{1,0},{2,1},{3,2},{4,3},{5,4},{6,5},{7,6},{8,15},{9,8},{10,9... | collective-permute-start | bytes 786440 | tf_op jit(solution)/shard_map/ppermute | solution.py:19
  (18 other events, 100.5 us)

commit v2 on v1

v2 whole, which is shorter than its diff:
```python
import functools
import math

import jax
import jax.numpy as jnp
from jax import lax
from jax.experimental import pallas as pl
from jax.experimental.pallas import tpu as pltpu
from jax.sharding import PartitionSpec as P

BLOCK = 256
VMEM_LIMIT = 56 * 1024 * 1024
SMEM_SPEC = pl.BlockSpec(memory_space=pltpu.SMEM)
COST = pl.CostEstimate(flops=1, bytes_accessed=1, transcendentals=0)
BF16, F32 = jnp.bfloat16, jnp.float32


def shift(value, axis, by):
    size = lax.axis_size(axis)
    return lax.ppermute(value, axis, [(i, (i + by) % size) for i in range(size)])


def shift_col(value, by_x, swap=0):
    half = lax.axis_size("col") // 2
    pairs = [(i, (i // half ^ swap) * half + (i + by_x) % half) for i in range(2 * half)]
    return lax.ppermute(value, "col", pairs)


def params(steps=1):
    return pltpu.CompilerParams(
        vmem_limit_bytes=VMEM_LIMIT, dimension_semantics=("arbitrary",) * steps
    )


def masked_copy(mask_ref, w_ref, out_ref, row0, col0):
    for i in range(w_ref.shape[0] // BLOCK):
        for j in range(w_ref.shape[1] // BLOCK):
            part = (pl.ds(i * BLOCK, BLOCK), pl.ds(j * BLOCK, BLOCK))
            kept = mask_ref[row0 + i, col0 + j] != 0
            out_ref[part] = jnp.where(kept, w_ref[part], jnp.zeros((BLOCK, BLOCK), BF16))


def up_kernel(n_col, n_row, pos_ref, mask_ref, *refs):
    parts, w_ref = refs[:n_col], refs[n_col]
    own_ref, sends = refs[n_col + 1], refs[n_col + 2 : n_col + 1 + n_row]
    x_ref, wm_ref, acc_ref = refs[-3:]
    rows = parts[0].shape[2]
    tok = rows * 2 * n_col
    step = pl.program_id(0)

    @pl.when(step == 0)
    def _():
        for t in range(2):
            for j in range(n_col):
                for side in range(2):
                    x_ref[pl.ds(t * tok + (2 * j + side) * rows, rows), :] = parts[j][side, t]

    masked_copy(mask_ref, w_ref, wm_ref, 0, step * (w_ref.shape[1] // BLOCK))
    acc_ref[...] = jnp.dot(x_ref[...], wm_ref[...], preferred_element_type=F32)
    share = tok // n_row
    me = pos_ref[0]
    for t in range(2):
        for k in range(n_row):
            first = pl.multiple_of(t * tok + lax.rem(me + k, n_row) * share, share)
            value = acc_ref[pl.ds(first, share), :]
            if k == 0:
                own_ref[t] = value
            else:
                sends[k - 1][t] = value.astype(BF16)


def up(pos, mask, parts, weight, n_row, width=512):
    n_col, (_, _, rows, depth) = len(parts), parts[0].shape
    cols = weight.shape[1]
    tok = rows * 2 * n_col
    share = tok // n_row
    return pl.pallas_call(
        functools.partial(up_kernel, n_col, n_row),
        grid=(cols // width,),
        in_specs=[SMEM_SPEC, SMEM_SPEC]
        + [pl.BlockSpec((2, 2, rows, depth), lambda n: (0, 0, 0, 0))] * n_col
        + [pl.BlockSpec((depth, width), lambda n: (0, n))],
        out_specs=[pl.BlockSpec((2, share, width), lambda n: (0, 0, n))] * n_row,
        out_shape=[jax.ShapeDtypeStruct((2, share, cols), F32)]
        + [jax.ShapeDtypeStruct((2, share, cols), BF16)] * (n_row - 1),
        scratch_shapes=[
            pltpu.VMEM((2 * tok, depth), BF16),
            pltpu.VMEM((depth, width), BF16),
            pltpu.VMEM((2 * tok, width), F32),
        ],
        cost_estimate=COST,
        compiler_params=params(),
        name="up",
    )(pos, mask, *parts, weight)


def act_kernel(n_row, *refs):
    own_ref, recv = refs[0], refs[1:n_row]
    both_ref = refs[n_row]
    pre = own_ref[0]
    grad_hidden = own_ref[1]
    for ref in recv:
        pre = pre + ref[0].astype(F32)
        grad_hidden = grad_hidden + ref[1].astype(F32)
    sig = jax.nn.sigmoid(pre)
    both_ref[0] = (pre * sig).astype(BF16)
    both_ref[1] = (grad_hidden * sig * (1.0 + pre * (1.0 - sig))).astype(BF16)


def act(own, recv):
    _, share, cols = own.shape
    return pl.pallas_call(
        functools.partial(act_kernel, len(recv) + 1),
        in_specs=[pl.BlockSpec(memory_space=pltpu.VMEM)] * (len(recv) + 1),
        out_specs=pl.BlockSpec(memory_space=pltpu.VMEM),
        out_shape=jax.ShapeDtypeStruct((2, share, cols), BF16),
        cost_estimate=COST,
        compiler_params=params(0),
        name="act",
    )(own, *recv)


def down_kernel(n_col, n_row, pos_ref, mask_ref, *refs):
    parts, w_ref, send_ref = refs[:n_row], refs[n_row], refs[n_row + 1]
    x_ref, wm_ref, acc_ref = refs[-3:]
    share = parts[0].shape[1]
    tok = share * n_row
    step = pl.program_id(0)

    @pl.when(step == 0)
    def _():
        for t in range(2):
            for k in range(n_row):
                owner = lax.rem(pos_ref[0] + n_row - k, n_row)
                first = pl.multiple_of(t * tok + owner * share, share)
                x_ref[pl.ds(first, share), :] = parts[k][t]

    masked_copy(mask_ref, w_ref, wm_ref, step * (w_ref.shape[0] // BLOCK), 0)
    acc_ref[...] = lax.dot_general(
        x_ref[...], wm_ref[...], (((1,), (1,)), ((), ())), preferred_element_type=F32
    )
    rows = tok // n_col
    n_x = n_col // 2
    for j in range(n_x):
        for side in range(2):
            to_z = pos_ref[5] if side == 0 else 1 - pos_ref[5]
            to = to_z * n_x + lax.rem(pos_ref[4] + n_x - j, n_x)
            for t in range(2):
                first = t * tok + (2 * j + side) * rows
                send_ref[to, t] = acc_ref[pl.ds(first, rows), :].astype(BF16)


def down(pos, mask, parts, weight, n_col, width=512):
    n_row, (_, share, depth) = len(parts), parts[0].shape
    feats = weight.shape[0]
    tok = share * n_row
    rows = tok // n_col
    return pl.pallas_call(
        functools.partial(down_kernel, n_col, n_row),
        grid=(feats // width,),
        in_specs=[SMEM_SPEC, SMEM_SPEC]
        + [pl.BlockSpec((2, share, depth), lambda n: (0, 0, 0))] * n_row
        + [pl.BlockSpec((width, depth), lambda n: (n, 0))],
        out_specs=pl.BlockSpec((n_col, 2, rows, width), lambda n: (0, 0, 0, n)),
        out_shape=jax.ShapeDtypeStruct((n_col, 2, rows, feats), BF16),
        scratch_shapes=[
            pltpu.VMEM((2 * tok, depth), BF16),
            pltpu.VMEM((width, depth), BF16),
            pltpu.VMEM((2 * tok, width), F32),
        ],
        cost_estimate=COST,
        compiler_params=params(),
        name="down",
    )(pos, mask, *parts, weight)


def grad_kernel(n_col, n_row, n_z, pos_ref, *refs):
    near, far = refs[:n_col], refs[n_col : 2 * n_col + 1]
    hidden = refs[2 * n_col + 1 : 2 * n_col + 1 + n_row]
    mine_ref, other_ref, x_ref, h_ref, sum_ref = refs[-5:]
    rows = near[0].shape[2]
    share = hidden[0].shape[2]
    tok = rows * 2 * n_col

    @pl.when(pl.program_id(0) == 0)
    def _():
        for k in range(n_row):
            owner = lax.rem(pos_ref[0] + n_row - k, n_row)
            for z in range(n_z):
                behind = lax.rem(pos_ref[1] + n_z - z, n_z)
                first = pl.multiple_of(behind * tok + owner * share, share)
                for t in range(2):
                    h_ref[t, pl.ds(first, share), :] = hidden[k][z, t]

    for t in range(2):
        for j in range(n_col):
            for side in range(2):
                first = (2 * j + side) * rows
                x_ref[t, pl.ds(first, rows), :] = near[j][side, t]
                source = far[n_col if j == 2 and side == 1 else j]
                for z in range(1, n_z):
                    at = 0 if j == 2 else side
                    x_ref[t, pl.ds(z * tok + first, rows), :] = source[at, z - 1, t]
    over_tokens = (((0,), (0,)), ((), ()))
    total = lax.dot_general(x_ref[1], h_ref[0], over_tokens, preferred_element_type=F32)
    total += lax.dot_general(x_ref[0], h_ref[1], over_tokens, preferred_element_type=F32)
    sum_ref[...] = total
    mine = pl.multiple_of(pos_ref[2] * BLOCK, BLOCK)
    mine_ref[...] = sum_ref[:, pl.ds(mine, BLOCK)]
    other_ref[...] = sum_ref[:, pl.ds(BLOCK - mine, BLOCK)]


def grad(pos, near, far, hidden, width=512):
    n_col, n_row = len(near), len(hidden)
    _, _, rows, feats = near[0].shape
    n_z, _, share, cols = hidden[0].shape
    tok = n_z * rows * 2 * n_col
    return pl.pallas_call(
        functools.partial(grad_kernel, n_col, n_row, n_z),
        grid=(feats // width,),
        in_specs=[SMEM_SPEC]
        + [pl.BlockSpec((2, 2, rows, width), lambda n: (0, 0, 0, n))] * n_col
        + [
            pl.BlockSpec((f.shape[0], n_z - 1, 2, rows, width), lambda n: (0, 0, 0, 0, n))
            for f in far
        ]
        + [pl.BlockSpec((n_z, 2, share, cols), lambda n: (0, 0, 0, 0))] * n_row,
        out_specs=[pl.BlockSpec((width, BLOCK), lambda n: (n, 0))] * 2,
        out_shape=[jax.ShapeDtypeStruct((feats, BLOCK), F32)] * 2,
        scratch_shapes=[
            pltpu.VMEM((2, tok, width), BF16),
            pltpu.VMEM((2, tok, cols), BF16),
            pltpu.VMEM((width, cols), F32),
        ],
        cost_estimate=COST,
        compiler_params=params(),
        name="grad",
    )(pos, *near, *far, *hidden)


def finish_kernel(norm_scale, pos_ref, mask_ref, a_ref, b_ref, out_ref):
    blocks = a_ref.shape[0] // BLOCK
    for i in range(blocks):
        kept = mask_ref[pl.program_id(0) * blocks + i, pos_ref[3]] != 0
        part = pl.ds(i * BLOCK, BLOCK)
        total = (a_ref[part, :] + b_ref[part, :]) * norm_scale
        total = jnp.where(kept, total, jnp.zeros_like(total))
        out_ref[pl.ds(2 * i * BLOCK, BLOCK, 2), :] = total[:, :128]
        out_ref[pl.ds(2 * i * BLOCK + 1, BLOCK, 2), :] = total[:, 128:]


def finish(pos, mask, mine, theirs, norm_scale, height=1024):
    feats = mine.shape[0]
    block = pl.BlockSpec((height, BLOCK), lambda n: (n, 0))
    return pl.pallas_call(
        functools.partial(finish_kernel, norm_scale),
        grid=(feats // height,),
        in_specs=[SMEM_SPEC, SMEM_SPEC, block, block],
        out_specs=pl.BlockSpec((2 * height, 128), lambda n: (n, 0)),
        out_shape=jax.ShapeDtypeStruct((2 * feats, 128), F32),
        cost_estimate=COST,
        compiler_params=params(),
        name="finish",
    )(pos, mask, mine, theirs)


def on_device(tokens, cotangent, weight, block_mask):
    n_dp, n_row, n_col = (lax.axis_size(a) for a in ("dp", "row", "col"))
    n_z = n_dp // 2
    n_x = n_col // 2
    dp_at, col_at = lax.axis_index("dp"), lax.axis_index("col")
    pos = jnp.stack(
        [lax.axis_index("row"), dp_at // 2, dp_at % 2, dp_at, col_at % n_x, col_at // n_x]
    ).astype(jnp.int32)
    both = jnp.stack([tokens, cotangent])

    pair = jnp.stack([both, shift_col(both, 0, 1)])
    near = [pair] + [shift_col(pair, j) for j in range(1, n_x)]
    far = [shift(pair, "dp", 2 * k) for k in range(1, n_z)]

    own, *sends = up(pos, block_mask, near, weight, n_row)
    recv = [shift(s, "row", k + 1) for k, s in enumerate(sends)]
    own, recv, far = lax.optimization_barrier((own, recv, far))
    far = jnp.stack(far, axis=1)
    left, right = shift_col(far, 1), shift_col(far, -1)
    z_groups = [list(range(c, n_dp, 2)) for c in range(2)]
    acts = act(own, recv)
    acts_all = [acts] + [shift(acts, "row", k) for k in range(1, n_row)]
    pieces = acts.reshape(2, acts.shape[1], n_z, -1).transpose(2, 0, 1, 3)
    pieces = lax.all_to_all(pieces, "dp", 0, 0, axis_index_groups=z_groups)
    acts_all, pieces, left, right = lax.optimization_barrier((acts_all, pieces, left, right))
    pieces_all = [pieces] + [shift(pieces, "row", k) for k in range(1, n_row)]
    across = [shift_col(left[:1], 1), shift_col(right[1:], -1)]
    far = [far, left, across[0], right, across[1]]

    sends = down(pos, block_mask, acts_all, weight, n_col)
    sends, near = lax.optimization_barrier((sends, near))
    total = lax.all_to_all(sends, "col", 0, 0).astype(F32).sum(axis=0) + both.astype(F32)
    output, input_grad = total[0].astype(BF16), total[1].astype(BF16)

    mine, given = grad(pos, near, far, pieces_all)
    theirs = lax.ppermute(given, "dp", [(i, i ^ 1) for i in range(n_dp)])
    tok_total = tokens.shape[0] * n_col * n_dp
    weight_grad = finish(pos, block_mask, mine, theirs, 1.0 / math.sqrt(tok_total))
    return output, input_grad, weight_grad.reshape(weight.shape[0], 1, BLOCK)


def solution(mesh):
    in_specs = (P(("dp", "col"), "row"), P(("dp", "col"), "row"), P("row", "col"), P("row", "col"))
    out_specs = (P(("dp", "col"), "row"), P(("dp", "col"), "row"), P("row", "dp", "col"))
    return jax.shard_map(
        on_device, mesh=mesh, in_specs=in_specs, out_specs=out_specs, check_vma=False
    )
```

time: 288 us -> 198 us (0.69); the launches traced: 284 us -> 197 us
  starting transfers between devices: 143 us -> 43 us
  waiting for transfers between devices: 87.7 us -> 108 us
  Pallas kernels: 42.7 us -> 34.3 us
  local copies, waits for them, and re-layouts: 7.03 us -> 10.2 us
    ppermute x36 -> x12, starting transfers between devices: 134 us -> 18.9 us  [shift(): lax.ppermute(value, axis, [(i, (i + by) % size) for i in range(size)])]
    ppermute x0 -> x8, waiting for transfers between devices: none -> 32.1 us  [shift_col(): return lax.ppermute(value, 'col', pairs)]
    ppermute x36 -> x12, waiting for transfers between devices: 87.7 us -> 71.5 us  [shift(): lax.ppermute(value, axis, [(i, (i + by) % size) for i in range(size)])]
    all_to_all x0 -> x2, starting transfers between devices: none -> 11.8 us  [the longest x1 8.24 us: on_device(): pieces = lax.all_to_all(pieces, 'dp', 0, 0, axis_index_groups=z_groups)]
    ppermute x0 -> x8, starting transfers between devices: none -> 11.4 us  [shift_col(): return lax.ppermute(value, 'col', pairs)]
    ppermute x1, starting transfers between devices: 8.21 us -> 0.88 us  [on_device(): theirs = lax.ppermute(given, 'dp', [(i, i ^ 1) for i in range(n_dp)])]
    pallas_call x3 -> x2, Pallas kernels: 18.4 us -> 12.6 us  [the longest x1 9.76 us: grad(): pl.pallas_call(functools.partial(grad_kernel, n_col, n_row, n_z), grid=(f...]
    ppermute x1, waiting for transfers between devices: 0.01 us -> 4 us  [on_device(): theirs = lax.ppermute(given, 'dp', [(i, i ^ 1) for i in range(n_dp)])]
  transfers between devices with their start and end apart: 37 -> 23, of which waited for: 13 -> 15; matrix products, arithmetic and copies ran while one was open for 1% -> 3% of each run, Pallas kernels for 10% -> 13%
where the time goes in v2:
time: 198 us; the launch traced here: 197 us
  waiting for transfers between devices  108 us (55%)
  starting transfers between devices  43 us (22%)
  Pallas kernels  34.3 us (17%)
  local copies, waits for them, and re-layouts  10.2 us (5%)
    ppermute x12, waiting for transfers between devices, shift(): lax.ppermute(value, axis, [(i, (i + by) % size) for i in range(size)])  71.5 us
    ppermute x8, waiting for transfers between devices, shift_col(): return lax.ppermute(value, 'col', pairs)  32.1 us
    ppermute x12, starting transfers between devices, shift(): lax.ppermute(value, axis, [(i, (i + by) % size) for i in range(size)])  18.9 us
    ppermute x8, starting transfers between devices, shift_col(): return lax.ppermute(value, 'col', pairs)  11.4 us
    pallas_call x1, Pallas kernels, grad(): pl.pallas_call(functools.partial(grad_kernel, n_col, n_row, n_z), grid=(f...  9.76 us
    pallas_call x1, Pallas kernels, up(): pl.pallas_call(functools.partial(up_kernel, n_col, n_row), grid=(cols //...  9.24 us
    pallas_call x1, Pallas kernels, down(): pl.pallas_call(functools.partial(down_kernel, n_col, n_row), grid=(feats...  9.15 us
    all_to_all x1, starting transfers between devices, on_device(): pieces = lax.all_to_all(pieces, 'dp', 0, 0, axis_index_groups=z_groups)  8.24 us
  transfers between devices with their start and end apart: 23, of which 15 were waited for; matrix products, arithmetic and copies ran while one was open for 3% of the time, Pallas kernels for 13%

profile of v2, /device:TPU:1, one launch (start us, length us, event | category | flops | bytes accessed | tf_op | source)
XLA Modules:
  0.0 197.5 jit_solution(9019072444335147917)
XLA Ops:
  0.6 1.0 fusion
  1.6 2.6 %collective-permute-start = (bf16[2,32,2048]{2,1,0:T(8,128)(2,1)S(1)}, bf16[2,32,2048]{2,1,0:T(8,128)(2,1)S(1)}, u32[]{:S(2)}, u32[]{:S(2)}) collective-permute-start(bf16[2,32,2048]{2,1,0:T(8,128)(2,1)S(1)} %get-tuple-element.62), channel_id=1, source_target_pairs={{0,4},{1,5},{2,6},{3,7},{4,0},{5,1},{6,2},{7,3},{8,12},{9,13},{10,... | collective-permute-start | bytes 786440 | tf_op jit(solution)/shard_map/ppermute | solution.py:26
  4.2 5.0 %collective-permute-done = bf16[2,32,2048]{2,1,0:T(8,128)(2,1)S(1)} collective-permute-done((bf16[2,32,2048]{2,1,0:T(8,128)(2,1)S(1)}, bf16[2,32,2048]{2,1,0:T(8,128)(2,1)S(1)}, u32[]{:S(2)}, u32[]{:S(2)}) %collective-permute-start) | collective-permute-done | bytes 262176 | tf_op jit(solution)/shard_map/ppermute | solution.py:26
  9.2 3.5 %collective-permute-start.3 = (bf16[2,2,32,2048]{3,2,1,0:T(8,128)(2,1)S(1)}, bf16[2,2,32,2048]{3,2,1,0:T(8,128)(2,1)S(1)}, u32[]{:S(2)}, u32[]{:S(2)}) collective-permute-start(bf16[2,2,32,2048]{3,2,1,0:T(8,128)(2,1)S(1)} %pad_maximum_fusion.1.refs_0_), channel_id=1, source_target_pairs={{0,3},{1,0},{2,1},{3,2},{4,7},{5,4},{6,5},{7,6},{8,11},{9,8},{10,9... | collective-permute-start | bytes 1572872 | tf_op jit(solution)/shard_map/ppermute | solution.py:26
  13.2 0.6 collective-permute-start.1
  13.9 5.6 %collective-permute-start.9 = (bf16[2,2,32,2048]{3,2,1,0:T(8,128)(2,1)S(1)}, bf16[2,2,32,2048]{3,2,1,0:T(8,128)(2,1)S(1)}, u32[]{:S(2)}, u32[]{:S(2)}) collective-permute-start(bf16[2,2,32,2048]{3,2,1,0:T(8,128)(2,1)S(1)} %pad_maximum_fusion.1.refs_0_), channel_id=1, source_target_pairs={{0,192},{32,224},{64,0},{96,32},{128,64},{160,96},{192,128},{224,1... | collective-permute-start | bytes 1572872 | tf_op jit(solution)/shard_map/ppermute | solution.py:20
  19.5 0.6 stack.57.pos_ref
  20.1 0.9 collective-permute-start.8
  21.0 2.9 %collective-permute-done.3.refs_3_ = bf16[2,2,32,2048]{3,2,1,0:T(8,128)(2,1)S(1)} collective-permute-done((bf16[2,2,32,2048]{3,2,1,0:T(8,128)(2,1)S(1)}, bf16[2,2,32,2048]{3,2,1,0:T(8,128)(2,1)S(1)}, u32[]{:S(2)}, u32[]{:S(2)}) %collective-permute-start.3) | collective-permute-done | bytes 524320 | tf_op jit(solution)/shard_map/ppermute | solution.py:26
  23.9 2.5 %collective-permute-start.7 = (bf16[2,2,32,2048]{3,2,1,0:T(8,128)(2,1)S(1)}, bf16[2,2,32,2048]{3,2,1,0:T(8,128)(2,1)S(1)}, u32[]{:S(2)}, u32[]{:S(2)}) collective-permute-start(bf16[2,2,32,2048]{3,2,1,0:T(8,128)(2,1)S(1)} %pad_maximum_fusion.1.refs_0_), channel_id=1, source_target_pairs={{0,64},{32,96},{64,128},{96,160},{128,192},{160,224},{192,0},{224,... | collective-permute-start | bytes 1572872 | tf_op jit(solution)/shard_map/ppermute | solution.py:20
  26.4 12.9 %collective-permute-done.1.refs_1_ = bf16[2,2,32,2048]{3,2,1,0:T(8,128)(2,1)S(1)} collective-permute-done((bf16[2,2,32,2048]{3,2,1,0:T(8,128)(2,1)S(1)}, bf16[2,2,32,2048]{3,2,1,0:T(8,128)(2,1)S(1)}, u32[]{:S(2)}, u32[]{:S(2)}) %collective-permute-start.1) | collective-permute-done | bytes 524320 | tf_op jit(solution)/shard_map/ppermute | solution.py:26
  39.3 0.8 copy-done.6
  40.1 9.2 %up.1 = (f32[2,64,2048]{2,1,0:T(8,128)}, bf16[2,64,2048]{2,1,0:T(8,128)(2,1)}, bf16[2,64,2048]{2,1,0:T(8,128)(2,1)}, bf16[2,64,2048]{2,1,0:T(8,128)(2,1)}) custom-call(s32[6]{0:T(128)} %stack.57.pos_ref, s32[8,8]{1,0:T(8,128)} %mask_ref.5, bf16[2,2,32,2048]{3,2,1,0:T(8,128)(2,1)} %copy-done.2, bf16[2,2,32,2048]{3,2,1,0:T(8,128)(2,1)} %copy-done.6, ...), custom_call_target="tpu_custom_call" | custom-call | flops 1 | bytes 1 | tf_op jit(solution)/shard_map/up/pallas_call | solution.py:77
  49.4 1.3 collective-permute-start.4
  50.7 2.6 %collective-permute-start.5 = (bf16[2,64,2048]{2,1,0:T(8,128)(2,1)}, bf16[2,64,2048]{2,1,0:T(8,128)(2,1)S(1)}, u32[]{:S(2)}, u32[]{:S(2)}) collective-permute-start(bf16[2,64,2048]{2,1,0:T(8,128)(2,1)} %get-tuple-element.30), channel_id=1, source_target_pairs={{0,16},{8,24},{16,0},{24,8},{1,17},{9,25},{17,1},{25,9},{2,18},{10... | collective-permute-start | bytes 1572872 | tf_op jit(solution)/shard_map/ppermute | solution.py:20
  53.3 1.1 collective-permute-start.6
  54.4 0.9 collective-permute-done.7
  55.3 8.2 %collective-permute-done.4.refs_1_ = bf16[2,64,2048]{2,1,0:T(8,128)(2,1)S(1)} collective-permute-done((bf16[2,64,2048]{2,1,0:T(8,128)(2,1)}, bf16[2,64,2048]{2,1,0:T(8,128)(2,1)S(1)}, u32[]{:S(2)}, u32[]{:S(2)}) %collective-permute-start.4) | collective-permute-done | bytes 524320 | tf_op jit(solution)/shard_map/ppermute | solution.py:20
  63.5 12.3 %collective-permute-done.5.refs_2_ = bf16[2,64,2048]{2,1,0:T(8,128)(2,1)S(1)} collective-permute-done((bf16[2,64,2048]{2,1,0:T(8,128)(2,1)}, bf16[2,64,2048]{2,1,0:T(8,128)(2,1)S(1)}, u32[]{:S(2)}, u32[]{:S(2)}) %collective-permute-start.5) | collective-permute-done | bytes 524320 | tf_op jit(solution)/shard_map/ppermute | solution.py:20
  76.1 1.5 collective-permute-start.13
  77.6 2.9 %act.1.refs_0_ = bf16[2,64,2048]{2,1,0:T(8,128)(2,1)} custom-call(f32[2,64,2048]{2,1,0:T(8,128)} %get-tuple-element.32.refs_0_, bf16[2,64,2048]{2,1,0:T(8,128)(2,1)} %copy-done.12, bf16[2,64,2048]{2,1,0:T(8,128)(2,1)} %copy-done.13, bf16[2,64,2048]{2,1,0:T(8,128)(2,1)} %copy-done.14), custom_call_target="tpu_custom_call" | custom-call | flops 1 | bytes 1 | tf_op jit(solution)/shard_map/act/pallas_call | solution.py:112
  80.5 2.0 copy.16
  82.4 8.2 %all-to-all-start = ((bf16[4,2,64,512]{3,2,1,0:T(8,128)(2,1)}), bf16[4,2,64,512]{3,2,1,0:T(8,128)(2,1)S(1)}, u32[]{:S(2)}, u32[]{:S(2)}) async-start(bf16[4,2,64,512]{3,2,1,0:T(8,128)(2,1)} %bitcast.29), calls=%async_computation | async-start | bytes 1048576 | tf_op jit(solution)/shard_map/all_to_all | solution.py:290
  90.7 2.7 %collective-permute-start.12 = (bf16[2,64,2048]{2,1,0:T(8,128)(2,1)S(1)}, bf16[2,64,2048]{2,1,0:T(8,128)(2,1)S(1)}, u32[]{:S(2)}, u32[]{:S(2)}) collective-permute-start(bf16[2,64,2048]{2,1,0:T(8,128)(2,1)S(1)} %copy-done.1), channel_id=1, source_target_pairs={{0,24},{8,0},{16,8},{24,16},{1,25},{9,1},{17,9},{25,17},{2,26},{10... | collective-permute-start | bytes 1572872 | tf_op jit(solution)/shard_map/ppermute | solution.py:20
  93.5 0.6 collective-permute-start.10
  94.1 11.1 %collective-permute-done.12.refs_3_ = bf16[2,64,2048]{2,1,0:T(8,128)(2,1)S(1)} collective-permute-done((bf16[2,64,2048]{2,1,0:T(8,128)(2,1)S(1)}, bf16[2,64,2048]{2,1,0:T(8,128)(2,1)S(1)}, u32[]{:S(2)}, u32[]{:S(2)}) %collective-permute-start.12) | collective-permute-done | bytes 524320 | tf_op jit(solution)/shard_map/ppermute | solution.py:20
  105.2 1.6 collective-permute-done.11.refs_2_
  106.8 0.8 copy-done.11
  107.6 12.1 %collective-permute-done.10.refs_1_ = bf16[2,64,2048]{2,1,0:T(8,128)(2,1)} collective-permute-done((bf16[2,64,2048]{2,1,0:T(8,128)(2,1)S(1)}, bf16[2,64,2048]{2,1,0:T(8,128)(2,1)}, u32[]{:S(2)}, u32[]{:S(2)}) %collective-permute-start.10) | collective-permute-done | bytes 524320 | tf_op jit(solution)/shard_map/ppermute | solution.py:20
  119.8 9.2 %down.1 = bf16[8,2,32,2048]{3,2,1,0:T(8,128)(2,1)} custom-call(s32[6]{0:T(128)} %stack.57.pos_ref, s32[8,8]{1,0:T(8,128)} %mask_ref.5, bf16[2,64,2048]{2,1,0:T(8,128)(2,1)} %act.1.refs_0_, bf16[2,64,2048]{2,1,0:T(8,128)(2,1)} %collective-permute-done.10.refs_1_, bf16[2,64,2048]{2,1,0:T(8,128)(2,1)} %copy-done.11, bf16[2,64,2048]{2,1,0:T(8,128)(2,1)} %copy-done.10, ...), custom_call_target="tpu_custom_call" | custom-call | flops 1 | bytes 1 | tf_op jit(solution)/shard_map/down/pallas_call | solution.py:158
  128.9 3.6 %all-to-all-start.1 = ((bf16[8,2,32,2048]{3,2,1,0:T(8,128)(2,1)}), bf16[8,2,32,2048]{3,2,1,0:T(8,128)(2,1)S(1)}, u32[]{:S(2)}, u32[]{:S(2)}) async-start(bf16[8,2,32,2048]{3,2,1,0:T(8,128)(2,1)} %down.1), calls=%async_computation.1 | async-start | bytes 4194304 | tf_op jit(solution)/shard_map/all_to_all | solution.py:298
  132.5 1.2 slice.16
  133.7 1.2 slice.17
  135.0 2.7 %collective-permute-start.16 = (bf16[1,3,2,32,2048]{4,3,2,1,0:T(8,128)(2,1)S(1)}, bf16[1,3,2,32,2048]{4,3,2,1,0:T(8,128)(2,1)S(1)}, u32[]{:S(2)}, u32[]{:S(2)}) collective-permute-start(bf16[1,3,2,32,2048]{4,3,2,1,0:T(8,128)(2,1)S(1)} %slice.17), channel_id=1, source_target_pairs={{0,3},{1,0},{2,1},{3,2},{4,7},{5,4},{6,5},{7,6},{8,11},{9,8},{10,9... | collective-permute-start | bytes 2359304 | tf_op jit(solution)/shard_map/ppermute | solution.py:26
  138.1 1.0 collective-permute-start.17
  139.1 10.7 %collective-permute-done.19.refs_12_ = bf16[4,2,64,512]{3,2,1,0:T(8,128)(2,1)S(1)} collective-permute-done((bf16[4,2,64,512]{3,2,1,0:T(8,128)(2,1)S(1)}, bf16[4,2,64,512]{3,2,1,0:T(8,128)(2,1)S(1)}, u32[]{:S(2)}, u32[]{:S(2)}) %collective-permute-start.19) | collective-permute-done | bytes 524320 | tf_op jit(solution)/shard_map/ppermute | solution.py:20
  149.8 0.7 collective-permute-done.18.refs_11_
  150.5 13.7 %collective-permute-done.17.refs_10_ = bf16[4,2,64,512]{3,2,1,0:T(8,128)(2,1)S(1)} collective-permute-done((bf16[4,2,64,512]{3,2,1,0:T(8,128)(2,1)S(1)}, bf16[4,2,64,512]{3,2,1,0:T(8,128)(2,1)S(1)}, u32[]{:S(2)}, u32[]{:S(2)}) %collective-permute-start.17) | collective-permute-done | bytes 524320 | tf_op jit(solution)/shard_map/ppermute | solution.py:20
  164.2 9.5 %collective-permute-done.16.refs_8_ = bf16[1,3,2,32,2048]{4,3,2,1,0:T(8,128)(2,1)S(1)} collective-permute-done((bf16[1,3,2,32,2048]{4,3,2,1,0:T(8,128)(2,1)S(1)}, bf16[1,3,2,32,2048]{4,3,2,1,0:T(8,128)(2,1)S(1)}, u32[]{:S(2)}, u32[]{:S(2)}) %collective-permute-start.16) | collective-permute-done | bytes 786464 | tf_op jit(solution)/shard_map/ppermute | solution.py:26
  173.7 1.8 collective-permute-done.15.refs_6_
  175.5 0.9 copy-done.9
  176.4 9.8 %grad.1 = (f32[2048,256]{1,0:T(8,128)}, f32[2048,256]{1,0:T(8,128)}) custom-call(s32[6]{0:T(128)} %stack.57.pos_ref, bf16[2,2,32,2048]{3,2,1,0:T(8,128)(2,1)} %copy-done.2, bf16[2,2,32,2048]{3,2,1,0:T(8,128)(2,1)} %copy-done.6, bf16[2,2,32,2048]{3,2,1,0:T(8,128)(2,1)} %copy-done.5, bf16[2,2,32,2048]{3,2,1,0:T(8,128)(2,1)} %copy-done.4, ...), custom_call_target="tpu_custom_call" | custom-call | flops 1 | bytes 1 | tf_op jit(solution)/shard_map/grad/pallas_call | solution.py:218
  186.2 0.9 collective-permute-start.20
  187.1 4.0 %collective-permute-done.20.b_ref = f32[2048,256]{1,0:T(8,128)S(1)} collective-permute-done((f32[2048,256]{1,0:T(8,128)}, f32[2048,256]{1,0:T(8,128)S(1)}, u32[]{:S(2)}, u32[]{:S(2)}) %collective-permute-start.20) | collective-permute-done | bytes 2097184 | tf_op jit(solution)/shard_map/ppermute | solution.py:302
  191.1 1.4 copy-done.3
  192.4 3.3 %finish.1 = f32[4096,128]{1,0:T(8,128)} custom-call(s32[6]{0:T(128)} %stack.57.pos_ref, s32[8,8]{1,0:T(8,128)} %mask_ref.5, f32[2048,256]{1,0:T(8,128)} %get-tuple-element.51.a_ref, f32[2048,256]{1,0:T(8,128)} %copy-done.3), custom_call_target="tpu_custom_call" | custom-call | flops 1 | bytes 1 | tf_op jit(solution)/shard_map/finish/pallas_call | solution.py:255
  196.1 0.5 copy-done.15
  196.8 0.7 slice_bitcast_fusion
  (53 shorter events, 2.0 us)
Async XLA Ops:
  1.6 7.5 %collective-permute-start = (bf16[2,32,2048]{2,1,0:T(8,128)(2,1)S(1)}, bf16[2,32,2048]{2,1,0:T(8,128)(2,1)S(1)}, u32[]{:S(2)}, u32[]{:S(2)}) collective-permute-start(bf16[2,32,2048]{2,1,0:T(8,128)(2,1)S(1)} %get-tuple-element.62), channel_id=1, source_target_pairs={{0,4},{1,5},{2,6},{3,7},{4,0},{5,1},{6,2},{7,3},{8,12},{9,13},{10,... | collective-permute-start | bytes 786440 | tf_op jit(solution)/shard_map/ppermute | solution.py:26
  9.2 30.1 %copy-start.2 = (bf16[2,2,32,2048]{3,2,1,0:T(8,128)(2,1)}, bf16[2,2,32,2048]{3,2,1,0:T(8,128)(2,1)S(1)}, u32[]{:S(2)}) copy-start(bf16[2,2,32,2048]{3,2,1,0:T(8,128)(2,1)S(1)} %pad_maximum_fusion.1.refs_0_) | copy-start | bytes 1572868
  9.2 14.7 %collective-permute-start.3 = (bf16[2,2,32,2048]{3,2,1,0:T(8,128)(2,1)S(1)}, bf16[2,2,32,2048]{3,2,1,0:T(8,128)(2,1)S(1)}, u32[]{:S(2)}, u32[]{:S(2)}) collective-permute-start(bf16[2,2,32,2048]{3,2,1,0:T(8,128)(2,1)S(1)} %pad_maximum_fusion.1.refs_0_), channel_id=1, source_target_pairs={{0,3},{1,0},{2,1},{3,2},{4,7},{5,4},{6,5},{7,6},{8,11},{9,8},{10,9... | collective-permute-start | bytes 1572872 | tf_op jit(solution)/shard_map/ppermute | solution.py:26
  12.7 13.7 %collective-permute-start.2 = (bf16[2,2,32,2048]{3,2,1,0:T(8,128)(2,1)S(1)}, bf16[2,2,32,2048]{3,2,1,0:T(8,128)(2,1)S(1)}, u32[]{:S(2)}, u32[]{:S(2)}) collective-permute-start(bf16[2,2,32,2048]{3,2,1,0:T(8,128)(2,1)S(1)} %pad_maximum_fusion.1.refs_0_), channel_id=1, source_target_pairs={{0,2},{1,3},{2,0},{3,1},{4,6},{5,7},{6,4},{7,5},{8,10},{9,11},{10,... | collective-permute-start | bytes 1572872 | tf_op jit(solution)/shard_map/ppermute | solution.py:26
  13.2 26.1 %collective-permute-start.1 = (bf16[2,2,32,2048]{3,2,1,0:T(8,128)(2,1)S(1)}, bf16[2,2,32,2048]{3,2,1,0:T(8,128)(2,1)S(1)}, u32[]{:S(2)}, u32[]{:S(2)}) collective-permute-start(bf16[2,2,32,2048]{3,2,1,0:T(8,128)(2,1)S(1)} %pad_maximum_fusion.1.refs_0_), channel_id=1, source_target_pairs={{0,1},{1,2},{2,3},{3,0},{4,5},{5,6},{6,7},{7,4},{8,9},{9,10},{10,1... | collective-permute-start | bytes 1572872 | tf_op jit(solution)/shard_map/ppermute | solution.py:26
  13.9 39.5 %collective-permute-start.9 = (bf16[2,2,32,2048]{3,2,1,0:T(8,128)(2,1)S(1)}, bf16[2,2,32,2048]{3,2,1,0:T(8,128)(2,1)S(1)}, u32[]{:S(2)}, u32[]{:S(2)}) collective-permute-start(bf16[2,2,32,2048]{3,2,1,0:T(8,128)(2,1)S(1)} %pad_maximum_fusion.1.refs_0_), channel_id=1, source_target_pairs={{0,192},{32,224},{64,0},{96,32},{128,64},{160,96},{192,128},{224,1... | collective-permute-start | bytes 1572872 | tf_op jit(solution)/shard_map/ppermute | solution.py:20
  20.1 34.3 %collective-permute-start.8 = (bf16[2,2,32,2048]{3,2,1,0:T(8,128)(2,1)S(1)}, bf16[2,2,32,2048]{3,2,1,0:T(8,128)(2,1)S(1)}, u32[]{:S(2)}, u32[]{:S(2)}) collective-permute-start(bf16[2,2,32,2048]{3,2,1,0:T(8,128)(2,1)S(1)} %pad_maximum_fusion.1.refs_0_), channel_id=1, source_target_pairs={{0,128},{32,160},{64,192},{96,224},{128,0},{160,32},{192,64},{224,... | collective-permute-start | bytes 1572872 | tf_op jit(solution)/shard_map/ppermute | solution.py:20
  23.9 15.4 %copy-start.4 = (bf16[2,2,32,2048]{3,2,1,0:T(8,128)(2,1)}, bf16[2,2,32,2048]{3,2,1,0:T(8,128)(2,1)S(1)}, u32[]{:S(2)}) copy-start(bf16[2,2,32,2048]{3,2,1,0:T(8,128)(2,1)S(1)} %collective-permute-done.3.refs_3_) | copy-start | bytes 1572868
  23.9 31.4 %collective-permute-start.7 = (bf16[2,2,32,2048]{3,2,1,0:T(8,128)(2,1)S(1)}, bf16[2,2,32,2048]{3,2,1,0:T(8,128)(2,1)S(1)}, u32[]{:S(2)}, u32[]{:S(2)}) collective-permute-start(bf16[2,2,32,2048]{3,2,1,0:T(8,128)(2,1)S(1)} %pad_maximum_fusion.1.refs_0_), channel_id=1, source_target_pairs={{0,64},{32,96},{64,128},{96,160},{128,192},{160,224},{192,0},{224,... | collective-permute-start | bytes 1572872 | tf_op jit(solution)/shard_map/ppermute | solution.py:20
  26.4 12.9 %copy-start.5 = (bf16[2,2,32,2048]{3,2,1,0:T(8,128)(2,1)}, bf16[2,2,32,2048]{3,2,1,0:T(8,128)(2,1)S(1)}, u32[]{:S(2)}) copy-start(bf16[2,2,32,2048]{3,2,1,0:T(8,128)(2,1)S(1)} %collective-permute-done.2.refs_2_) | copy-start | bytes 1572868
  39.3 0.8 copy-start.6
  49.4 14.1 %collective-permute-start.4 = (bf16[2,64,2048]{2,1,0:T(8,128)(2,1)}, bf16[2,64,2048]{2,1,0:T(8,128)(2,1)S(1)}, u32[]{:S(2)}, u32[]{:S(2)}) collective-permute-start(bf16[2,64,2048]{2,1,0:T(8,128)(2,1)} %get-tuple-element.29), channel_id=1, source_target_pairs={{0,8},{8,16},{16,24},{24,0},{1,9},{9,17},{17,25},{25,1},{2,10},{10... | collective-permute-start | bytes 1572872 | tf_op jit(solution)/shard_map/ppermute | solution.py:20
  50.7 25.2 %collective-permute-start.5 = (bf16[2,64,2048]{2,1,0:T(8,128)(2,1)}, bf16[2,64,2048]{2,1,0:T(8,128)(2,1)S(1)}, u32[]{:S(2)}, u32[]{:S(2)}) collective-permute-start(bf16[2,64,2048]{2,1,0:T(8,128)(2,1)} %get-tuple-element.30), channel_id=1, source_target_pairs={{0,16},{8,24},{16,0},{24,8},{1,17},{9,25},{17,1},{25,9},{2,18},{10... | collective-permute-start | bytes 1572872 | tf_op jit(solution)/shard_map/ppermute | solution.py:20
  53.3 22.5 %collective-permute-start.6 = (bf16[2,64,2048]{2,1,0:T(8,128)(2,1)}, bf16[2,64,2048]{2,1,0:T(8,128)(2,1)S(1)}, u32[]{:S(2)}, u32[]{:S(2)}) collective-permute-start(bf16[2,64,2048]{2,1,0:T(8,128)(2,1)} %get-tuple-element.31), channel_id=1, source_target_pairs={{0,24},{8,0},{16,8},{24,16},{1,25},{9,1},{17,9},{25,17},{2,26},{10... | collective-permute-start | bytes 1572872 | tf_op jit(solution)/shard_map/ppermute | solution.py:20
  63.5 14.1 %copy-start.12 = (bf16[2,64,2048]{2,1,0:T(8,128)(2,1)}, bf16[2,64,2048]{2,1,0:T(8,128)(2,1)S(1)}, u32[]{:S(2)}) copy-start(bf16[2,64,2048]{2,1,0:T(8,128)(2,1)S(1)} %collective-permute-done.4.refs_1_) | copy-start | bytes 1572868
  75.8 1.7 copy-start.13
  75.8 1.7 copy-start.14
  76.0 6.4 %copy-start = (bf16[2,3,2,32,2048]{4,3,2,1,0:T(8,128)(2,1)}, bf16[2,3,2,32,2048]{4,3,2,1,0:T(8,128)(2,1)S(1)}, u32[]{:S(2)}) copy-start(bf16[2,3,2,32,2048]{4,3,2,1,0:T(8,128)(2,1)S(1)} %pad_maximum_fusion.refs_4_) | copy-start | bytes 4718596
  76.0 43.7 %collective-permute-start.14 = (bf16[2,3,2,32,2048]{4,3,2,1,0:T(8,128)(2,1)S(1)}, bf16[2,3,2,32,2048]{4,3,2,1,0:T(8,128)(2,1)}, u32[]{:S(2)}, u32[]{:S(2)}) collective-permute-start(bf16[2,3,2,32,2048]{4,3,2,1,0:T(8,128)(2,1)S(1)} %pad_maximum_fusion.refs_4_), channel_id=1, source_target_pairs={{0,3},{1,0},{2,1},{3,2},{4,7},{5,4},{6,5},{7,6},{8,11},{9,8},{10,9... | collective-permute-start | bytes 4718600 | tf_op jit(solution)/shard_map/ppermute | solution.py:26
  76.1 43.6 %collective-permute-start.13 = (bf16[2,3,2,32,2048]{4,3,2,1,0:T(8,128)(2,1)S(1)}, bf16[2,3,2,32,2048]{4,3,2,1,0:T(8,128)(2,1)}, u32[]{:S(2)}, u32[]{:S(2)}) collective-permute-start(bf16[2,3,2,32,2048]{4,3,2,1,0:T(8,128)(2,1)S(1)} %pad_maximum_fusion.refs_4_), channel_id=1, source_target_pairs={{0,1},{1,2},{2,3},{3,0},{4,5},{5,6},{6,7},{7,4},{8,9},{9,10},{10,1... | collective-permute-start | bytes 4718600 | tf_op jit(solution)/shard_map/ppermute | solution.py:26
  80.5 10.2 %copy-start.1 = (bf16[2,64,2048]{2,1,0:T(8,128)(2,1)S(1)}, bf16[2,64,2048]{2,1,0:T(8,128)(2,1)}, u32[]{:S(2)}) copy-start(bf16[2,64,2048]{2,1,0:T(8,128)(2,1)} %act.1.refs_0_) | copy-start | bytes 1572868
  82.4 37.3 %all-to-all-start = ((bf16[4,2,64,512]{3,2,1,0:T(8,128)(2,1)}), bf16[4,2,64,512]{3,2,1,0:T(8,128)(2,1)S(1)}, u32[]{:S(2)}, u32[]{:S(2)}) async-start(bf16[4,2,64,512]{3,2,1,0:T(8,128)(2,1)} %bitcast.29), calls=%async_computation | async-start | bytes 1048576 | tf_op jit(solution)/shard_map/all_to_all | solution.py:290
  90.7 14.5 %collective-permute-start.12 = (bf16[2,64,2048]{2,1,0:T(8,128)(2,1)S(1)}, bf16[2,64,2048]{2,1,0:T(8,128)(2,1)S(1)}, u32[]{:S(2)}, u32[]{:S(2)}) collective-permute-start(bf16[2,64,2048]{2,1,0:T(8,128)(2,1)S(1)} %copy-done.1), channel_id=1, source_target_pairs={{0,24},{8,0},{16,8},{24,16},{1,25},{9,1},{17,9},{25,17},{2,26},{10... | collective-permute-start | bytes 1572872 | tf_op jit(solution)/shard_map/ppermute | solution.py:20
  93.4 13.4 %collective-permute-start.11 = (bf16[2,64,2048]{2,1,0:T(8,128)(2,1)S(1)}, bf16[2,64,2048]{2,1,0:T(8,128)(2,1)S(1)}, u32[]{:S(2)}, u32[]{:S(2)}) collective-permute-start(bf16[2,64,2048]{2,1,0:T(8,128)(2,1)S(1)} %copy-done.1), channel_id=1, source_target_pairs={{0,16},{8,24},{16,0},{24,8},{1,17},{9,25},{17,1},{25,9},{2,18},{10... | collective-permute-start | bytes 1572872 | tf_op jit(solution)/shard_map/ppermute | solution.py:20
  93.5 26.2 %collective-permute-start.10 = (bf16[2,64,2048]{2,1,0:T(8,128)(2,1)S(1)}, bf16[2,64,2048]{2,1,0:T(8,128)(2,1)}, u32[]{:S(2)}, u32[]{:S(2)}) collective-permute-start(bf16[2,64,2048]{2,1,0:T(8,128)(2,1)S(1)} %copy-done.1), channel_id=1, source_target_pairs={{0,8},{8,16},{16,24},{24,0},{1,9},{9,17},{17,25},{25,1},{2,10},{10... | collective-permute-start | bytes 1572872 | tf_op jit(solution)/shard_map/ppermute | solution.py:20
  105.2 14.6 %copy-start.10 = (bf16[2,64,2048]{2,1,0:T(8,128)(2,1)}, bf16[2,64,2048]{2,1,0:T(8,128)(2,1)S(1)}, u32[]{:S(2)}) copy-start(bf16[2,64,2048]{2,1,0:T(8,128)(2,1)S(1)} %collective-permute-done.12.refs_3_) | copy-start | bytes 1572868
  106.8 0.8 copy-start.11
  119.7 18.4 %copy-start.7 = (bf16[4,2,64,512]{3,2,1,0:T(8,128)(2,1)}, bf16[4,2,64,512]{3,2,1,0:T(8,128)(2,1)S(1)}, u32[]{:S(2)}) copy-start(bf16[4,2,64,512]{3,2,1,0:T(8,128)(2,1)S(1)} %all-to-all-done.refs_9_) | copy-start | bytes 1572868
  128.9 66.8 %all-to-all-start.1 = ((bf16[8,2,32,2048]{3,2,1,0:T(8,128)(2,1)}), bf16[8,2,32,2048]{3,2,1,0:T(8,128)(2,1)S(1)}, u32[]{:S(2)}, u32[]{:S(2)}) async-start(bf16[8,2,32,2048]{3,2,1,0:T(8,128)(2,1)} %down.1), calls=%async_computation.1 | async-start | bytes 4194304 | tf_op jit(solution)/shard_map/all_to_all | solution.py:298
  135.0 38.7 %collective-permute-start.16 = (bf16[1,3,2,32,2048]{4,3,2,1,0:T(8,128)(2,1)S(1)}, bf16[1,3,2,32,2048]{4,3,2,1,0:T(8,128)(2,1)S(1)}, u32[]{:S(2)}, u32[]{:S(2)}) collective-permute-start(bf16[1,3,2,32,2048]{4,3,2,1,0:T(8,128)(2,1)S(1)} %slice.17), channel_id=1, source_target_pairs={{0,3},{1,0},{2,1},{3,2},{4,7},{5,4},{6,5},{7,6},{8,11},{9,8},{10,9... | collective-permute-start | bytes 2359304 | tf_op jit(solution)/shard_map/ppermute | solution.py:26
  137.6 37.9 %collective-permute-start.15 = (bf16[1,3,2,32,2048]{4,3,2,1,0:T(8,128)(2,1)S(1)}, bf16[1,3,2,32,2048]{4,3,2,1,0:T(8,128)(2,1)S(1)}, u32[]{:S(2)}, u32[]{:S(2)}) collective-permute-start(bf16[1,3,2,32,2048]{4,3,2,1,0:T(8,128)(2,1)S(1)} %slice.16), channel_id=1, source_target_pairs={{0,1},{1,2},{2,3},{3,0},{4,5},{5,6},{6,7},{7,4},{8,9},{9,10},{10,1... | collective-permute-start | bytes 2359304 | tf_op jit(solution)/shard_map/ppermute | solution.py:26
  137.6 12.2 %collective-permute-start.19 = (bf16[4,2,64,512]{3,2,1,0:T(8,128)(2,1)S(1)}, bf16[4,2,64,512]{3,2,1,0:T(8,128)(2,1)S(1)}, u32[]{:S(2)}, u32[]{:S(2)}) collective-permute-start(bf16[4,2,64,512]{3,2,1,0:T(8,128)(2,1)S(1)} %all-to-all-done.refs_9_), channel_id=1, source_target_pairs={{0,24},{8,0},{16,8},{24,16},{1,25},{9,1},{17,9},{25,17},{2,26},{10... | collective-permute-start | bytes 1572872 | tf_op jit(solution)/shard_map/ppermute | solution.py:20
  137.6 12.9 %collective-permute-start.18 = (bf16[4,2,64,512]{3,2,1,0:T(8,128)(2,1)S(1)}, bf16[4,2,64,512]{3,2,1,0:T(8,128)(2,1)S(1)}, u32[]{:S(2)}, u32[]{:S(2)}) collective-permute-start(bf16[4,2,64,512]{3,2,1,0:T(8,128)(2,1)S(1)} %all-to-all-done.refs_9_), channel_id=1, source_target_pairs={{0,16},{8,24},{16,0},{24,8},{1,17},{9,25},{17,1},{25,9},{2,18},{10... | collective-permute-start | bytes 1572872 | tf_op jit(solution)/shard_map/ppermute | solution.py:20
  138.1 26.1 %collective-permute-start.17 = (bf16[4,2,64,512]{3,2,1,0:T(8,128)(2,1)S(1)}, bf16[4,2,64,512]{3,2,1,0:T(8,128)(2,1)S(1)}, u32[]{:S(2)}, u32[]{:S(2)}) collective-permute-start(bf16[4,2,64,512]{3,2,1,0:T(8,128)(2,1)S(1)} %all-to-all-done.refs_9_), channel_id=1, source_target_pairs={{0,8},{8,16},{16,24},{24,0},{1,9},{9,17},{17,25},{25,1},{2,10},{10... | collective-permute-start | bytes 1572872 | tf_op jit(solution)/shard_map/ppermute | solution.py:20
  149.8 25.7 %copy-start.17 = (bf16[4,2,64,512]{3,2,1,0:T(8,128)(2,1)}, bf16[4,2,64,512]{3,2,1,0:T(8,128)(2,1)S(1)}, u32[]{:S(2)}) copy-start(bf16[4,2,64,512]{3,2,1,0:T(8,128)(2,1)S(1)} %collective-permute-done.19.refs_12_) | copy-start | bytes 1572868
  150.5 25.0 %copy-start.18 = (bf16[4,2,64,512]{3,2,1,0:T(8,128)(2,1)}, bf16[4,2,64,512]{3,2,1,0:T(8,128)(2,1)S(1)}, u32[]{:S(2)}) copy-start(bf16[4,2,64,512]{3,2,1,0:T(8,128)(2,1)S(1)} %collective-permute-done.18.refs_11_) | copy-start | bytes 1572868
  164.2 11.3 %copy-start.19 = (bf16[4,2,64,512]{3,2,1,0:T(8,128)(2,1)}, bf16[4,2,64,512]{3,2,1,0:T(8,128)(2,1)S(1)}, u32[]{:S(2)}) copy-start(bf16[4,2,64,512]{3,2,1,0:T(8,128)(2,1)S(1)} %collective-permute-done.17.refs_10_) | copy-start | bytes 1572868
  173.7 1.8 copy-start.8
  175.5 0.9 copy-start.9
  186.2 4.9 %collective-permute-start.20 = (f32[2048,256]{1,0:T(8,128)}, f32[2048,256]{1,0:T(8,128)S(1)}, u32[]{:S(2)}, u32[]{:S(2)}) collective-permute-start(f32[2048,256]{1,0:T(8,128)} %get-tuple-element.52), channel_id=1, source_target_pairs={{0,32},{32,0},{64,96},{96,64},{128,160},{160,128},{192,224},{224,1... | collective-permute-start | bytes 6291464 | tf_op jit(solution)/shard_map/ppermute | solution.py:302
  191.1 1.4 copy-start.3
  195.7 0.9 copy-start.15
  195.7 1.0 copy-start.16

commit v3 on v2

--- a/solution.py
+++ b/solution.py
@@ -9,9 +9,11 @@
 from jax.sharding import PartitionSpec as P
 
 BLOCK = 256
-VMEM_LIMIT = 56 * 1024 * 1024
+VMEM_LIMIT = 24 * 1024 * 1024
+WIDE_LIMIT = 56 * 1024 * 1024
 SMEM_SPEC = pl.BlockSpec(memory_space=pltpu.SMEM)
 COST = pl.CostEstimate(flops=1, bytes_accessed=1, transcendentals=0)
+LONG = pl.CostEstimate(flops=100000000000, bytes_accessed=1000000000, transcendentals=0)
 BF16, F32 = jnp.bfloat16, jnp.float32
 
 
@@ -26,9 +28,9 @@
     return lax.ppermute(value, "col", pairs)
 
 
-def params(steps=1):
+def params(steps=1, limit=VMEM_LIMIT):
     return pltpu.CompilerParams(
-        vmem_limit_bytes=VMEM_LIMIT, dimension_semantics=("arbitrary",) * steps
+        vmem_limit_bytes=limit, dimension_semantics=("arbitrary",) * steps
     )
 
 
@@ -91,49 +93,55 @@
         cost_estimate=COST,
         compiler_params=params(),
         name="up",
-    )(pos, mask, *parts, weight)
-
-
-def act_kernel(n_row, *refs):
+    )(pos, mask, *parts, pltpu.with_memory_space_constraint(weight, pltpu.HBM))
+
+
+def act_kernel(n_row, n_z, pos_ref, *refs):
     own_ref, recv = refs[0], refs[1:n_row]
-    both_ref = refs[n_row]
+    all_ref, pieces = refs[n_row], refs[n_row + 1 :]
     pre = own_ref[0]
     grad_hidden = own_ref[1]
     for ref in recv:
         pre = pre + ref[0].astype(F32)
         grad_hidden = grad_hidden + ref[1].astype(F32)
     sig = jax.nn.sigmoid(pre)
-    both_ref[0] = (pre * sig).astype(BF16)
-    both_ref[1] = (grad_hidden * sig * (1.0 + pre * (1.0 - sig))).astype(BF16)
-
-
-def act(own, recv):
+    all_ref[0, 0] = (pre * sig).astype(BF16)
+    all_ref[0, 1] = (grad_hidden * sig * (1.0 + pre * (1.0 - sig))).astype(BF16)
+    for r in range(1, n_row):
+        all_ref[r] = all_ref[0]
+    width = all_ref.shape[3] // n_z
+    for k in range(n_z):
+        first = pl.multiple_of(lax.rem(pos_ref[1] + k, n_z) * width, width)
+        pieces[k][...] = all_ref[0, :, :, pl.ds(first, width)]
+
+
+def act(pos, own, recv, n_z):
     _, share, cols = own.shape
-    return pl.pallas_call(
-        functools.partial(act_kernel, len(recv) + 1),
-        in_specs=[pl.BlockSpec(memory_space=pltpu.VMEM)] * (len(recv) + 1),
-        out_specs=pl.BlockSpec(memory_space=pltpu.VMEM),
-        out_shape=jax.ShapeDtypeStruct((2, share, cols), BF16),
+    n_row = len(recv) + 1
+    return pl.pallas_call(
+        functools.partial(act_kernel, n_row, n_z),
+        in_specs=[SMEM_SPEC] + [pl.BlockSpec(memory_space=pltpu.VMEM)] * n_row,
+        out_specs=[pl.BlockSpec(memory_space=pltpu.VMEM)] * (n_z + 1),
+        out_shape=[jax.ShapeDtypeStruct((n_row, 2, share, cols), BF16)]
+        + [jax.ShapeDtypeStruct((2, share, cols // n_z), BF16)] * n_z,
         cost_estimate=COST,
         compiler_params=params(0),
         name="act",
-    )(own, *recv)
+    )(pos, own, *recv)
 
 
 def down_kernel(n_col, n_row, pos_ref, mask_ref, *refs):
-    parts, w_ref, send_ref = refs[:n_row], refs[n_row], refs[n_row + 1]
+    parts_ref, w_ref, send_ref = refs[:3]
     x_ref, wm_ref, acc_ref = refs[-3:]
-    share = parts[0].shape[1]
+    share = parts_ref.shape[2]
     tok = share * n_row
     step = pl.program_id(0)
 
     @pl.when(step == 0)
     def _():
         for t in range(2):
-            for k in range(n_row):
-                owner = lax.rem(pos_ref[0] + n_row - k, n_row)
-                first = pl.multiple_of(t * tok + owner * share, share)
-                x_ref[pl.ds(first, share), :] = parts[k][t]
+            for r in range(n_row):
+                x_ref[pl.ds(t * tok + r * share, share), :] = parts_ref[r, t]
 
     masked_copy(mask_ref, w_ref, wm_ref, step * (w_ref.shape[0] // BLOCK), 0)
     acc_ref[...] = lax.dot_general(
@@ -151,7 +159,7 @@
 
 
 def down(pos, mask, parts, weight, n_col, width=512):
-    n_row, (_, share, depth) = len(parts), parts[0].shape
+    n_row, _, share, depth = parts.shape
     feats = weight.shape[0]
     tok = share * n_row
     rows = tok // n_col
@@ -159,7 +167,7 @@
         functools.partial(down_kernel, n_col, n_row),
         grid=(feats // width,),
         in_specs=[SMEM_SPEC, SMEM_SPEC]
-        + [pl.BlockSpec((2, share, depth), lambda n: (0, 0, 0))] * n_row
+        + [pl.BlockSpec((n_row, 2, share, depth), lambda n: (0, 0, 0, 0))]
         + [pl.BlockSpec((width, depth), lambda n: (n, 0))],
         out_specs=pl.BlockSpec((n_col, 2, rows, width), lambda n: (0, 0, 0, n)),
         out_shape=jax.ShapeDtypeStruct((n_col, 2, rows, feats), BF16),
@@ -168,10 +176,10 @@
             pltpu.VMEM((width, depth), BF16),
             pltpu.VMEM((2 * tok, width), F32),
         ],
-        cost_estimate=COST,
-        compiler_params=params(),
+        cost_estimate=LONG,
+        compiler_params=params(limit=WIDE_LIMIT),
         name="down",
-    )(pos, mask, *parts, weight)
+    )(pos, mask, parts, pltpu.with_memory_space_constraint(weight, pltpu.HBM))
 
 
 def grad_kernel(n_col, n_row, n_z, pos_ref, *refs):
@@ -187,8 +195,7 @@
         for k in range(n_row):
             owner = lax.rem(pos_ref[0] + n_row - k, n_row)
             for z in range(n_z):
-                behind = lax.rem(pos_ref[1] + n_z - z, n_z)
-                first = pl.multiple_of(behind * tok + owner * share, share)
+                first = pl.multiple_of(z * tok + owner * share, share)
                 for t in range(2):
                     h_ref[t, pl.ds(first, share), :] = hidden[k][z, t]
 
@@ -232,8 +239,8 @@
             pltpu.VMEM((2, tok, cols), BF16),
             pltpu.VMEM((width, cols), F32),
         ],
-        cost_estimate=COST,
-        compiler_params=params(),
+        cost_estimate=LONG,
+        compiler_params=params(limit=WIDE_LIMIT),
         name="grad",
     )(pos, *near, *far, *hidden)
 
@@ -274,26 +281,28 @@
     ).astype(jnp.int32)
     both = jnp.stack([tokens, cotangent])
 
-    pair = jnp.stack([both, shift_col(both, 0, 1)])
+    both, swapped = lax.optimization_barrier((both, shift_col(both, 0, 1)))
+    pair = jnp.stack([both, swapped])
     near = [pair] + [shift_col(pair, j) for j in range(1, n_x)]
-    far = [shift(pair, "dp", 2 * k) for k in range(1, n_z)]
+    far = [shift(both, "dp", 2 * k) for k in range(1, n_z)]
 
     own, *sends = up(pos, block_mask, near, weight, n_row)
+    own, sends, far = lax.optimization_barrier((own, sends, far))
+    far = jnp.stack(far)
+    far_swap = shift_col(far, 0, 1)
     recv = [shift(s, "row", k + 1) for k, s in enumerate(sends)]
-    own, recv, far = lax.optimization_barrier((own, recv, far))
-    far = jnp.stack(far, axis=1)
+    far = jnp.stack([far, far_swap])
+    own, far = lax.optimization_barrier((own, far))
     left, right = shift_col(far, 1), shift_col(far, -1)
-    z_groups = [list(range(c, n_dp, 2)) for c in range(2)]
-    acts = act(own, recv)
-    acts_all = [acts] + [shift(acts, "row", k) for k in range(1, n_row)]
-    pieces = acts.reshape(2, acts.shape[1], n_z, -1).transpose(2, 0, 1, 3)
-    pieces = lax.all_to_all(pieces, "dp", 0, 0, axis_index_groups=z_groups)
-    acts_all, pieces, left, right = lax.optimization_barrier((acts_all, pieces, left, right))
-    pieces_all = [pieces] + [shift(pieces, "row", k) for k in range(1, n_row)]
+    acts, *pieces = act(pos, own, recv, n_z)
+    acts = lax.all_to_all(acts, "row", 0, 0)
+    pieces = jnp.stack([pieces[0]] + [shift(pieces[k], "dp", 2 * k) for k in range(1, n_z)])
+    pieces, left, right = lax.optimization_barrier((pieces, left, right))
     across = [shift_col(left[:1], 1), shift_col(right[1:], -1)]
     far = [far, left, across[0], right, across[1]]
-
-    sends = down(pos, block_mask, acts_all, weight, n_col)
+    pieces_all = [pieces] + [shift(pieces, "row", k) for k in range(1, n_row)]
+
+    sends = down(pos, block_mask, acts, weight, n_col)
     sends, near = lax.optimization_barrier((sends, near))
     total = lax.all_to_all(sends, "col", 0, 0).astype(F32).sum(axis=0) + both.astype(F32)
     output, input_grad = total[0].astype(BF16), total[1].astype(BF16)

time: 198 us -> 167 us (0.84)
  waiting for transfers between devices: 108 us -> 62.2 us
  starting transfers between devices: 43 us -> 60 us
  Pallas kernels: 34.3 us -> 31.3 us
    ppermute x12, waiting for transfers between devices: 71.5 us -> 23.2 us  [shift(): lax.ppermute(value, axis, [(i, (i + by) % size) for i in range(size)])]
    ppermute x1, starting transfers between devices: 0.88 us -> 13 us  [on_device(): theirs = lax.ppermute(given, 'dp', [(i, i ^ 1) for i in range(n_dp)])]
    ppermute x12, starting transfers between devices: 18.9 us -> 27.4 us  [shift(): lax.ppermute(value, axis, [(i, (i + by) % size) for i in range(size)])]
    all_to_all x1, starting transfers between devices: 8.24 us -> 4.59 us  [on_device(): acts = lax.all_to_all(acts, 'row', 0, 0)]
    ppermute x8 -> x9, waiting for transfers between devices: 32.1 us -> 35 us  [shift_col(): return lax.ppermute(value, 'col', pairs)]
    unnamed x40 -> x26, local copies, waits for them, and re-layouts: 4.5 us -> 4.22 us
    ppermute x8 -> x9, starting transfers between devices: 11.4 us -> 11.4 us  [shift_col(): return lax.ppermute(value, 'col', pairs)]
  transfers between devices with their start and end apart: 23 -> 24, of which waited for: 15 -> 11; matrix products, arithmetic and copies ran while one was open for 3% -> 3% of each run, Pallas kernels for 13% -> 19%
where the time goes in v3:
time: 167 us; the launch traced here: 166 us
  waiting for transfers between devices  62.2 us (37%)
  starting transfers between devices  60 us (36%)
  Pallas kernels  31.3 us (19%)
  local copies, waits for them, and re-layouts  8.31 us (5%)
  other arithmetic  2.94 us (2%)
    ppermute x9, waiting for transfers between devices, shift_col(): return lax.ppermute(value, 'col', pairs)  35 us
    ppermute x12, starting transfers between devices, shift(): lax.ppermute(value, axis, [(i, (i + by) % size) for i in range(size)])  27.4 us
    ppermute x12, waiting for transfers between devices, shift(): lax.ppermute(value, axis, [(i, (i + by) % size) for i in range(size)])  23.2 us
    ppermute x1, starting transfers between devices, on_device(): theirs = lax.ppermute(given, 'dp', [(i, i ^ 1) for i in range(n_dp)])  13 us
    ppermute x9, starting transfers between devices, shift_col(): return lax.ppermute(value, 'col', pairs)  11.4 us
    pallas_call x1, Pallas kernels, grad(): pl.pallas_call(functools.partial(grad_kernel, n_col, n_row, n_z), grid=(f...  9.78 us
    pallas_call x1, Pallas kernels, down(): pl.pallas_call(functools.partial(down_kernel, n_col, n_row), grid=(feats...  9.03 us
    pallas_call x1, Pallas kernels, up(): pl.pallas_call(functools.partial(up_kernel, n_col, n_row), grid=(cols //...  7.87 us
  transfers between devices with their start and end apart: 24, of which 11 were waited for; matrix products, arithmetic and copies ran while one was open for 3% of the time, Pallas kernels for 19%

profile of v3, /device:TPU:1, one launch (start us, length us, event | category | flops | bytes accessed | tf_op | source)
XLA Modules:
  0.0 165.6 jit_solution(8180485189780997775)
XLA Ops:
  0.6 1.0 pad_maximum_fusion.4
  1.6 2.6 %collective-permute-start = (bf16[2,32,2048]{2,1,0:T(8,128)(2,1)S(1)}, bf16[2,32,2048]{2,1,0:T(8,128)(2,1)S(1)}, u32[]{:S(2)}, u32[]{:S(2)}) collective-permute-start(bf16[2,32,2048]{2,1,0:T(8,128)(2,1)S(1)} %pad_maximum_fusion.4), channel_id=1, source_target_pairs={{0,4},{1,5},{2,6},{3,7},{4,0},{5,1},{6,2},{7,3},{8,12},{9,13},{10,... | collective-permute-start | bytes 786440 | tf_op jit(solution)/shard_map/ppermute | solution.py:28
  4.2 5.0 %collective-permute-done = bf16[2,32,2048]{2,1,0:T(8,128)(2,1)S(1)} collective-permute-done((bf16[2,32,2048]{2,1,0:T(8,128)(2,1)S(1)}, bf16[2,32,2048]{2,1,0:T(8,128)(2,1)S(1)}, u32[]{:S(2)}, u32[]{:S(2)}) %collective-permute-start) | collective-permute-done | bytes 262176 | tf_op jit(solution)/shard_map/ppermute | solution.py:28
  9.2 3.5 %collective-permute-start.3 = (bf16[2,2,32,2048]{3,2,1,0:T(8,128)(2,1)S(1)}, bf16[2,2,32,2048]{3,2,1,0:T(8,128)(2,1)S(1)}, u32[]{:S(2)}, u32[]{:S(2)}) collective-permute-start(bf16[2,2,32,2048]{3,2,1,0:T(8,128)(2,1)S(1)} %pad_maximum_fusion.2.refs_0_), channel_id=1, source_target_pairs={{0,3},{1,0},{2,1},{3,2},{4,7},{5,4},{6,5},{7,6},{8,11},{9,8},{10,9... | collective-permute-start | bytes 1572872 | tf_op jit(solution)/shard_map/ppermute | solution.py:28
  12.7 0.5 collective-permute-start.2
  13.2 0.6 collective-permute-start.1
  13.8 5.6 %collective-permute-start.6 = (bf16[2,32,2048]{2,1,0:T(8,128)(2,1)S(1)}, bf16[2,32,2048]{2,1,0:T(8,128)(2,1)S(1)}, u32[]{:S(2)}, u32[]{:S(2)}) collective-permute-start(bf16[2,32,2048]{2,1,0:T(8,128)(2,1)S(1)} %pad_maximum_fusion.4), channel_id=1, source_target_pairs={{0,192},{32,224},{64,0},{96,32},{128,64},{160,96},{192,128},{224,1... | collective-permute-start | bytes 786440 | tf_op jit(solution)/shard_map/ppermute | solution.py:22
  19.5 0.9 collective-permute-start.5
  20.4 3.5 %collective-permute-done.3.refs_3_ = bf16[2,2,32,2048]{3,2,1,0:T(8,128)(2,1)S(1)} collective-permute-done((bf16[2,2,32,2048]{3,2,1,0:T(8,128)(2,1)S(1)}, bf16[2,2,32,2048]{3,2,1,0:T(8,128)(2,1)S(1)}, u32[]{:S(2)}, u32[]{:S(2)}) %collective-permute-start.3) | collective-permute-done | bytes 524320 | tf_op jit(solution)/shard_map/ppermute | solution.py:28
  23.9 2.5 %collective-permute-start.4 = (bf16[2,32,2048]{2,1,0:T(8,128)(2,1)S(1)}, bf16[2,32,2048]{2,1,0:T(8,128)(2,1)S(1)}, u32[]{:S(2)}, u32[]{:S(2)}) collective-permute-start(bf16[2,32,2048]{2,1,0:T(8,128)(2,1)S(1)} %pad_maximum_fusion.4), channel_id=1, source_target_pairs={{0,64},{32,96},{64,128},{96,160},{128,192},{160,224},{192,0},{224,... | collective-permute-start | bytes 786440 | tf_op jit(solution)/shard_map/ppermute | solution.py:22
  26.5 12.8 %collective-permute-done.1.refs_1_ = bf16[2,2,32,2048]{3,2,1,0:T(8,128)(2,1)S(1)} collective-permute-done((bf16[2,2,32,2048]{3,2,1,0:T(8,128)(2,1)S(1)}, bf16[2,2,32,2048]{3,2,1,0:T(8,128)(2,1)S(1)}, u32[]{:S(2)}, u32[]{:S(2)}) %collective-permute-start.1) | collective-permute-done | bytes 524320 | tf_op jit(solution)/shard_map/ppermute | solution.py:28
  39.3 0.7 copy-done.5
  40.0 7.9 %up.1 = (f32[2,64,2048]{2,1,0:T(8,128)S(1)}, bf16[2,64,2048]{2,1,0:T(8,128)(2,1)S(1)}, bf16[2,64,2048]{2,1,0:T(8,128)(2,1)S(1)}, bf16[2,64,2048]{2,1,0:T(8,128)(2,1)S(1)}) custom-call(s32[6]{0:T(128)S(1)} %stack.81.pos_ref, s32[8,8]{1,0:T(8,128)S(1)} %copy-done.5, bf16[2,2,32,2048]{3,2,1,0:T(8,128)(2,1)S(1)} %pad_maximum_fusion.2.refs_0_, ...), custom_call_target="tpu_custom_call" | custom-call | flops 1 | bytes 1 | tf_op jit(solution)/shard_map/up/pallas_call | solution.py:79
  48.1 1.3 collective-permute-start.7
  49.4 1.3 collective-permute-start.8
  50.7 2.6 %collective-permute-start.9 = (bf16[2,64,2048]{2,1,0:T(8,128)(2,1)S(1)}, bf16[2,64,2048]{2,1,0:T(8,128)(2,1)S(1)}, u32[]{:S(2)}, u32[]{:S(2)}) collective-permute-start(bf16[2,64,2048]{2,1,0:T(8,128)(2,1)S(1)} %get-tuple-element.45), channel_id=1, source_target_pairs={{0,16},{8,24},{16,0},{24,8},{1,17},{9,25},{17,1},{25,9},{2,18},{10... | collective-permute-start | bytes 1572872 | tf_op jit(solution)/shard_map/ppermute | solution.py:22
  53.4 1.1 collective-permute-start.10
  54.4 12.4 %collective-permute-done.7 = bf16[3,2,32,2048]{3,2,1,0:T(8,128)(2,1)S(1)} collective-permute-done((bf16[3,2,32,2048]{3,2,1,0:T(8,128)(2,1)S(1)}, bf16[3,2,32,2048]{3,2,1,0:T(8,128)(2,1)S(1)}, u32[]{:S(2)}, u32[]{:S(2)}) %collective-permute-start.7) | collective-permute-done | bytes 786464 | tf_op jit(solution)/shard_map/ppermute | solution.py:28
  66.8 1.3 pad_maximum_fusion.refs_4_
  68.1 1.5 collective-permute-start.14
  69.6 6.0 %collective-permute-done.9.refs_2_ = bf16[2,64,2048]{2,1,0:T(8,128)(2,1)S(1)} collective-permute-done((bf16[2,64,2048]{2,1,0:T(8,128)(2,1)S(1)}, bf16[2,64,2048]{2,1,0:T(8,128)(2,1)S(1)}, u32[]{:S(2)}, u32[]{:S(2)}) %collective-permute-start.9) | collective-permute-done | bytes 524320 | tf_op jit(solution)/shard_map/ppermute | solution.py:22
  75.5 2.6 %act.1 = (bf16[4,2,64,2048]{3,2,1,0:T(8,128)(2,1)}, bf16[2,64,512]{2,1,0:T(8,128)(2,1)S(1)}, bf16[2,64,512]{2,1,0:T(8,128)(2,1)S(1)}, bf16[2,64,512]{2,1,0:T(8,128)(2,1)S(1)}, bf16[2,64,512]{2,1,0:T(8,128)(2,1)S(1)}) custom-call(s32[6]{0:T(128)S(1)} %stack.81.pos_ref, f32[2,64,2048]{2,1,0:T(8,128)S(1)} %get-tuple-element.43.refs_0_, ...), custom_call_target="tpu_custom_call" | custom-call | flops 1 | bytes 1 | tf_op jit(solution)/shard_map/act/pallas_call | solution.py:121
  78.1 4.6 %all-to-all-start = ((bf16[4,2,64,2048]{3,2,1,0:T(8,128)(2,1)}), bf16[4,2,64,2048]{3,2,1,0:T(8,128)(2,1)S(1)}, u32[]{:S(2)}, u32[]{:S(2)}) async-start(bf16[4,2,64,2048]{3,2,1,0:T(8,128)(2,1)} %get-tuple-element.47), calls=%async_computation | async-start | bytes 4194304 | tf_op jit(solution)/shard_map/all_to_all | solution.py:298
  82.7 3.0 %collective-permute-start.11 = (bf16[2,64,512]{2,1,0:T(8,128)(2,1)S(1)}, bf16[2,64,512]{2,1,0:T(8,128)(2,1)S(1)}, u32[]{:S(2)}, u32[]{:S(2)}) collective-permute-start(bf16[2,64,512]{2,1,0:T(8,128)(2,1)S(1)} %get-tuple-element.55), channel_id=1, source_target_pairs={{0,64},{32,96},{64,128},{96,160},{128,192},{160,224},{192,0},{224,... | collective-permute-start | bytes 393224 | tf_op jit(solution)/shard_map/ppermute | solution.py:22
  85.7 4.2 %collective-permute-start.12 = (bf16[2,64,512]{2,1,0:T(8,128)(2,1)S(1)}, bf16[2,64,512]{2,1,0:T(8,128)(2,1)S(1)}, u32[]{:S(2)}, u32[]{:S(2)}) collective-permute-start(bf16[2,64,512]{2,1,0:T(8,128)(2,1)S(1)} %get-tuple-element.56), channel_id=1, source_target_pairs={{0,128},{32,160},{64,192},{96,224},{128,0},{160,32},{192,64},{224,... | collective-permute-start | bytes 393224 | tf_op jit(solution)/shard_map/ppermute | solution.py:22
  89.9 2.4 %collective-permute-start.13 = (bf16[2,64,512]{2,1,0:T(8,128)(2,1)S(1)}, bf16[2,64,512]{2,1,0:T(8,128)(2,1)S(1)}, u32[]{:S(2)}, u32[]{:S(2)}) collective-permute-start(bf16[2,64,512]{2,1,0:T(8,128)(2,1)S(1)} %get-tuple-element.57), channel_id=1, source_target_pairs={{0,192},{32,224},{64,0},{96,32},{128,64},{160,96},{192,128},{224,1... | collective-permute-start | bytes 393224 | tf_op jit(solution)/shard_map/ppermute | solution.py:22
  92.3 4.6 %collective-permute-done.12 = bf16[2,64,512]{2,1,0:T(8,128)(2,1)S(1)} collective-permute-done((bf16[2,64,512]{2,1,0:T(8,128)(2,1)S(1)}, bf16[2,64,512]{2,1,0:T(8,128)(2,1)S(1)}, u32[]{:S(2)}, u32[]{:S(2)}) %collective-permute-start.12) | collective-permute-done | bytes 131104 | tf_op jit(solution)/shard_map/ppermute | solution.py:22
  96.9 5.7 %collective-permute-done.13 = bf16[2,64,512]{2,1,0:T(8,128)(2,1)S(1)} collective-permute-done((bf16[2,64,512]{2,1,0:T(8,128)(2,1)S(1)}, bf16[2,64,512]{2,1,0:T(8,128)(2,1)S(1)}, u32[]{:S(2)}, u32[]{:S(2)}) %collective-permute-start.13) | collective-permute-done | bytes 131104 | tf_op jit(solution)/shard_map/ppermute | solution.py:22
  103.0 1.1 collective-permute-done.14.refs_5_
  104.0 2.7 %collective-permute-start.20 = (bf16[4,2,64,512]{3,2,1,0:T(8,128)(2,1)S(1)}, bf16[4,2,64,512]{3,2,1,0:T(8,128)(2,1)}, u32[]{:S(2)}, u32[]{:S(2)}) collective-permute-start(bf16[4,2,64,512]{3,2,1,0:T(8,128)(2,1)S(1)} %pad_maximum_fusion.3.refs_9_), channel_id=1, source_target_pairs={{0,24},{8,0},{16,8},{24,16},{1,25},{9,1},{17,9},{25,17},{2,26},{10... | collective-permute-start | bytes 1572872 | tf_op jit(solution)/shard_map/ppermute | solution.py:22
  106.8 0.3 collective-permute-start.19
  107.1 0.7 collective-permute-start.18
  107.8 1.2 slice.16
  109.0 2.1 %slice.17 = bf16[1,3,2,32,2048]{4,3,2,1,0:T(8,128)(2,1)} slice(bf16[2,3,2,32,2048]{4,3,2,1,0:T(8,128)(2,1)} %collective-permute-done.15.refs_7_), slice={[1:2], [0:3], [0:2], [0:32], [0:2048]} | slice | bytes 1572864 | tf_op jit(solution)/shard_map/slice | solution.py:301
  111.1 0.3 collective-permute-start.17
  111.4 1.2 collective-permute-start.16
  112.6 1.3 copy-done.11
  113.9 9.0 %down.1 = bf16[8,2,32,2048]{3,2,1,0:T(8,128)(2,1)} custom-call(s32[6]{0:T(128)} %copy-done.7, s32[8,8]{1,0:T(8,128)} %mask_ref.5, bf16[4,2,64,2048]{3,2,1,0:T(8,128)(2,1)} %copy-done.11, bf16[2048,2048]{1,0:T(8,128)(2,1)} %refs_1_.1), custom_call_target="tpu_custom_call" | custom-call | flops 99999997952 | bytes 1000000000 | tf_op jit(solution)/shard_map/down/pallas_call | solution.py:166
  122.9 3.6 %all-to-all-start.1 = ((bf16[8,2,32,2048]{3,2,1,0:T(8,128)(2,1)}), bf16[8,2,32,2048]{3,2,1,0:T(8,128)(2,1)S(1)}, u32[]{:S(2)}, u32[]{:S(2)}) async-start(bf16[8,2,32,2048]{3,2,1,0:T(8,128)(2,1)} %down.1), calls=%async_computation.1 | async-start | bytes 4194304 | tf_op jit(solution)/shard_map/all_to_all | solution.py:307
  126.6 6.9 %collective-permute-done.18.refs_10_ = bf16[4,2,64,512]{3,2,1,0:T(8,128)(2,1)} collective-permute-done((bf16[4,2,64,512]{3,2,1,0:T(8,128)(2,1)S(1)}, bf16[4,2,64,512]{3,2,1,0:T(8,128)(2,1)}, u32[]{:S(2)}, u32[]{:S(2)}) %collective-permute-start.18) | collective-permute-done | bytes 524320 | tf_op jit(solution)/shard_map/ppermute | solution.py:22
  133.5 9.8 %grad.1 = (f32[2048,256]{1,0:T(8,128)}, f32[2048,256]{1,0:T(8,128)}) custom-call(s32[6]{0:T(128)} %copy-done.7, bf16[2,2,32,2048]{3,2,1,0:T(8,128)(2,1)} %copy-done, bf16[2,2,32,2048]{3,2,1,0:T(8,128)(2,1)} %copy-done.4, bf16[2,2,32,2048]{3,2,1,0:T(8,128)(2,1)} %copy-done.3, bf16[2,2,32,2048]{3,2,1,0:T(8,128)(2,1)} %copy-done.2, ...), custom_call_target="tpu_custom_call" | custom-call | flops 99999997952 | bytes 1000000000 | tf_op jit(solution)/shard_map/grad/pallas_call | solution.py:225
  143.2 13.0 %collective-permute-start.21 = (f32[2048,256]{1,0:T(8,128)}, f32[2048,256]{1,0:T(8,128)S(1)}, u32[]{:S(2)}, u32[]{:S(2)}) collective-permute-start(f32[2048,256]{1,0:T(8,128)} %get-tuple-element.62), channel_id=1, source_target_pairs={{0,32},{32,0},{64,96},{96,64},{128,160},{160,128},{192,224},{224,1... | collective-permute-start | bytes 6291464 | tf_op jit(solution)/shard_map/ppermute | solution.py:311
  156.2 4.0 %collective-permute-done.21.b_ref = f32[2048,256]{1,0:T(8,128)S(1)} collective-permute-done((f32[2048,256]{1,0:T(8,128)}, f32[2048,256]{1,0:T(8,128)S(1)}, u32[]{:S(2)}, u32[]{:S(2)}) %collective-permute-start.21) | collective-permute-done | bytes 2097184 | tf_op jit(solution)/shard_map/ppermute | solution.py:311
  160.2 1.6 copy-done.1
  161.8 2.1 %finish.1 = f32[4096,128]{1,0:T(8,128)} custom-call(s32[6]{0:T(128)S(1)} %copy-done.8, s32[8,8]{1,0:T(8,128)S(1)} %copy-done.6, f32[2048,256]{1,0:T(8,128)S(1)} %copy-done.1, f32[2048,256]{1,0:T(8,128)S(1)} %collective-permute-done.21.b_ref), custom_call_target="tpu_custom_call" | custom-call | flops 1 | bytes 1 | tf_op jit(solution)/shard_map/finish/pallas_call | solution.py:262
  163.9 0.4 convert_reduce_fusion
  164.3 0.6 copy-done.10
  164.9 0.7 slice_bitcast_fusion
  (42 shorter events, 0.7 us)
Async XLA Ops:
  1.6 46.2 %copy-start.9 = (bf16[2,32,2048]{2,1,0:T(8,128)(2,1)}, bf16[2,32,2048]{2,1,0:T(8,128)(2,1)S(1)}, u32[]{:S(2)}) copy-start(bf16[2,32,2048]{2,1,0:T(8,128)(2,1)S(1)} %pad_maximum_fusion.4) | copy-start | bytes 786436
  1.6 7.5 %collective-permute-start = (bf16[2,32,2048]{2,1,0:T(8,128)(2,1)S(1)}, bf16[2,32,2048]{2,1,0:T(8,128)(2,1)S(1)}, u32[]{:S(2)}, u32[]{:S(2)}) collective-permute-start(bf16[2,32,2048]{2,1,0:T(8,128)(2,1)S(1)} %pad_maximum_fusion.4), channel_id=1, source_target_pairs={{0,4},{1,5},{2,6},{3,7},{4,0},{5,1},{6,2},{7,3},{8,12},{9,13},{10,... | collective-permute-start | bytes 786440 | tf_op jit(solution)/shard_map/ppermute | solution.py:28
  9.2 38.7 %copy-start = (bf16[2,2,32,2048]{3,2,1,0:T(8,128)(2,1)}, bf16[2,2,32,2048]{3,2,1,0:T(8,128)(2,1)S(1)}, u32[]{:S(2)}) copy-start(bf16[2,2,32,2048]{3,2,1,0:T(8,128)(2,1)S(1)} %pad_maximum_fusion.2.refs_0_) | copy-start | bytes 1572868
  9.2 14.7 %collective-permute-start.3 = (bf16[2,2,32,2048]{3,2,1,0:T(8,128)(2,1)S(1)}, bf16[2,2,32,2048]{3,2,1,0:T(8,128)(2,1)S(1)}, u32[]{:S(2)}, u32[]{:S(2)}) collective-permute-start(bf16[2,2,32,2048]{3,2,1,0:T(8,128)(2,1)S(1)} %pad_maximum_fusion.2.refs_0_), channel_id=1, source_target_pairs={{0,3},{1,0},{2,1},{3,2},{4,7},{5,4},{6,5},{7,6},{8,11},{9,8},{10,9... | collective-permute-start | bytes 1572872 | tf_op jit(solution)/shard_map/ppermute | solution.py:28
  12.7 13.7 %collective-permute-start.2 = (bf16[2,2,32,2048]{3,2,1,0:T(8,128)(2,1)S(1)}, bf16[2,2,32,2048]{3,2,1,0:T(8,128)(2,1)S(1)}, u32[]{:S(2)}, u32[]{:S(2)}) collective-permute-start(bf16[2,2,32,2048]{3,2,1,0:T(8,128)(2,1)S(1)} %pad_maximum_fusion.2.refs_0_), channel_id=1, source_target_pairs={{0,2},{1,3},{2,0},{3,1},{4,6},{5,7},{6,4},{7,5},{8,10},{9,11},{10,... | collective-permute-start | bytes 1572872 | tf_op jit(solution)/shard_map/ppermute | solution.py:28
  13.2 26.1 %collective-permute-start.1 = (bf16[2,2,32,2048]{3,2,1,0:T(8,128)(2,1)S(1)}, bf16[2,2,32,2048]{3,2,1,0:T(8,128)(2,1)S(1)}, u32[]{:S(2)}, u32[]{:S(2)}) collective-permute-start(bf16[2,2,32,2048]{3,2,1,0:T(8,128)(2,1)S(1)} %pad_maximum_fusion.2.refs_0_), channel_id=1, source_target_pairs={{0,1},{1,2},{2,3},{3,0},{4,5},{5,6},{6,7},{7,4},{8,9},{9,10},{10,1... | collective-permute-start | bytes 1572872 | tf_op jit(solution)/shard_map/ppermute | solution.py:28
  13.8 34.1 %collective-permute-start.6 = (bf16[2,32,2048]{2,1,0:T(8,128)(2,1)S(1)}, bf16[2,32,2048]{2,1,0:T(8,128)(2,1)S(1)}, u32[]{:S(2)}, u32[]{:S(2)}) collective-permute-start(bf16[2,32,2048]{2,1,0:T(8,128)(2,1)S(1)} %pad_maximum_fusion.4), channel_id=1, source_target_pairs={{0,192},{32,224},{64,0},{96,32},{128,64},{160,96},{192,128},{224,1... | collective-permute-start | bytes 786440 | tf_op jit(solution)/shard_map/ppermute | solution.py:22
  19.5 28.4 %collective-permute-start.5 = (bf16[2,32,2048]{2,1,0:T(8,128)(2,1)S(1)}, bf16[2,32,2048]{2,1,0:T(8,128)(2,1)S(1)}, u32[]{:S(2)}, u32[]{:S(2)}) collective-permute-start(bf16[2,32,2048]{2,1,0:T(8,128)(2,1)S(1)} %pad_maximum_fusion.4), channel_id=1, source_target_pairs={{0,128},{32,160},{64,192},{96,224},{128,0},{160,32},{192,64},{224,... | collective-permute-start | bytes 786440 | tf_op jit(solution)/shard_map/ppermute | solution.py:22
  23.9 24.0 %copy-start.2 = (bf16[2,2,32,2048]{3,2,1,0:T(8,128)(2,1)}, bf16[2,2,32,2048]{3,2,1,0:T(8,128)(2,1)S(1)}, u32[]{:S(2)}) copy-start(bf16[2,2,32,2048]{3,2,1,0:T(8,128)(2,1)S(1)} %collective-permute-done.3.refs_3_) | copy-start | bytes 1572868
  23.9 24.1 %collective-permute-start.4 = (bf16[2,32,2048]{2,1,0:T(8,128)(2,1)S(1)}, bf16[2,32,2048]{2,1,0:T(8,128)(2,1)S(1)}, u32[]{:S(2)}, u32[]{:S(2)}) collective-permute-start(bf16[2,32,2048]{2,1,0:T(8,128)(2,1)S(1)} %pad_maximum_fusion.4), channel_id=1, source_target_pairs={{0,64},{32,96},{64,128},{96,160},{128,192},{160,224},{192,0},{224,... | collective-permute-start | bytes 786440 | tf_op jit(solution)/shard_map/ppermute | solution.py:22
  26.5 49.1 %copy-start.7 = (s32[6]{0:T(128)}, s32[6]{0:T(128)S(1)}, u32[]{:S(2)}) copy-start(s32[6]{0:T(128)S(1)} %stack.81.pos_ref) | copy-start | bytes 76
  26.5 21.4 %copy-start.3 = (bf16[2,2,32,2048]{3,2,1,0:T(8,128)(2,1)}, bf16[2,2,32,2048]{3,2,1,0:T(8,128)(2,1)S(1)}, u32[]{:S(2)}) copy-start(bf16[2,2,32,2048]{3,2,1,0:T(8,128)(2,1)S(1)} %collective-permute-done.2.refs_2_) | copy-start | bytes 1572868
  39.3 0.7 copy-start.5
  40.0 7.9 %copy-start.4 = (bf16[2,2,32,2048]{3,2,1,0:T(8,128)(2,1)}, bf16[2,2,32,2048]{3,2,1,0:T(8,128)(2,1)S(1)}, u32[]{:S(2)}) copy-start(bf16[2,2,32,2048]{3,2,1,0:T(8,128)(2,1)S(1)} %collective-permute-done.1.refs_1_) | copy-start | bytes 1572868
  48.1 18.7 %collective-permute-start.7 = (bf16[3,2,32,2048]{3,2,1,0:T(8,128)(2,1)S(1)}, bf16[3,2,32,2048]{3,2,1,0:T(8,128)(2,1)S(1)}, u32[]{:S(2)}, u32[]{:S(2)}) collective-permute-start(bf16[3,2,32,2048]{3,2,1,0:T(8,128)(2,1)S(1)} %get-tuple-element.67), channel_id=1, source_target_pairs={{0,4},{1,5},{2,6},{3,7},{4,0},{5,1},{6,2},{7,3},{8,12},{9,13},{10,... | collective-permute-start | bytes 2359304 | tf_op jit(solution)/shard_map/ppermute | solution.py:28
  49.4 20.1 %collective-permute-start.8 = (bf16[2,64,2048]{2,1,0:T(8,128)(2,1)S(1)}, bf16[2,64,2048]{2,1,0:T(8,128)(2,1)S(1)}, u32[]{:S(2)}, u32[]{:S(2)}) collective-permute-start(bf16[2,64,2048]{2,1,0:T(8,128)(2,1)S(1)} %get-tuple-element.44), channel_id=1, source_target_pairs={{0,8},{8,16},{16,24},{24,0},{1,9},{9,17},{17,25},{25,1},{2,10},{10... | collective-permute-start | bytes 1572872 | tf_op jit(solution)/shard_map/ppermute | solution.py:22
  50.7 24.8 %collective-permute-start.9 = (bf16[2,64,2048]{2,1,0:T(8,128)(2,1)S(1)}, bf16[2,64,2048]{2,1,0:T(8,128)(2,1)S(1)}, u32[]{:S(2)}, u32[]{:S(2)}) collective-permute-start(bf16[2,64,2048]{2,1,0:T(8,128)(2,1)S(1)} %get-tuple-element.45), channel_id=1, source_target_pairs={{0,16},{8,24},{16,0},{24,8},{1,17},{9,25},{17,1},{25,9},{2,18},{10... | collective-permute-start | bytes 1572872 | tf_op jit(solution)/shard_map/ppermute | solution.py:22
  53.4 22.2 %collective-permute-start.10 = (bf16[2,64,2048]{2,1,0:T(8,128)(2,1)S(1)}, bf16[2,64,2048]{2,1,0:T(8,128)(2,1)S(1)}, u32[]{:S(2)}, u32[]{:S(2)}) collective-permute-start(bf16[2,64,2048]{2,1,0:T(8,128)(2,1)S(1)} %get-tuple-element.46), channel_id=1, source_target_pairs={{0,24},{8,0},{16,8},{24,16},{1,25},{9,1},{17,9},{25,17},{2,26},{10... | collective-permute-start | bytes 1572872 | tf_op jit(solution)/shard_map/ppermute | solution.py:22
  68.1 34.9 %collective-permute-start.15 = (bf16[2,3,2,32,2048]{4,3,2,1,0:T(8,128)(2,1)}, bf16[2,3,2,32,2048]{4,3,2,1,0:T(8,128)(2,1)}, u32[]{:S(2)}, u32[]{:S(2)}) collective-permute-start(bf16[2,3,2,32,2048]{4,3,2,1,0:T(8,128)(2,1)} %pad_maximum_fusion.refs_4_), channel_id=1, source_target_pairs={{0,3},{1,0},{2,1},{3,2},{4,7},{5,4},{6,5},{7,6},{8,11},{9,8},{10,9... | collective-permute-start | bytes 4718600 | tf_op jit(solution)/shard_map/ppermute | solution.py:28
  68.1 35.9 %collective-permute-start.14 = (bf16[2,3,2,32,2048]{4,3,2,1,0:T(8,128)(2,1)}, bf16[2,3,2,32,2048]{4,3,2,1,0:T(8,128)(2,1)}, u32[]{:S(2)}, u32[]{:S(2)}) collective-permute-start(bf16[2,3,2,32,2048]{4,3,2,1,0:T(8,128)(2,1)} %pad_maximum_fusion.refs_4_), channel_id=1, source_target_pairs={{0,1},{1,2},{2,3},{3,0},{4,5},{5,6},{6,7},{7,4},{8,9},{9,10},{10,1... | collective-permute-start | bytes 4718600 | tf_op jit(solution)/shard_map/ppermute | solution.py:28
  78.1 34.4 %all-to-all-start = ((bf16[4,2,64,2048]{3,2,1,0:T(8,128)(2,1)}), bf16[4,2,64,2048]{3,2,1,0:T(8,128)(2,1)S(1)}, u32[]{:S(2)}, u32[]{:S(2)}) async-start(bf16[4,2,64,2048]{3,2,1,0:T(8,128)(2,1)} %get-tuple-element.47), calls=%async_computation | async-start | bytes 4194304 | tf_op jit(solution)/shard_map/all_to_all | solution.py:298
  82.7 9.6 %collective-permute-start.11 = (bf16[2,64,512]{2,1,0:T(8,128)(2,1)S(1)}, bf16[2,64,512]{2,1,0:T(8,128)(2,1)S(1)}, u32[]{:S(2)}, u32[]{:S(2)}) collective-permute-start(bf16[2,64,512]{2,1,0:T(8,128)(2,1)S(1)} %get-tuple-element.55), channel_id=1, source_target_pairs={{0,64},{32,96},{64,128},{96,160},{128,192},{160,224},{192,0},{224,... | collective-permute-start | bytes 393224 | tf_op jit(solution)/shard_map/ppermute | solution.py:22
  85.7 11.2 %collective-permute-start.12 = (bf16[2,64,512]{2,1,0:T(8,128)(2,1)S(1)}, bf16[2,64,512]{2,1,0:T(8,128)(2,1)S(1)}, u32[]{:S(2)}, u32[]{:S(2)}) collective-permute-start(bf16[2,64,512]{2,1,0:T(8,128)(2,1)S(1)} %get-tuple-element.56), channel_id=1, source_target_pairs={{0,128},{32,160},{64,192},{96,224},{128,0},{160,32},{192,64},{224,... | collective-permute-start | bytes 393224 | tf_op jit(solution)/shard_map/ppermute | solution.py:22
  89.9 12.7 %collective-permute-start.13 = (bf16[2,64,512]{2,1,0:T(8,128)(2,1)S(1)}, bf16[2,64,512]{2,1,0:T(8,128)(2,1)S(1)}, u32[]{:S(2)}, u32[]{:S(2)}) collective-permute-start(bf16[2,64,512]{2,1,0:T(8,128)(2,1)S(1)} %get-tuple-element.57), channel_id=1, source_target_pairs={{0,192},{32,224},{64,0},{96,32},{128,64},{160,96},{192,128},{224,1... | collective-permute-start | bytes 393224 | tf_op jit(solution)/shard_map/ppermute | solution.py:22
  102.7 20.2 %copy-start.12 = (bf16[4,2,64,512]{3,2,1,0:T(8,128)(2,1)}, bf16[4,2,64,512]{3,2,1,0:T(8,128)(2,1)S(1)}, u32[]{:S(2)}) copy-start(bf16[4,2,64,512]{3,2,1,0:T(8,128)(2,1)S(1)} %pad_maximum_fusion.3.refs_9_) | copy-start | bytes 1572868
  104.0 22.5 %collective-permute-start.20 = (bf16[4,2,64,512]{3,2,1,0:T(8,128)(2,1)S(1)}, bf16[4,2,64,512]{3,2,1,0:T(8,128)(2,1)}, u32[]{:S(2)}, u32[]{:S(2)}) collective-permute-start(bf16[4,2,64,512]{3,2,1,0:T(8,128)(2,1)S(1)} %pad_maximum_fusion.3.refs_9_), channel_id=1, source_target_pairs={{0,24},{8,0},{16,8},{24,16},{1,25},{9,1},{17,9},{25,17},{2,26},{10... | collective-permute-start | bytes 1572872 | tf_op jit(solution)/shard_map/ppermute | solution.py:22
  106.8 19.8 %collective-permute-start.19 = (bf16[4,2,64,512]{3,2,1,0:T(8,128)(2,1)S(1)}, bf16[4,2,64,512]{3,2,1,0:T(8,128)(2,1)}, u32[]{:S(2)}, u32[]{:S(2)}) collective-permute-start(bf16[4,2,64,512]{3,2,1,0:T(8,128)(2,1)S(1)} %pad_maximum_fusion.3.refs_9_), channel_id=1, source_target_pairs={{0,16},{8,24},{16,0},{24,8},{1,17},{9,25},{17,1},{25,9},{2,18},{10... | collective-permute-start | bytes 1572872 | tf_op jit(solution)/shard_map/ppermute | solution.py:22
  107.1 26.4 %collective-permute-start.18 = (bf16[4,2,64,512]{3,2,1,0:T(8,128)(2,1)S(1)}, bf16[4,2,64,512]{3,2,1,0:T(8,128)(2,1)}, u32[]{:S(2)}, u32[]{:S(2)}) collective-permute-start(bf16[4,2,64,512]{3,2,1,0:T(8,128)(2,1)S(1)} %pad_maximum_fusion.3.refs_9_), channel_id=1, source_target_pairs={{0,8},{8,16},{16,24},{24,0},{1,9},{9,17},{17,25},{25,1},{2,10},{10... | collective-permute-start | bytes 1572872 | tf_op jit(solution)/shard_map/ppermute | solution.py:22
  111.1 22.4 %collective-permute-start.17 = (bf16[1,3,2,32,2048]{4,3,2,1,0:T(8,128)(2,1)}, bf16[1,3,2,32,2048]{4,3,2,1,0:T(8,128)(2,1)}, u32[]{:S(2)}, u32[]{:S(2)}) collective-permute-start(bf16[1,3,2,32,2048]{4,3,2,1,0:T(8,128)(2,1)} %slice.17), channel_id=1, source_target_pairs={{0,3},{1,0},{2,1},{3,2},{4,7},{5,4},{6,5},{7,6},{8,11},{9,8},{10,9... | collective-permute-start | bytes 2359304 | tf_op jit(solution)/shard_map/ppermute | solution.py:28
  111.4 22.1 %collective-permute-start.16 = (bf16[1,3,2,32,2048]{4,3,2,1,0:T(8,128)(2,1)S(1)}, bf16[1,3,2,32,2048]{4,3,2,1,0:T(8,128)(2,1)}, u32[]{:S(2)}, u32[]{:S(2)}) collective-permute-start(bf16[1,3,2,32,2048]{4,3,2,1,0:T(8,128)(2,1)S(1)} %slice.16), channel_id=1, source_target_pairs={{0,1},{1,2},{2,3},{3,0},{4,5},{5,6},{6,7},{7,4},{8,9},{9,10},{10,1... | collective-permute-start | bytes 2359304 | tf_op jit(solution)/shard_map/ppermute | solution.py:28
  112.6 1.3 copy-start.11
  122.9 41.0 %all-to-all-start.1 = ((bf16[8,2,32,2048]{3,2,1,0:T(8,128)(2,1)}), bf16[8,2,32,2048]{3,2,1,0:T(8,128)(2,1)S(1)}, u32[]{:S(2)}, u32[]{:S(2)}) async-start(bf16[8,2,32,2048]{3,2,1,0:T(8,128)(2,1)} %down.1), calls=%async_computation.1 | async-start | bytes 4194304 | tf_op jit(solution)/shard_map/all_to_all | solution.py:307
  126.5 33.7 %copy-start.6 = (s32[8,8]{1,0:T(8,128)S(1)}, s32[8,8]{1,0:T(8,128)}, u32[]{:S(2)}) copy-start(s32[8,8]{1,0:T(8,128)} %mask_ref.5) | copy-start | bytes 772
  126.5 33.7 %copy-start.8 = (s32[6]{0:T(128)S(1)}, s32[6]{0:T(128)}, u32[]{:S(2)}) copy-start(s32[6]{0:T(128)} %copy-done.7) | copy-start | bytes 76
  143.2 17.0 %collective-permute-start.21 = (f32[2048,256]{1,0:T(8,128)}, f32[2048,256]{1,0:T(8,128)S(1)}, u32[]{:S(2)}, u32[]{:S(2)}) collective-permute-start(f32[2048,256]{1,0:T(8,128)} %get-tuple-element.62), channel_id=1, source_target_pairs={{0,32},{32,0},{64,96},{96,64},{128,160},{160,128},{192,224},{224,1... | collective-permute-start | bytes 6291464 | tf_op jit(solution)/shard_map/ppermute | solution.py:311
  160.2 1.6 copy-start.1
  163.9 0.9 copy-start.10

commit v4 on v3

--- a/solution.py
+++ b/solution.py
@@ -13,6 +13,7 @@
 WIDE_LIMIT = 56 * 1024 * 1024
 SMEM_SPEC = pl.BlockSpec(memory_space=pltpu.SMEM)
 COST = pl.CostEstimate(flops=1, bytes_accessed=1, transcendentals=0)
+MEDIUM = pl.CostEstimate(flops=3000000000, bytes_accessed=1, transcendentals=0)
 LONG = pl.CostEstimate(flops=100000000000, bytes_accessed=1000000000, transcendentals=0)
 BF16, F32 = jnp.bfloat16, jnp.float32
 
@@ -176,7 +177,7 @@
             pltpu.VMEM((width, depth), BF16),
             pltpu.VMEM((2 * tok, width), F32),
         ],
-        cost_estimate=LONG,
+        cost_estimate=MEDIUM,
         compiler_params=params(limit=WIDE_LIMIT),
         name="down",
     )(pos, mask, parts, pltpu.with_memory_space_constraint(weight, pltpu.HBM))
@@ -268,7 +269,27 @@
         cost_estimate=COST,
         compiler_params=params(),
         name="finish",
-    )(pos, mask, mine, theirs)
+    )(pos, mask, mine, pltpu.with_memory_space_constraint(theirs, pltpu.HBM))
+
+
+def add_kernel(sums_ref, tok_ref, cot_ref, *out_refs):
+    for t, (first, out_ref) in enumerate(zip((tok_ref, cot_ref), out_refs)):
+        total = first[...].astype(F32)
+        for c in range(sums_ref.shape[0]):
+            total = total + sums_ref[c, t].astype(F32)
+        out_ref[...] = total.astype(BF16)
+
+
+def add(sums, tokens, cotangent):
+    return pl.pallas_call(
+        add_kernel,
+        in_specs=[pl.BlockSpec(memory_space=pltpu.VMEM)] * 3,
+        out_specs=[pl.BlockSpec(memory_space=pltpu.VMEM)] * 2,
+        out_shape=[jax.ShapeDtypeStruct(tokens.shape, BF16)] * 2,
+        cost_estimate=COST,
+        compiler_params=params(0),
+        name="add",
+    )(sums, tokens, cotangent)
 
 
 def on_device(tokens, cotangent, weight, block_mask):
@@ -297,15 +318,15 @@
     acts, *pieces = act(pos, own, recv, n_z)
     acts = lax.all_to_all(acts, "row", 0, 0)
     pieces = jnp.stack([pieces[0]] + [shift(pieces[k], "dp", 2 * k) for k in range(1, n_z)])
-    pieces, left, right = lax.optimization_barrier((pieces, left, right))
-    across = [shift_col(left[:1], 1), shift_col(right[1:], -1)]
+    halves = (left[:1], right[1:])
+    pieces, halves, left, right = lax.optimization_barrier((pieces, halves, left, right))
+    across = [shift_col(halves[0], 1), shift_col(halves[1], -1)]
     far = [far, left, across[0], right, across[1]]
     pieces_all = [pieces] + [shift(pieces, "row", k) for k in range(1, n_row)]
 
     sends = down(pos, block_mask, acts, weight, n_col)
     sends, near = lax.optimization_barrier((sends, near))
-    total = lax.all_to_all(sends, "col", 0, 0).astype(F32).sum(axis=0) + both.astype(F32)
-    output, input_grad = total[0].astype(BF16), total[1].astype(BF16)
+    output, input_grad = add(lax.all_to_all(sends, "col", 0, 0), tokens, cotangent)
 
     mine, given = grad(pos, near, far, pieces_all)
     theirs = lax.ppermute(given, "dp", [(i, i ^ 1) for i in range(n_dp)])

time: 167 us -> 160 us (0.958)
  starting transfers between devices: 60 us -> 48.9 us
  waiting for transfers between devices: 62.2 us -> 65.8 us
  Pallas kernels: 31.3 us -> 33 us
    ppermute x1, starting transfers between devices: 13 us -> 0.59 us  [on_device(): theirs = lax.ppermute(given, 'dp', [(i, i ^ 1) for i in range(n_dp)])]
    ppermute x12, waiting for transfers between devices: 23.2 us -> 28 us  [shift(): lax.ppermute(value, axis, [(i, (i + by) % size) for i in range(size)])]
    unnamed x26 -> x28, local copies, waits for them, and re-layouts: 4.22 us -> 4.96 us
  transfers between devices with their start and end apart: 24 -> 24, of which waited for: 11 -> 10; matrix products, arithmetic and copies ran while one was open for 3% -> 3% of each run, Pallas kernels for 19% -> 20%
where the time goes in v4:
time: 160 us; the launch traced here: 159 us
  waiting for transfers between devices  65.8 us (41%)
  starting transfers between devices  48.9 us (31%)
  Pallas kernels  33 us (21%)
  local copies, waits for them, and re-layouts  8.33 us (5%)
  other arithmetic  2.53 us (2%)
    ppermute x9, waiting for transfers between devices, shift_col(): return lax.ppermute(value, 'col', pairs)  33.8 us
    ppermute x12, waiting for transfers between devices, shift(): lax.ppermute(value, axis, [(i, (i + by) % size) for i in range(size)])  28 us
    ppermute x12, starting transfers between devices, shift(): lax.ppermute(value, axis, [(i, (i + by) % size) for i in range(size)])  27.4 us
    ppermute x9, starting transfers between devices, shift_col(): return lax.ppermute(value, 'col', pairs)  12.7 us
    pallas_call x1, Pallas kernels, grad(): pl.pallas_call(functools.partial(grad_kernel, n_col, n_row, n_z), grid=(f...  9.75 us
    pallas_call x1, Pallas kernels, down(): pl.pallas_call(functools.partial(down_kernel, n_col, n_row), grid=(feats...  9.05 us
    pallas_call x1, Pallas kernels, up(): pl.pallas_call(functools.partial(up_kernel, n_col, n_row), grid=(cols //...  7.86 us
    unnamed x28, local copies, waits for them, and re-layouts  4.96 us
  transfers between devices with their start and end apart: 24, of which 10 were waited for; matrix products, arithmetic and copies ran while one was open for 3% of the time, Pallas kernels for 20%

profile of v4, /device:TPU:1, one launch (start us, length us, event | category | flops | bytes accessed | tf_op | source)
XLA Modules:
  0.0 159.4 jit_solution(11422781678641498177)
XLA Ops:
  0.6 1.0 pad_maximum_fusion.4
  1.6 2.6 %collective-permute-start = (bf16[2,32,2048]{2,1,0:T(8,128)(2,1)S(1)}, bf16[2,32,2048]{2,1,0:T(8,128)(2,1)S(1)}, u32[]{:S(2)}, u32[]{:S(2)}) collective-permute-start(bf16[2,32,2048]{2,1,0:T(8,128)(2,1)S(1)} %pad_maximum_fusion.4), channel_id=1, source_target_pairs={{0,4},{1,5},{2,6},{3,7},{4,0},{5,1},{6,2},{7,3},{8,12},{9,13},{10,... | collective-permute-start | bytes 786440 | tf_op jit(solution)/shard_map/ppermute | solution.py:29
  4.2 5.0 %collective-permute-done = bf16[2,32,2048]{2,1,0:T(8,128)(2,1)S(1)} collective-permute-done((bf16[2,32,2048]{2,1,0:T(8,128)(2,1)S(1)}, bf16[2,32,2048]{2,1,0:T(8,128)(2,1)S(1)}, u32[]{:S(2)}, u32[]{:S(2)}) %collective-permute-start) | collective-permute-done | bytes 262176 | tf_op jit(solution)/shard_map/ppermute | solution.py:29
  9.2 3.5 %collective-permute-start.3 = (bf16[2,2,32,2048]{3,2,1,0:T(8,128)(2,1)S(1)}, bf16[2,2,32,2048]{3,2,1,0:T(8,128)(2,1)S(1)}, u32[]{:S(2)}, u32[]{:S(2)}) collective-permute-start(bf16[2,2,32,2048]{3,2,1,0:T(8,128)(2,1)S(1)} %pad_maximum_fusion.2.refs_0_), channel_id=1, source_target_pairs={{0,3},{1,0},{2,1},{3,2},{4,7},{5,4},{6,5},{7,6},{8,11},{9,8},{10,9... | collective-permute-start | bytes 1572872 | tf_op jit(solution)/shard_map/ppermute | solution.py:29
  12.7 0.5 collective-permute-start.2
  13.2 0.6 collective-permute-start.1
  13.8 5.6 %collective-permute-start.6 = (bf16[2,32,2048]{2,1,0:T(8,128)(2,1)S(1)}, bf16[2,32,2048]{2,1,0:T(8,128)(2,1)S(1)}, u32[]{:S(2)}, u32[]{:S(2)}) collective-permute-start(bf16[2,32,2048]{2,1,0:T(8,128)(2,1)S(1)} %pad_maximum_fusion.4), channel_id=1, source_target_pairs={{0,192},{32,224},{64,0},{96,32},{128,64},{160,96},{192,128},{224,1... | collective-permute-start | bytes 786440 | tf_op jit(solution)/shard_map/ppermute | solution.py:23
  19.5 0.9 collective-permute-start.5
  20.4 3.5 %collective-permute-done.3.refs_3_ = bf16[2,2,32,2048]{3,2,1,0:T(8,128)(2,1)S(1)} collective-permute-done((bf16[2,2,32,2048]{3,2,1,0:T(8,128)(2,1)S(1)}, bf16[2,2,32,2048]{3,2,1,0:T(8,128)(2,1)S(1)}, u32[]{:S(2)}, u32[]{:S(2)}) %collective-permute-start.3) | collective-permute-done | bytes 524320 | tf_op jit(solution)/shard_map/ppermute | solution.py:29
  23.9 2.5 %collective-permute-start.4 = (bf16[2,32,2048]{2,1,0:T(8,128)(2,1)S(1)}, bf16[2,32,2048]{2,1,0:T(8,128)(2,1)S(1)}, u32[]{:S(2)}, u32[]{:S(2)}) collective-permute-start(bf16[2,32,2048]{2,1,0:T(8,128)(2,1)S(1)} %pad_maximum_fusion.4), channel_id=1, source_target_pairs={{0,64},{32,96},{64,128},{96,160},{128,192},{160,224},{192,0},{224,... | collective-permute-start | bytes 786440 | tf_op jit(solution)/shard_map/ppermute | solution.py:23
  26.4 0.1 stack.81.pos_ref
  26.5 12.8 %collective-permute-done.1.refs_1_ = bf16[2,2,32,2048]{3,2,1,0:T(8,128)(2,1)S(1)} collective-permute-done((bf16[2,2,32,2048]{3,2,1,0:T(8,128)(2,1)S(1)}, bf16[2,2,32,2048]{3,2,1,0:T(8,128)(2,1)S(1)}, u32[]{:S(2)}, u32[]{:S(2)}) %collective-permute-start.1) | collective-permute-done | bytes 524320 | tf_op jit(solution)/shard_map/ppermute | solution.py:29
  39.3 0.7 copy-done.7
  40.0 7.9 %up.1 = (f32[2,64,2048]{2,1,0:T(8,128)S(1)}, bf16[2,64,2048]{2,1,0:T(8,128)(2,1)S(1)}, bf16[2,64,2048]{2,1,0:T(8,128)(2,1)S(1)}, bf16[2,64,2048]{2,1,0:T(8,128)(2,1)S(1)}) custom-call(s32[6]{0:T(128)S(1)} %stack.81.pos_ref, s32[8,8]{1,0:T(8,128)S(1)} %copy-done.7, bf16[2,2,32,2048]{3,2,1,0:T(8,128)(2,1)S(1)} %pad_maximum_fusion.2.refs_0_, ...), custom_call_target="tpu_custom_call" | custom-call | flops 1 | bytes 1 | tf_op jit(solution)/shard_map/up/pallas_call | solution.py:80
  47.9 0.1 fusion
  48.1 1.3 collective-permute-start.7
  49.4 1.3 collective-permute-start.8
  50.7 2.6 %collective-permute-start.9 = (bf16[2,64,2048]{2,1,0:T(8,128)(2,1)S(1)}, bf16[2,64,2048]{2,1,0:T(8,128)(2,1)S(1)}, u32[]{:S(2)}, u32[]{:S(2)}) collective-permute-start(bf16[2,64,2048]{2,1,0:T(8,128)(2,1)S(1)} %get-tuple-element.49), channel_id=1, source_target_pairs={{0,16},{8,24},{16,0},{24,8},{1,17},{9,25},{17,1},{25,9},{2,18},{10... | collective-permute-start | bytes 1572872 | tf_op jit(solution)/shard_map/ppermute | solution.py:23
  53.3 1.1 collective-permute-start.10
  54.4 12.3 %collective-permute-done.7 = bf16[3,2,32,2048]{3,2,1,0:T(8,128)(2,1)S(1)} collective-permute-done((bf16[3,2,32,2048]{3,2,1,0:T(8,128)(2,1)S(1)}, bf16[3,2,32,2048]{3,2,1,0:T(8,128)(2,1)S(1)}, u32[]{:S(2)}, u32[]{:S(2)}) %collective-permute-start.7) | collective-permute-done | bytes 786464 | tf_op jit(solution)/shard_map/ppermute | solution.py:29
  66.7 1.3 pad_maximum_fusion.refs_4_
  68.0 1.5 collective-permute-start.14
  69.5 6.0 %collective-permute-done.9.refs_2_ = bf16[2,64,2048]{2,1,0:T(8,128)(2,1)S(1)} collective-permute-done((bf16[2,64,2048]{2,1,0:T(8,128)(2,1)S(1)}, bf16[2,64,2048]{2,1,0:T(8,128)(2,1)S(1)}, u32[]{:S(2)}, u32[]{:S(2)}) %collective-permute-start.9) | collective-permute-done | bytes 524320 | tf_op jit(solution)/shard_map/ppermute | solution.py:23
  75.5 2.6 %act.1 = (bf16[4,2,64,2048]{3,2,1,0:T(8,128)(2,1)}, bf16[2,64,512]{2,1,0:T(8,128)(2,1)S(1)}, bf16[2,64,512]{2,1,0:T(8,128)(2,1)S(1)}, bf16[2,64,512]{2,1,0:T(8,128)(2,1)S(1)}, bf16[2,64,512]{2,1,0:T(8,128)(2,1)S(1)}) custom-call(s32[6]{0:T(128)S(1)} %stack.81.pos_ref, f32[2,64,2048]{2,1,0:T(8,128)S(1)} %get-tuple-element.47.refs_0_, ...), custom_call_target="tpu_custom_call" | custom-call | flops 1 | bytes 1 | tf_op jit(solution)/shard_map/act/pallas_call | solution.py:122
  78.1 4.6 %all-to-all-start = ((bf16[4,2,64,2048]{3,2,1,0:T(8,128)(2,1)}), bf16[4,2,64,2048]{3,2,1,0:T(8,128)(2,1)S(1)}, u32[]{:S(2)}, u32[]{:S(2)}) async-start(bf16[4,2,64,2048]{3,2,1,0:T(8,128)(2,1)} %get-tuple-element.51), calls=%async_computation | async-start | bytes 4194304 | tf_op jit(solution)/shard_map/all_to_all | solution.py:319
  82.7 3.0 %collective-permute-start.11 = (bf16[2,64,512]{2,1,0:T(8,128)(2,1)S(1)}, bf16[2,64,512]{2,1,0:T(8,128)(2,1)S(1)}, u32[]{:S(2)}, u32[]{:S(2)}) collective-permute-start(bf16[2,64,512]{2,1,0:T(8,128)(2,1)S(1)} %get-tuple-element.61), channel_id=1, source_target_pairs={{0,64},{32,96},{64,128},{96,160},{128,192},{160,224},{192,0},{224,... | collective-permute-start | bytes 393224 | tf_op jit(solution)/shard_map/ppermute | solution.py:23
  85.7 4.2 %collective-permute-start.12 = (bf16[2,64,512]{2,1,0:T(8,128)(2,1)S(1)}, bf16[2,64,512]{2,1,0:T(8,128)(2,1)S(1)}, u32[]{:S(2)}, u32[]{:S(2)}) collective-permute-start(bf16[2,64,512]{2,1,0:T(8,128)(2,1)S(1)} %get-tuple-element.62), channel_id=1, source_target_pairs={{0,128},{32,160},{64,192},{96,224},{128,0},{160,32},{192,64},{224,... | collective-permute-start | bytes 393224 | tf_op jit(solution)/shard_map/ppermute | solution.py:23
  89.9 2.4 %collective-permute-start.13 = (bf16[2,64,512]{2,1,0:T(8,128)(2,1)S(1)}, bf16[2,64,512]{2,1,0:T(8,128)(2,1)S(1)}, u32[]{:S(2)}, u32[]{:S(2)}) collective-permute-start(bf16[2,64,512]{2,1,0:T(8,128)(2,1)S(1)} %get-tuple-element.63), channel_id=1, source_target_pairs={{0,192},{32,224},{64,0},{96,32},{128,64},{160,96},{192,128},{224,1... | collective-permute-start | bytes 393224 | tf_op jit(solution)/shard_map/ppermute | solution.py:23
  92.3 4.6 %collective-permute-done.12 = bf16[2,64,512]{2,1,0:T(8,128)(2,1)S(1)} collective-permute-done((bf16[2,64,512]{2,1,0:T(8,128)(2,1)S(1)}, bf16[2,64,512]{2,1,0:T(8,128)(2,1)S(1)}, u32[]{:S(2)}, u32[]{:S(2)}) %collective-permute-start.12) | collective-permute-done | bytes 131104 | tf_op jit(solution)/shard_map/ppermute | solution.py:23
  96.9 5.7 %collective-permute-done.13 = bf16[2,64,512]{2,1,0:T(8,128)(2,1)S(1)} collective-permute-done((bf16[2,64,512]{2,1,0:T(8,128)(2,1)S(1)}, bf16[2,64,512]{2,1,0:T(8,128)(2,1)S(1)}, u32[]{:S(2)}, u32[]{:S(2)}) %collective-permute-start.13) | collective-permute-done | bytes 131104 | tf_op jit(solution)/shard_map/ppermute | solution.py:23
  102.7 0.2 collective-permute-done.15.refs_7_
  102.9 1.2 slice.9
  104.1 2.1 %slice.8 = bf16[1,3,2,32,2048]{4,3,2,1,0:T(8,128)(2,1)} slice(bf16[2,3,2,32,2048]{4,3,2,1,0:T(8,128)(2,1)} %collective-permute-done.14.refs_5_), slice={[0:1], [0:3], [0:2], [0:32], [0:2048]} | slice | bytes 1572864 | tf_op jit(solution)/shard_map/slice | solution.py:321
  106.2 2.7 %collective-permute-start.17 = (bf16[1,3,2,32,2048]{4,3,2,1,0:T(8,128)(2,1)S(1)}, bf16[1,3,2,32,2048]{4,3,2,1,0:T(8,128)(2,1)}, u32[]{:S(2)}, u32[]{:S(2)}) collective-permute-start(bf16[1,3,2,32,2048]{4,3,2,1,0:T(8,128)(2,1)S(1)} %slice.9), channel_id=1, source_target_pairs={{0,3},{1,0},{2,1},{3,2},{4,7},{5,4},{6,5},{7,6},{8,11},{9,8},{10,9... | collective-permute-start | bytes 2359304 | tf_op jit(solution)/shard_map/ppermute | solution.py:29
  108.9 2.8 %collective-permute-start.20 = (bf16[4,2,64,512]{3,2,1,0:T(8,128)(2,1)S(1)}, bf16[4,2,64,512]{3,2,1,0:T(8,128)(2,1)}, u32[]{:S(2)}, u32[]{:S(2)}) collective-permute-start(bf16[4,2,64,512]{3,2,1,0:T(8,128)(2,1)S(1)} %pad_maximum_fusion.3.refs_9_), channel_id=1, source_target_pairs={{0,24},{8,0},{16,8},{24,16},{1,25},{9,1},{17,9},{25,17},{2,26},{10... | collective-permute-start | bytes 1572872 | tf_op jit(solution)/shard_map/ppermute | solution.py:23
  111.6 0.3 collective-permute-start.19
  112.0 0.7 collective-permute-start.18
  112.7 1.3 copy-done.11
  114.0 9.0 %down.1 = bf16[8,2,32,2048]{3,2,1,0:T(8,128)(2,1)} custom-call(s32[6]{0:T(128)} %copy-done.9, s32[8,8]{1,0:T(8,128)} %mask_ref.5, bf16[4,2,64,2048]{3,2,1,0:T(8,128)(2,1)} %copy-done.11, bf16[2048,2048]{1,0:T(8,128)(2,1)} %refs_1_.1), custom_call_target="tpu_custom_call" | custom-call | flops 3000000000 | bytes 1 | tf_op jit(solution)/shard_map/down/pallas_call | solution.py:167
  123.1 3.6 %all-to-all-start.1 = ((bf16[8,2,32,2048]{3,2,1,0:T(8,128)(2,1)}), bf16[8,2,32,2048]{3,2,1,0:T(8,128)(2,1)S(1)}, u32[]{:S(2)}, u32[]{:S(2)}) async-start(bf16[8,2,32,2048]{3,2,1,0:T(8,128)(2,1)} %down.1), calls=%async_computation.1 | async-start | bytes 4194304 | tf_op jit(solution)/shard_map/all_to_all | solution.py:329
  126.7 11.6 %collective-permute-done.18.refs_10_ = bf16[4,2,64,512]{3,2,1,0:T(8,128)(2,1)} collective-permute-done((bf16[4,2,64,512]{3,2,1,0:T(8,128)(2,1)S(1)}, bf16[4,2,64,512]{3,2,1,0:T(8,128)(2,1)}, u32[]{:S(2)}, u32[]{:S(2)}) %collective-permute-start.18) | collective-permute-done | bytes 524320 | tf_op jit(solution)/shard_map/ppermute | solution.py:23
  138.3 9.8 %grad.1 = (f32[2048,256]{1,0:T(8,128)}, f32[2048,256]{1,0:T(8,128)}) custom-call(s32[6]{0:T(128)} %copy-done.9, bf16[2,2,32,2048]{3,2,1,0:T(8,128)(2,1)} %copy-done, bf16[2,2,32,2048]{3,2,1,0:T(8,128)(2,1)} %copy-done.4, bf16[2,2,32,2048]{3,2,1,0:T(8,128)(2,1)} %copy-done.3, bf16[2,2,32,2048]{3,2,1,0:T(8,128)(2,1)} %copy-done.2, ...), custom_call_target="tpu_custom_call" | custom-call | flops 99999997952 | bytes 1000000000 | tf_op jit(solution)/shard_map/grad/pallas_call | solution.py:226
  148.1 0.6 collective-permute-start.21
  148.7 4.0 %collective-permute-done.21.b_ref = f32[2048,256]{1,0:T(8,128)S(1)} collective-permute-done((f32[2048,256]{1,0:T(8,128)}, f32[2048,256]{1,0:T(8,128)S(1)}, u32[]{:S(2)}, u32[]{:S(2)}) %collective-permute-start.21) | collective-permute-done | bytes 2097184 | tf_op jit(solution)/shard_map/ppermute | solution.py:332
  152.7 1.3 copy-done.12
  154.0 1.6 copy-done.1
  155.6 2.8 %finish.1 = f32[4096,128]{1,0:T(8,128)} custom-call(s32[6]{0:T(128)S(1)} %copy-done.10, s32[8,8]{1,0:T(8,128)S(1)} %copy-done.8, f32[2048,256]{1,0:T(8,128)S(1)} %copy-done.1, f32[2048,256]{1,0:T(8,128)} %copy-done.12), custom_call_target="tpu_custom_call" | custom-call | flops 1 | bytes 1 | tf_op jit(solution)/shard_map/finish/pallas_call | solution.py:263
  158.4 1.0 add.12
  (42 shorter events, 0.2 us)
Async XLA Ops:
  1.6 7.5 %collective-permute-start = (bf16[2,32,2048]{2,1,0:T(8,128)(2,1)S(1)}, bf16[2,32,2048]{2,1,0:T(8,128)(2,1)S(1)}, u32[]{:S(2)}, u32[]{:S(2)}) collective-permute-start(bf16[2,32,2048]{2,1,0:T(8,128)(2,1)S(1)} %pad_maximum_fusion.4), channel_id=1, source_target_pairs={{0,4},{1,5},{2,6},{3,7},{4,0},{5,1},{6,2},{7,3},{8,12},{9,13},{10,... | collective-permute-start | bytes 786440 | tf_op jit(solution)/shard_map/ppermute | solution.py:29
  9.2 38.7 %copy-start = (bf16[2,2,32,2048]{3,2,1,0:T(8,128)(2,1)}, bf16[2,2,32,2048]{3,2,1,0:T(8,128)(2,1)S(1)}, u32[]{:S(2)}) copy-start(bf16[2,2,32,2048]{3,2,1,0:T(8,128)(2,1)S(1)} %pad_maximum_fusion.2.refs_0_) | copy-start | bytes 1572868
  9.2 14.7 %collective-permute-start.3 = (bf16[2,2,32,2048]{3,2,1,0:T(8,128)(2,1)S(1)}, bf16[2,2,32,2048]{3,2,1,0:T(8,128)(2,1)S(1)}, u32[]{:S(2)}, u32[]{:S(2)}) collective-permute-start(bf16[2,2,32,2048]{3,2,1,0:T(8,128)(2,1)S(1)} %pad_maximum_fusion.2.refs_0_), channel_id=1, source_target_pairs={{0,3},{1,0},{2,1},{3,2},{4,7},{5,4},{6,5},{7,6},{8,11},{9,8},{10,9... | collective-permute-start | bytes 1572872 | tf_op jit(solution)/shard_map/ppermute | solution.py:29
  12.7 13.7 %collective-permute-start.2 = (bf16[2,2,32,2048]{3,2,1,0:T(8,128)(2,1)S(1)}, bf16[2,2,32,2048]{3,2,1,0:T(8,128)(2,1)S(1)}, u32[]{:S(2)}, u32[]{:S(2)}) collective-permute-start(bf16[2,2,32,2048]{3,2,1,0:T(8,128)(2,1)S(1)} %pad_maximum_fusion.2.refs_0_), channel_id=1, source_target_pairs={{0,2},{1,3},{2,0},{3,1},{4,6},{5,7},{6,4},{7,5},{8,10},{9,11},{10,... | collective-permute-start | bytes 1572872 | tf_op jit(solution)/shard_map/ppermute | solution.py:29
  13.2 26.1 %collective-permute-start.1 = (bf16[2,2,32,2048]{3,2,1,0:T(8,128)(2,1)S(1)}, bf16[2,2,32,2048]{3,2,1,0:T(8,128)(2,1)S(1)}, u32[]{:S(2)}, u32[]{:S(2)}) collective-permute-start(bf16[2,2,32,2048]{3,2,1,0:T(8,128)(2,1)S(1)} %pad_maximum_fusion.2.refs_0_), channel_id=1, source_target_pairs={{0,1},{1,2},{2,3},{3,0},{4,5},{5,6},{6,7},{7,4},{8,9},{9,10},{10,1... | collective-permute-start | bytes 1572872 | tf_op jit(solution)/shard_map/ppermute | solution.py:29
  13.8 34.1 %collective-permute-start.6 = (bf16[2,32,2048]{2,1,0:T(8,128)(2,1)S(1)}, bf16[2,32,2048]{2,1,0:T(8,128)(2,1)S(1)}, u32[]{:S(2)}, u32[]{:S(2)}) collective-permute-start(bf16[2,32,2048]{2,1,0:T(8,128)(2,1)S(1)} %pad_maximum_fusion.4), channel_id=1, source_target_pairs={{0,192},{32,224},{64,0},{96,32},{128,64},{160,96},{192,128},{224,1... | collective-permute-start | bytes 786440 | tf_op jit(solution)/shard_map/ppermute | solution.py:23
  19.5 28.4 %collective-permute-start.5 = (bf16[2,32,2048]{2,1,0:T(8,128)(2,1)S(1)}, bf16[2,32,2048]{2,1,0:T(8,128)(2,1)S(1)}, u32[]{:S(2)}, u32[]{:S(2)}) collective-permute-start(bf16[2,32,2048]{2,1,0:T(8,128)(2,1)S(1)} %pad_maximum_fusion.4), channel_id=1, source_target_pairs={{0,128},{32,160},{64,192},{96,224},{128,0},{160,32},{192,64},{224,... | collective-permute-start | bytes 786440 | tf_op jit(solution)/shard_map/ppermute | solution.py:23
  23.9 24.0 %copy-start.2 = (bf16[2,2,32,2048]{3,2,1,0:T(8,128)(2,1)}, bf16[2,2,32,2048]{3,2,1,0:T(8,128)(2,1)S(1)}, u32[]{:S(2)}) copy-start(bf16[2,2,32,2048]{3,2,1,0:T(8,128)(2,1)S(1)} %collective-permute-done.3.refs_3_) | copy-start | bytes 1572868
  23.9 24.0 %collective-permute-start.4 = (bf16[2,32,2048]{2,1,0:T(8,128)(2,1)S(1)}, bf16[2,32,2048]{2,1,0:T(8,128)(2,1)S(1)}, u32[]{:S(2)}, u32[]{:S(2)}) collective-permute-start(bf16[2,32,2048]{2,1,0:T(8,128)(2,1)S(1)} %pad_maximum_fusion.4), channel_id=1, source_target_pairs={{0,64},{32,96},{64,128},{96,160},{128,192},{160,224},{192,0},{224,... | collective-permute-start | bytes 786440 | tf_op jit(solution)/shard_map/ppermute | solution.py:23
  26.5 49.1 %copy-start.9 = (s32[6]{0:T(128)}, s32[6]{0:T(128)S(1)}, u32[]{:S(2)}) copy-start(s32[6]{0:T(128)S(1)} %stack.81.pos_ref) | copy-start | bytes 76
  26.5 21.4 %copy-start.3 = (bf16[2,2,32,2048]{3,2,1,0:T(8,128)(2,1)}, bf16[2,2,32,2048]{3,2,1,0:T(8,128)(2,1)S(1)}, u32[]{:S(2)}) copy-start(bf16[2,2,32,2048]{3,2,1,0:T(8,128)(2,1)S(1)} %collective-permute-done.2.refs_2_) | copy-start | bytes 1572868
  39.3 0.7 copy-start.7
  40.0 7.9 %copy-start.4 = (bf16[2,2,32,2048]{3,2,1,0:T(8,128)(2,1)}, bf16[2,2,32,2048]{3,2,1,0:T(8,128)(2,1)S(1)}, u32[]{:S(2)}) copy-start(bf16[2,2,32,2048]{3,2,1,0:T(8,128)(2,1)S(1)} %collective-permute-done.1.refs_1_) | copy-start | bytes 1572868
  48.1 18.7 %collective-permute-start.7 = (bf16[3,2,32,2048]{3,2,1,0:T(8,128)(2,1)S(1)}, bf16[3,2,32,2048]{3,2,1,0:T(8,128)(2,1)S(1)}, u32[]{:S(2)}, u32[]{:S(2)}) collective-permute-start(bf16[3,2,32,2048]{3,2,1,0:T(8,128)(2,1)S(1)} %get-tuple-element.75), channel_id=1, source_target_pairs={{0,4},{1,5},{2,6},{3,7},{4,0},{5,1},{6,2},{7,3},{8,12},{9,13},{10,... | collective-permute-start | bytes 2359304 | tf_op jit(solution)/shard_map/ppermute | solution.py:29
  49.4 20.1 %collective-permute-start.8 = (bf16[2,64,2048]{2,1,0:T(8,128)(2,1)S(1)}, bf16[2,64,2048]{2,1,0:T(8,128)(2,1)S(1)}, u32[]{:S(2)}, u32[]{:S(2)}) collective-permute-start(bf16[2,64,2048]{2,1,0:T(8,128)(2,1)S(1)} %get-tuple-element.48), channel_id=1, source_target_pairs={{0,8},{8,16},{16,24},{24,0},{1,9},{9,17},{17,25},{25,1},{2,10},{10... | collective-permute-start | bytes 1572872 | tf_op jit(solution)/shard_map/ppermute | solution.py:23
  50.7 24.8 %collective-permute-start.9 = (bf16[2,64,2048]{2,1,0:T(8,128)(2,1)S(1)}, bf16[2,64,2048]{2,1,0:T(8,128)(2,1)S(1)}, u32[]{:S(2)}, u32[]{:S(2)}) collective-permute-start(bf16[2,64,2048]{2,1,0:T(8,128)(2,1)S(1)} %get-tuple-element.49), channel_id=1, source_target_pairs={{0,16},{8,24},{16,0},{24,8},{1,17},{9,25},{17,1},{25,9},{2,18},{10... | collective-permute-start | bytes 1572872 | tf_op jit(solution)/shard_map/ppermute | solution.py:23
  53.3 22.2 %collective-permute-start.10 = (bf16[2,64,2048]{2,1,0:T(8,128)(2,1)S(1)}, bf16[2,64,2048]{2,1,0:T(8,128)(2,1)S(1)}, u32[]{:S(2)}, u32[]{:S(2)}) collective-permute-start(bf16[2,64,2048]{2,1,0:T(8,128)(2,1)S(1)} %get-tuple-element.50), channel_id=1, source_target_pairs={{0,24},{8,0},{16,8},{24,16},{1,25},{9,1},{17,9},{25,17},{2,26},{10... | collective-permute-start | bytes 1572872 | tf_op jit(solution)/shard_map/ppermute | solution.py:23
  68.0 34.8 %collective-permute-start.15 = (bf16[2,3,2,32,2048]{4,3,2,1,0:T(8,128)(2,1)}, bf16[2,3,2,32,2048]{4,3,2,1,0:T(8,128)(2,1)}, u32[]{:S(2)}, u32[]{:S(2)}) collective-permute-start(bf16[2,3,2,32,2048]{4,3,2,1,0:T(8,128)(2,1)} %pad_maximum_fusion.refs_4_), channel_id=1, source_target_pairs={{0,3},{1,0},{2,1},{3,2},{4,7},{5,4},{6,5},{7,6},{8,11},{9,8},{10,9... | collective-permute-start | bytes 4718600 | tf_op jit(solution)/shard_map/ppermute | solution.py:29
  68.0 36.0 %collective-permute-start.14 = (bf16[2,3,2,32,2048]{4,3,2,1,0:T(8,128)(2,1)}, bf16[2,3,2,32,2048]{4,3,2,1,0:T(8,128)(2,1)}, u32[]{:S(2)}, u32[]{:S(2)}) collective-permute-start(bf16[2,3,2,32,2048]{4,3,2,1,0:T(8,128)(2,1)} %pad_maximum_fusion.refs_4_), channel_id=1, source_target_pairs={{0,1},{1,2},{2,3},{3,0},{4,5},{5,6},{6,7},{7,4},{8,9},{9,10},{10,1... | collective-permute-start | bytes 4718600 | tf_op jit(solution)/shard_map/ppermute | solution.py:29
  78.1 34.6 %all-to-all-start = ((bf16[4,2,64,2048]{3,2,1,0:T(8,128)(2,1)}), bf16[4,2,64,2048]{3,2,1,0:T(8,128)(2,1)S(1)}, u32[]{:S(2)}, u32[]{:S(2)}) async-start(bf16[4,2,64,2048]{3,2,1,0:T(8,128)(2,1)} %get-tuple-element.51), calls=%async_computation | async-start | bytes 4194304 | tf_op jit(solution)/shard_map/all_to_all | solution.py:319
  82.7 9.6 %collective-permute-start.11 = (bf16[2,64,512]{2,1,0:T(8,128)(2,1)S(1)}, bf16[2,64,512]{2,1,0:T(8,128)(2,1)S(1)}, u32[]{:S(2)}, u32[]{:S(2)}) collective-permute-start(bf16[2,64,512]{2,1,0:T(8,128)(2,1)S(1)} %get-tuple-element.61), channel_id=1, source_target_pairs={{0,64},{32,96},{64,128},{96,160},{128,192},{160,224},{192,0},{224,... | collective-permute-start | bytes 393224 | tf_op jit(solution)/shard_map/ppermute | solution.py:23
  85.7 11.2 %collective-permute-start.12 = (bf16[2,64,512]{2,1,0:T(8,128)(2,1)S(1)}, bf16[2,64,512]{2,1,0:T(8,128)(2,1)S(1)}, u32[]{:S(2)}, u32[]{:S(2)}) collective-permute-start(bf16[2,64,512]{2,1,0:T(8,128)(2,1)S(1)} %get-tuple-element.62), channel_id=1, source_target_pairs={{0,128},{32,160},{64,192},{96,224},{128,0},{160,32},{192,64},{224,... | collective-permute-start | bytes 393224 | tf_op jit(solution)/shard_map/ppermute | solution.py:23
  89.9 12.7 %collective-permute-start.13 = (bf16[2,64,512]{2,1,0:T(8,128)(2,1)S(1)}, bf16[2,64,512]{2,1,0:T(8,128)(2,1)S(1)}, u32[]{:S(2)}, u32[]{:S(2)}) collective-permute-start(bf16[2,64,512]{2,1,0:T(8,128)(2,1)S(1)} %get-tuple-element.63), channel_id=1, source_target_pairs={{0,192},{32,224},{64,0},{96,32},{128,64},{160,96},{192,128},{224,1... | collective-permute-start | bytes 393224 | tf_op jit(solution)/shard_map/ppermute | solution.py:23
  102.7 20.4 %copy-start.13 = (bf16[4,2,64,512]{3,2,1,0:T(8,128)(2,1)}, bf16[4,2,64,512]{3,2,1,0:T(8,128)(2,1)S(1)}, u32[]{:S(2)}) copy-start(bf16[4,2,64,512]{3,2,1,0:T(8,128)(2,1)S(1)} %pad_maximum_fusion.3.refs_9_) | copy-start | bytes 1572868
  106.2 32.1 %collective-permute-start.16 = (bf16[1,3,2,32,2048]{4,3,2,1,0:T(8,128)(2,1)}, bf16[1,3,2,32,2048]{4,3,2,1,0:T(8,128)(2,1)}, u32[]{:S(2)}, u32[]{:S(2)}) collective-permute-start(bf16[1,3,2,32,2048]{4,3,2,1,0:T(8,128)(2,1)} %slice.8), channel_id=1, source_target_pairs={{0,1},{1,2},{2,3},{3,0},{4,5},{5,6},{6,7},{7,4},{8,9},{9,10},{10,1... | collective-permute-start | bytes 2359304 | tf_op jit(solution)/shard_map/ppermute | solution.py:29
  106.2 32.1 %collective-permute-start.17 = (bf16[1,3,2,32,2048]{4,3,2,1,0:T(8,128)(2,1)S(1)}, bf16[1,3,2,32,2048]{4,3,2,1,0:T(8,128)(2,1)}, u32[]{:S(2)}, u32[]{:S(2)}) collective-permute-start(bf16[1,3,2,32,2048]{4,3,2,1,0:T(8,128)(2,1)S(1)} %slice.9), channel_id=1, source_target_pairs={{0,3},{1,0},{2,1},{3,2},{4,7},{5,4},{6,5},{7,6},{8,11},{9,8},{10,9... | collective-permute-start | bytes 2359304 | tf_op jit(solution)/shard_map/ppermute | solution.py:29
  108.9 17.8 %collective-permute-start.20 = (bf16[4,2,64,512]{3,2,1,0:T(8,128)(2,1)S(1)}, bf16[4,2,64,512]{3,2,1,0:T(8,128)(2,1)}, u32[]{:S(2)}, u32[]{:S(2)}) collective-permute-start(bf16[4,2,64,512]{3,2,1,0:T(8,128)(2,1)S(1)} %pad_maximum_fusion.3.refs_9_), channel_id=1, source_target_pairs={{0,24},{8,0},{16,8},{24,16},{1,25},{9,1},{17,9},{25,17},{2,26},{10... | collective-permute-start | bytes 1572872 | tf_op jit(solution)/shard_map/ppermute | solution.py:23
  111.6 15.1 %collective-permute-start.19 = (bf16[4,2,64,512]{3,2,1,0:T(8,128)(2,1)S(1)}, bf16[4,2,64,512]{3,2,1,0:T(8,128)(2,1)}, u32[]{:S(2)}, u32[]{:S(2)}) collective-permute-start(bf16[4,2,64,512]{3,2,1,0:T(8,128)(2,1)S(1)} %pad_maximum_fusion.3.refs_9_), channel_id=1, source_target_pairs={{0,16},{8,24},{16,0},{24,8},{1,17},{9,25},{17,1},{25,9},{2,18},{10... | collective-permute-start | bytes 1572872 | tf_op jit(solution)/shard_map/ppermute | solution.py:23
  112.0 26.4 %collective-permute-start.18 = (bf16[4,2,64,512]{3,2,1,0:T(8,128)(2,1)S(1)}, bf16[4,2,64,512]{3,2,1,0:T(8,128)(2,1)}, u32[]{:S(2)}, u32[]{:S(2)}) collective-permute-start(bf16[4,2,64,512]{3,2,1,0:T(8,128)(2,1)S(1)} %pad_maximum_fusion.3.refs_9_), channel_id=1, source_target_pairs={{0,8},{8,16},{16,24},{24,0},{1,9},{9,17},{17,25},{25,1},{2,10},{10... | collective-permute-start | bytes 1572872 | tf_op jit(solution)/shard_map/ppermute | solution.py:23
  112.7 1.3 copy-start.11
  123.1 35.4 %all-to-all-start.1 = ((bf16[8,2,32,2048]{3,2,1,0:T(8,128)(2,1)}), bf16[8,2,32,2048]{3,2,1,0:T(8,128)(2,1)S(1)}, u32[]{:S(2)}, u32[]{:S(2)}) async-start(bf16[8,2,32,2048]{3,2,1,0:T(8,128)(2,1)} %down.1), calls=%async_computation.1 | async-start | bytes 4194304 | tf_op jit(solution)/shard_map/all_to_all | solution.py:329
  126.7 27.3 %copy-start.8 = (s32[8,8]{1,0:T(8,128)S(1)}, s32[8,8]{1,0:T(8,128)}, u32[]{:S(2)}) copy-start(s32[8,8]{1,0:T(8,128)} %mask_ref.5) | copy-start | bytes 772
  126.7 27.3 %copy-start.10 = (s32[6]{0:T(128)S(1)}, s32[6]{0:T(128)}, u32[]{:S(2)}) copy-start(s32[6]{0:T(128)} %copy-done.9) | copy-start | bytes 76
  148.1 4.6 %collective-permute-start.21 = (f32[2048,256]{1,0:T(8,128)}, f32[2048,256]{1,0:T(8,128)S(1)}, u32[]{:S(2)}, u32[]{:S(2)}) collective-permute-start(f32[2048,256]{1,0:T(8,128)} %get-tuple-element.70), channel_id=1, source_target_pairs={{0,32},{32,0},{64,96},{96,64},{128,160},{160,128},{192,224},{224,1... | collective-permute-start | bytes 6291464 | tf_op jit(solution)/shard_map/ppermute | solution.py:332
  152.7 1.3 copy-start.12
  154.0 1.6 copy-start.1
  155.6 2.8 %copy-start.5 = (bf16[32,2048]{1,0:T(8,128)(2,1)S(1)}, bf16[32,2048]{1,0:T(8,128)(2,1)}, u32[]{:S(2)}) copy-start(bf16[32,2048]{1,0:T(8,128)(2,1)} %cot_ref.1) | copy-start | bytes 393220
  155.6 2.8 %copy-start.6 = (bf16[32,2048]{1,0:T(8,128)(2,1)S(1)}, bf16[32,2048]{1,0:T(8,128)(2,1)}, u32[]{:S(2)}) copy-start(bf16[32,2048]{1,0:T(8,128)(2,1)} %tok_ref.1) | copy-start | bytes 393220

commit v5 on v4

--- a/solution.py
+++ b/solution.py
@@ -13,7 +13,7 @@
 WIDE_LIMIT = 56 * 1024 * 1024
 SMEM_SPEC = pl.BlockSpec(memory_space=pltpu.SMEM)
 COST = pl.CostEstimate(flops=1, bytes_accessed=1, transcendentals=0)
-MEDIUM = pl.CostEstimate(flops=3000000000, bytes_accessed=1, transcendentals=0)
+MEDIUM = pl.CostEstimate(flops=6000000000, bytes_accessed=1, transcendentals=0)
 LONG = pl.CostEstimate(flops=100000000000, bytes_accessed=1000000000, transcendentals=0)
 BF16, F32 = jnp.bfloat16, jnp.float32
 
@@ -269,7 +269,7 @@
         cost_estimate=COST,
         compiler_params=params(),
         name="finish",
-    )(pos, mask, mine, pltpu.with_memory_space_constraint(theirs, pltpu.HBM))
+    )(pos, mask, mine, theirs)
 
 
 def add_kernel(sums_ref, tok_ref, cot_ref, *out_refs):
@@ -319,7 +319,6 @@
     acts = lax.all_to_all(acts, "row", 0, 0)
     pieces = jnp.stack([pieces[0]] + [shift(pieces[k], "dp", 2 * k) for k in range(1, n_z)])
     halves = (left[:1], right[1:])
-    pieces, halves, left, right = lax.optimization_barrier((pieces, halves, left, right))
     across = [shift_col(halves[0], 1), shift_col(halves[1], -1)]
     far = [far, left, across[0], right, across[1]]
     pieces_all = [pieces] + [shift(pieces, "row", k) for k in range(1, n_row)]

time: 160 us -> 158 us (0.988)
    ppermute x9, waiting for transfers between devices: 33.8 us -> 44.3 us  [shift_col(): return lax.ppermute(value, 'col', pairs)]
    ppermute x12, waiting for transfers between devices: 28 us -> 17.6 us  [shift(): lax.ppermute(value, axis, [(i, (i + by) % size) for i in range(size)])]
    unnamed x28 -> x26, local copies, waits for them, and re-layouts: 4.96 us -> 3.64 us
  transfers between devices with their start and end apart: 24 -> 24, of which waited for: 10 -> 8; matrix products, arithmetic and copies ran while one was open for 3% -> 4% of each run, Pallas kernels for 20% -> 20%
where the time goes in v5:
time: 158 us; the launch traced here: 157 us
  waiting for transfers between devices  65.9 us (42%)
  starting transfers between devices  48 us (30%)
  Pallas kernels  32.3 us (20%)
  local copies, waits for them, and re-layouts  7.02 us (4%)
  other arithmetic  3.35 us (2%)
    ppermute x9, waiting for transfers between devices, shift_col(): return lax.ppermute(value, 'col', pairs)  44.3 us
    ppermute x12, starting transfers between devices, shift(): lax.ppermute(value, axis, [(i, (i + by) % size) for i in range(size)])  27.4 us
    ppermute x12, waiting for transfers between devices, shift(): lax.ppermute(value, axis, [(i, (i + by) % size) for i in range(size)])  17.6 us
    ppermute x9, starting transfers between devices, shift_col(): return lax.ppermute(value, 'col', pairs)  11.5 us
    pallas_call x1, Pallas kernels, grad(): pl.pallas_call(functools.partial(grad_kernel, n_col, n_row, n_z), grid=(f...  9.78 us
    pallas_call x1, Pallas kernels, down(): pl.pallas_call(functools.partial(down_kernel, n_col, n_row), grid=(feats...  9.03 us
    pallas_call x1, Pallas kernels, up(): pl.pallas_call(functools.partial(up_kernel, n_col, n_row), grid=(cols //...  7.86 us
    all_to_all x1, starting transfers between devices, on_device(): acts = lax.all_to_all(acts, 'row', 0, 0)  4.6 us
  transfers between devices with their start and end apart: 24, of which 8 were waited for; matrix products, arithmetic and copies ran while one was open for 4% of the time, Pallas kernels for 20%

profile of v5, /device:TPU:1, one launch (start us, length us, event | category | flops | bytes accessed | tf_op | source)
XLA Modules:
  0.0 157.4 jit_solution(10744102745054489830)
XLA Ops:
  0.6 1.0 pad_maximum_fusion.4
  1.6 2.6 %collective-permute-start = (bf16[2,32,2048]{2,1,0:T(8,128)(2,1)S(1)}, bf16[2,32,2048]{2,1,0:T(8,128)(2,1)S(1)}, u32[]{:S(2)}, u32[]{:S(2)}) collective-permute-start(bf16[2,32,2048]{2,1,0:T(8,128)(2,1)S(1)} %pad_maximum_fusion.4), channel_id=1, source_target_pairs={{0,4},{1,5},{2,6},{3,7},{4,0},{5,1},{6,2},{7,3},{8,12},{9,13},{10,... | collective-permute-start | bytes 786440 | tf_op jit(solution)/shard_map/ppermute | solution.py:29
  4.2 5.0 %collective-permute-done = bf16[2,32,2048]{2,1,0:T(8,128)(2,1)S(1)} collective-permute-done((bf16[2,32,2048]{2,1,0:T(8,128)(2,1)S(1)}, bf16[2,32,2048]{2,1,0:T(8,128)(2,1)S(1)}, u32[]{:S(2)}, u32[]{:S(2)}) %collective-permute-start) | collective-permute-done | bytes 262176 | tf_op jit(solution)/shard_map/ppermute | solution.py:29
  9.2 0.1 pad_maximum_fusion.2.refs_0_
  9.2 3.5 %collective-permute-start.3 = (bf16[2,2,32,2048]{3,2,1,0:T(8,128)(2,1)S(1)}, bf16[2,2,32,2048]{3,2,1,0:T(8,128)(2,1)S(1)}, u32[]{:S(2)}, u32[]{:S(2)}) collective-permute-start(bf16[2,2,32,2048]{3,2,1,0:T(8,128)(2,1)S(1)} %pad_maximum_fusion.2.refs_0_), channel_id=1, source_target_pairs={{0,3},{1,0},{2,1},{3,2},{4,7},{5,4},{6,5},{7,6},{8,11},{9,8},{10,9... | collective-permute-start | bytes 1572872 | tf_op jit(solution)/shard_map/ppermute | solution.py:29
  12.7 0.5 collective-permute-start.2
  13.2 0.6 collective-permute-start.1
  13.8 5.6 %collective-permute-start.6 = (bf16[2,32,2048]{2,1,0:T(8,128)(2,1)S(1)}, bf16[2,32,2048]{2,1,0:T(8,128)(2,1)S(1)}, u32[]{:S(2)}, u32[]{:S(2)}) collective-permute-start(bf16[2,32,2048]{2,1,0:T(8,128)(2,1)S(1)} %pad_maximum_fusion.4), channel_id=1, source_target_pairs={{0,192},{32,224},{64,0},{96,32},{128,64},{160,96},{192,128},{224,1... | collective-permute-start | bytes 786440 | tf_op jit(solution)/shard_map/ppermute | solution.py:23
  19.5 0.9 collective-permute-start.5
  20.4 3.5 %collective-permute-done.3.refs_3_ = bf16[2,2,32,2048]{3,2,1,0:T(8,128)(2,1)S(1)} collective-permute-done((bf16[2,2,32,2048]{3,2,1,0:T(8,128)(2,1)S(1)}, bf16[2,2,32,2048]{3,2,1,0:T(8,128)(2,1)S(1)}, u32[]{:S(2)}, u32[]{:S(2)}) %collective-permute-start.3) | collective-permute-done | bytes 524320 | tf_op jit(solution)/shard_map/ppermute | solution.py:29
  23.9 2.5 %collective-permute-start.4 = (bf16[2,32,2048]{2,1,0:T(8,128)(2,1)S(1)}, bf16[2,32,2048]{2,1,0:T(8,128)(2,1)S(1)}, u32[]{:S(2)}, u32[]{:S(2)}) collective-permute-start(bf16[2,32,2048]{2,1,0:T(8,128)(2,1)S(1)} %pad_maximum_fusion.4), channel_id=1, source_target_pairs={{0,64},{32,96},{64,128},{96,160},{128,192},{160,224},{192,0},{224,... | collective-permute-start | bytes 786440 | tf_op jit(solution)/shard_map/ppermute | solution.py:23
  26.4 0.1 stack.81.pos_ref
  26.5 12.8 %collective-permute-done.1.refs_1_ = bf16[2,2,32,2048]{3,2,1,0:T(8,128)(2,1)S(1)} collective-permute-done((bf16[2,2,32,2048]{3,2,1,0:T(8,128)(2,1)S(1)}, bf16[2,2,32,2048]{3,2,1,0:T(8,128)(2,1)S(1)}, u32[]{:S(2)}, u32[]{:S(2)}) %collective-permute-start.1) | collective-permute-done | bytes 524320 | tf_op jit(solution)/shard_map/ppermute | solution.py:29
  39.3 0.7 copy-done.7
  40.0 7.9 %up.1 = (f32[2,64,2048]{2,1,0:T(8,128)S(1)}, bf16[2,64,2048]{2,1,0:T(8,128)(2,1)S(1)}, bf16[2,64,2048]{2,1,0:T(8,128)(2,1)S(1)}, bf16[2,64,2048]{2,1,0:T(8,128)(2,1)S(1)}) custom-call(s32[6]{0:T(128)S(1)} %stack.81.pos_ref, s32[8,8]{1,0:T(8,128)S(1)} %copy-done.7, bf16[2,2,32,2048]{3,2,1,0:T(8,128)(2,1)S(1)} %pad_maximum_fusion.2.refs_0_, ...), custom_call_target="tpu_custom_call" | custom-call | flops 1 | bytes 1 | tf_op jit(solution)/shard_map/up/pallas_call | solution.py:80
  47.9 0.1 fusion
  48.1 1.3 collective-permute-start.7
  49.4 1.3 collective-permute-start.8
  50.7 2.6 %collective-permute-start.9 = (bf16[2,64,2048]{2,1,0:T(8,128)(2,1)S(1)}, bf16[2,64,2048]{2,1,0:T(8,128)(2,1)S(1)}, u32[]{:S(2)}, u32[]{:S(2)}) collective-permute-start(bf16[2,64,2048]{2,1,0:T(8,128)(2,1)S(1)} %get-tuple-element.44), channel_id=1, source_target_pairs={{0,16},{8,24},{16,0},{24,8},{1,17},{9,25},{17,1},{25,9},{2,18},{10... | collective-permute-start | bytes 1572872 | tf_op jit(solution)/shard_map/ppermute | solution.py:23
  53.3 1.1 collective-permute-start.10
  54.4 12.3 %collective-permute-done.7 = bf16[3,2,32,2048]{3,2,1,0:T(8,128)(2,1)S(1)} collective-permute-done((bf16[3,2,32,2048]{3,2,1,0:T(8,128)(2,1)S(1)}, bf16[3,2,32,2048]{3,2,1,0:T(8,128)(2,1)S(1)}, u32[]{:S(2)}, u32[]{:S(2)}) %collective-permute-start.7) | collective-permute-done | bytes 786464 | tf_op jit(solution)/shard_map/ppermute | solution.py:29
  66.7 1.3 pad_maximum_fusion.refs_4_
  68.1 1.5 collective-permute-start.11
  69.5 6.0 %collective-permute-done.9.refs_2_ = bf16[2,64,2048]{2,1,0:T(8,128)(2,1)S(1)} collective-permute-done((bf16[2,64,2048]{2,1,0:T(8,128)(2,1)S(1)}, bf16[2,64,2048]{2,1,0:T(8,128)(2,1)S(1)}, u32[]{:S(2)}, u32[]{:S(2)}) %collective-permute-start.9) | collective-permute-done | bytes 524320 | tf_op jit(solution)/shard_map/ppermute | solution.py:23
  75.5 2.6 %act.1 = (bf16[4,2,64,2048]{3,2,1,0:T(8,128)(2,1)}, bf16[2,64,512]{2,1,0:T(8,128)(2,1)S(1)}, bf16[2,64,512]{2,1,0:T(8,128)(2,1)S(1)}, bf16[2,64,512]{2,1,0:T(8,128)(2,1)S(1)}, bf16[2,64,512]{2,1,0:T(8,128)(2,1)S(1)}) custom-call(s32[6]{0:T(128)S(1)} %stack.81.pos_ref, f32[2,64,2048]{2,1,0:T(8,128)S(1)} %get-tuple-element.42.refs_0_, ...), custom_call_target="tpu_custom_call" | custom-call | flops 1 | bytes 1 | tf_op jit(solution)/shard_map/act/pallas_call | solution.py:122
  78.1 4.6 %all-to-all-start = ((bf16[4,2,64,2048]{3,2,1,0:T(8,128)(2,1)}), bf16[4,2,64,2048]{3,2,1,0:T(8,128)(2,1)S(1)}, u32[]{:S(2)}, u32[]{:S(2)}) async-start(bf16[4,2,64,2048]{3,2,1,0:T(8,128)(2,1)} %get-tuple-element.46), calls=%async_computation | async-start | bytes 4194304 | tf_op jit(solution)/shard_map/all_to_all | solution.py:319
  82.7 3.0 %collective-permute-start.15 = (bf16[2,64,512]{2,1,0:T(8,128)(2,1)S(1)}, bf16[2,64,512]{2,1,0:T(8,128)(2,1)S(1)}, u32[]{:S(2)}, u32[]{:S(2)}) collective-permute-start(bf16[2,64,512]{2,1,0:T(8,128)(2,1)S(1)} %get-tuple-element.56), channel_id=1, source_target_pairs={{0,64},{32,96},{64,128},{96,160},{128,192},{160,224},{192,0},{224,... | collective-permute-start | bytes 393224 | tf_op jit(solution)/shard_map/ppermute | solution.py:23
  85.7 4.2 %collective-permute-start.16 = (bf16[2,64,512]{2,1,0:T(8,128)(2,1)S(1)}, bf16[2,64,512]{2,1,0:T(8,128)(2,1)S(1)}, u32[]{:S(2)}, u32[]{:S(2)}) collective-permute-start(bf16[2,64,512]{2,1,0:T(8,128)(2,1)S(1)} %get-tuple-element.57), channel_id=1, source_target_pairs={{0,128},{32,160},{64,192},{96,224},{128,0},{160,32},{192,64},{224,... | collective-permute-start | bytes 393224 | tf_op jit(solution)/shard_map/ppermute | solution.py:23
  89.9 2.4 %collective-permute-start.17 = (bf16[2,64,512]{2,1,0:T(8,128)(2,1)S(1)}, bf16[2,64,512]{2,1,0:T(8,128)(2,1)S(1)}, u32[]{:S(2)}, u32[]{:S(2)}) collective-permute-start(bf16[2,64,512]{2,1,0:T(8,128)(2,1)S(1)} %get-tuple-element.58), channel_id=1, source_target_pairs={{0,192},{32,224},{64,0},{96,32},{128,64},{160,96},{192,128},{224,1... | collective-permute-start | bytes 393224 | tf_op jit(solution)/shard_map/ppermute | solution.py:23
  92.3 10.6 %collective-permute-done.13.refs_7_ = bf16[2,3,2,32,2048]{4,3,2,1,0:T(8,128)(2,1)} collective-permute-done((bf16[2,3,2,32,2048]{4,3,2,1,0:T(8,128)(2,1)}, bf16[2,3,2,32,2048]{4,3,2,1,0:T(8,128)(2,1)}, u32[]{:S(2)}, u32[]{:S(2)}) %collective-permute-start.13) | collective-permute-done | bytes 1572896 | tf_op jit(solution)/shard_map/ppermute | solution.py:29
  102.9 1.2 slice.9
  104.1 1.4 collective-permute-start.14
  105.5 2.1 %slice.8 = bf16[1,3,2,32,2048]{4,3,2,1,0:T(8,128)(2,1)} slice(bf16[2,3,2,32,2048]{4,3,2,1,0:T(8,128)(2,1)} %collective-permute-done.11.refs_5_), slice={[0:1], [0:3], [0:2], [0:32], [0:2048]} | slice | bytes 1572864 | tf_op jit(solution)/shard_map/slice | solution.py:321
  107.6 0.1 collective-permute-start.12
  107.8 0.9 pad_maximum_fusion.3.refs_9_
  108.6 2.8 %collective-permute-start.20 = (bf16[4,2,64,512]{3,2,1,0:T(8,128)(2,1)}, bf16[4,2,64,512]{3,2,1,0:T(8,128)(2,1)S(1)}, u32[]{:S(2)}, u32[]{:S(2)}) collective-permute-start(bf16[4,2,64,512]{3,2,1,0:T(8,128)(2,1)} %pad_maximum_fusion.3.refs_9_), channel_id=1, source_target_pairs={{0,24},{8,0},{16,8},{24,16},{1,25},{9,1},{17,9},{25,17},{2,26},{10... | collective-permute-start | bytes 1572872 | tf_op jit(solution)/shard_map/ppermute | solution.py:23
  111.4 0.3 collective-permute-start.19
  111.8 0.7 collective-permute-start.18
  112.5 1.3 copy-done.11
  113.8 9.0 %down.1 = bf16[8,2,32,2048]{3,2,1,0:T(8,128)(2,1)} custom-call(s32[6]{0:T(128)} %copy-done.9, s32[8,8]{1,0:T(8,128)} %mask_ref.5, bf16[4,2,64,2048]{3,2,1,0:T(8,128)(2,1)} %copy-done.11, bf16[2048,2048]{1,0:T(8,128)(2,1)} %refs_1_.1), custom_call_target="tpu_custom_call" | custom-call | flops 6000000000 | bytes 1 | tf_op jit(solution)/shard_map/down/pallas_call | solution.py:167
  122.8 3.8 %all-to-all-start.1 = ((bf16[8,2,32,2048]{3,2,1,0:T(8,128)(2,1)}), bf16[8,2,32,2048]{3,2,1,0:T(8,128)(2,1)S(1)}, u32[]{:S(2)}, u32[]{:S(2)}) async-start(bf16[8,2,32,2048]{3,2,1,0:T(8,128)(2,1)} %down.1), calls=%async_computation.1 | async-start | bytes 4194304 | tf_op jit(solution)/shard_map/all_to_all | solution.py:328
  126.7 11.6 %collective-permute-done.18.refs_10_ = bf16[4,2,64,512]{3,2,1,0:T(8,128)(2,1)} collective-permute-done((bf16[4,2,64,512]{3,2,1,0:T(8,128)(2,1)}, bf16[4,2,64,512]{3,2,1,0:T(8,128)(2,1)}, u32[]{:S(2)}, u32[]{:S(2)}) %collective-permute-start.18) | collective-permute-done | bytes 524320 | tf_op jit(solution)/shard_map/ppermute | solution.py:23
  138.3 9.8 %grad.1 = (f32[2048,256]{1,0:T(8,128)}, f32[2048,256]{1,0:T(8,128)}) custom-call(s32[6]{0:T(128)} %copy-done.9, bf16[2,2,32,2048]{3,2,1,0:T(8,128)(2,1)} %copy-done, bf16[2,2,32,2048]{3,2,1,0:T(8,128)(2,1)} %copy-done.4, bf16[2,2,32,2048]{3,2,1,0:T(8,128)(2,1)} %copy-done.3, bf16[2,2,32,2048]{3,2,1,0:T(8,128)(2,1)} %copy-done.2, ...), custom_call_target="tpu_custom_call" | custom-call | flops 99999997952 | bytes 1000000000 | tf_op jit(solution)/shard_map/grad/pallas_call | solution.py:226
  148.1 0.6 collective-permute-start.21
  148.7 4.0 %collective-permute-done.21.b_ref = f32[2048,256]{1,0:T(8,128)S(1)} collective-permute-done((f32[2048,256]{1,0:T(8,128)}, f32[2048,256]{1,0:T(8,128)S(1)}, u32[]{:S(2)}, u32[]{:S(2)}) %collective-permute-start.21) | collective-permute-done | bytes 2097184 | tf_op jit(solution)/shard_map/ppermute | solution.py:331
  152.7 1.6 %copy-done.1 = f32[2048,256]{1,0:T(8,128)S(1)} copy-done((f32[2048,256]{1,0:T(8,128)S(1)}, f32[2048,256]{1,0:T(8,128)}, u32[]{:S(2)}) %copy-start.1) | copy-done | bytes 2097176
  154.3 2.1 %finish.1 = f32[4096,128]{1,0:T(8,128)} custom-call(s32[6]{0:T(128)S(1)} %copy-done.10, s32[8,8]{1,0:T(8,128)S(1)} %copy-done.8, f32[2048,256]{1,0:T(8,128)S(1)} %copy-done.1, f32[2048,256]{1,0:T(8,128)S(1)} %collective-permute-done.21.b_ref), custom_call_target="tpu_custom_call" | custom-call | flops 1 | bytes 1 | tf_op jit(solution)/shard_map/finish/pallas_call | solution.py:263
  156.4 1.0 add.12
  (40 shorter events, 0.1 us)
Async XLA Ops:
  1.6 7.5 %collective-permute-start = (bf16[2,32,2048]{2,1,0:T(8,128)(2,1)S(1)}, bf16[2,32,2048]{2,1,0:T(8,128)(2,1)S(1)}, u32[]{:S(2)}, u32[]{:S(2)}) collective-permute-start(bf16[2,32,2048]{2,1,0:T(8,128)(2,1)S(1)} %pad_maximum_fusion.4), channel_id=1, source_target_pairs={{0,4},{1,5},{2,6},{3,7},{4,0},{5,1},{6,2},{7,3},{8,12},{9,13},{10,... | collective-permute-start | bytes 786440 | tf_op jit(solution)/shard_map/ppermute | solution.py:29
  9.2 38.7 %copy-start = (bf16[2,2,32,2048]{3,2,1,0:T(8,128)(2,1)}, bf16[2,2,32,2048]{3,2,1,0:T(8,128)(2,1)S(1)}, u32[]{:S(2)}) copy-start(bf16[2,2,32,2048]{3,2,1,0:T(8,128)(2,1)S(1)} %pad_maximum_fusion.2.refs_0_) | copy-start | bytes 1572868
  9.2 14.7 %collective-permute-start.3 = (bf16[2,2,32,2048]{3,2,1,0:T(8,128)(2,1)S(1)}, bf16[2,2,32,2048]{3,2,1,0:T(8,128)(2,1)S(1)}, u32[]{:S(2)}, u32[]{:S(2)}) collective-permute-start(bf16[2,2,32,2048]{3,2,1,0:T(8,128)(2,1)S(1)} %pad_maximum_fusion.2.refs_0_), channel_id=1, source_target_pairs={{0,3},{1,0},{2,1},{3,2},{4,7},{5,4},{6,5},{7,6},{8,11},{9,8},{10,9... | collective-permute-start | bytes 1572872 | tf_op jit(solution)/shard_map/ppermute | solution.py:29
  12.7 13.7 %collective-permute-start.2 = (bf16[2,2,32,2048]{3,2,1,0:T(8,128)(2,1)S(1)}, bf16[2,2,32,2048]{3,2,1,0:T(8,128)(2,1)S(1)}, u32[]{:S(2)}, u32[]{:S(2)}) collective-permute-start(bf16[2,2,32,2048]{3,2,1,0:T(8,128)(2,1)S(1)} %pad_maximum_fusion.2.refs_0_), channel_id=1, source_target_pairs={{0,2},{1,3},{2,0},{3,1},{4,6},{5,7},{6,4},{7,5},{8,10},{9,11},{10,... | collective-permute-start | bytes 1572872 | tf_op jit(solution)/shard_map/ppermute | solution.py:29
  13.2 26.1 %collective-permute-start.1 = (bf16[2,2,32,2048]{3,2,1,0:T(8,128)(2,1)S(1)}, bf16[2,2,32,2048]{3,2,1,0:T(8,128)(2,1)S(1)}, u32[]{:S(2)}, u32[]{:S(2)}) collective-permute-start(bf16[2,2,32,2048]{3,2,1,0:T(8,128)(2,1)S(1)} %pad_maximum_fusion.2.refs_0_), channel_id=1, source_target_pairs={{0,1},{1,2},{2,3},{3,0},{4,5},{5,6},{6,7},{7,4},{8,9},{9,10},{10,1... | collective-permute-start | bytes 1572872 | tf_op jit(solution)/shard_map/ppermute | solution.py:29
  13.8 34.1 %collective-permute-start.6 = (bf16[2,32,2048]{2,1,0:T(8,128)(2,1)S(1)}, bf16[2,32,2048]{2,1,0:T(8,128)(2,1)S(1)}, u32[]{:S(2)}, u32[]{:S(2)}) collective-permute-start(bf16[2,32,2048]{2,1,0:T(8,128)(2,1)S(1)} %pad_maximum_fusion.4), channel_id=1, source_target_pairs={{0,192},{32,224},{64,0},{96,32},{128,64},{160,96},{192,128},{224,1... | collective-permute-start | bytes 786440 | tf_op jit(solution)/shard_map/ppermute | solution.py:23
  19.5 28.4 %collective-permute-start.5 = (bf16[2,32,2048]{2,1,0:T(8,128)(2,1)S(1)}, bf16[2,32,2048]{2,1,0:T(8,128)(2,1)S(1)}, u32[]{:S(2)}, u32[]{:S(2)}) collective-permute-start(bf16[2,32,2048]{2,1,0:T(8,128)(2,1)S(1)} %pad_maximum_fusion.4), channel_id=1, source_target_pairs={{0,128},{32,160},{64,192},{96,224},{128,0},{160,32},{192,64},{224,... | collective-permute-start | bytes 786440 | tf_op jit(solution)/shard_map/ppermute | solution.py:23
  23.9 24.0 %copy-start.2 = (bf16[2,2,32,2048]{3,2,1,0:T(8,128)(2,1)}, bf16[2,2,32,2048]{3,2,1,0:T(8,128)(2,1)S(1)}, u32[]{:S(2)}) copy-start(bf16[2,2,32,2048]{3,2,1,0:T(8,128)(2,1)S(1)} %collective-permute-done.3.refs_3_) | copy-start | bytes 1572868
  23.9 24.0 %collective-permute-start.4 = (bf16[2,32,2048]{2,1,0:T(8,128)(2,1)S(1)}, bf16[2,32,2048]{2,1,0:T(8,128)(2,1)S(1)}, u32[]{:S(2)}, u32[]{:S(2)}) collective-permute-start(bf16[2,32,2048]{2,1,0:T(8,128)(2,1)S(1)} %pad_maximum_fusion.4), channel_id=1, source_target_pairs={{0,64},{32,96},{64,128},{96,160},{128,192},{160,224},{192,0},{224,... | collective-permute-start | bytes 786440 | tf_op jit(solution)/shard_map/ppermute | solution.py:23
  26.5 49.1 %copy-start.9 = (s32[6]{0:T(128)}, s32[6]{0:T(128)S(1)}, u32[]{:S(2)}) copy-start(s32[6]{0:T(128)S(1)} %stack.81.pos_ref) | copy-start | bytes 76
  26.5 21.4 %copy-start.3 = (bf16[2,2,32,2048]{3,2,1,0:T(8,128)(2,1)}, bf16[2,2,32,2048]{3,2,1,0:T(8,128)(2,1)S(1)}, u32[]{:S(2)}) copy-start(bf16[2,2,32,2048]{3,2,1,0:T(8,128)(2,1)S(1)} %collective-permute-done.2.refs_2_) | copy-start | bytes 1572868
  39.3 0.7 copy-start.7
  40.0 7.9 %copy-start.4 = (bf16[2,2,32,2048]{3,2,1,0:T(8,128)(2,1)}, bf16[2,2,32,2048]{3,2,1,0:T(8,128)(2,1)S(1)}, u32[]{:S(2)}) copy-start(bf16[2,2,32,2048]{3,2,1,0:T(8,128)(2,1)S(1)} %collective-permute-done.1.refs_1_) | copy-start | bytes 1572868
  48.1 18.7 %collective-permute-start.7 = (bf16[3,2,32,2048]{3,2,1,0:T(8,128)(2,1)S(1)}, bf16[3,2,32,2048]{3,2,1,0:T(8,128)(2,1)S(1)}, u32[]{:S(2)}, u32[]{:S(2)}) collective-permute-start(bf16[3,2,32,2048]{3,2,1,0:T(8,128)(2,1)S(1)} %get-tuple-element.65), channel_id=1, source_target_pairs={{0,4},{1,5},{2,6},{3,7},{4,0},{5,1},{6,2},{7,3},{8,12},{9,13},{10,... | collective-permute-start | bytes 2359304 | tf_op jit(solution)/shard_map/ppermute | solution.py:29
  49.4 20.1 %collective-permute-start.8 = (bf16[2,64,2048]{2,1,0:T(8,128)(2,1)S(1)}, bf16[2,64,2048]{2,1,0:T(8,128)(2,1)S(1)}, u32[]{:S(2)}, u32[]{:S(2)}) collective-permute-start(bf16[2,64,2048]{2,1,0:T(8,128)(2,1)S(1)} %get-tuple-element.43), channel_id=1, source_target_pairs={{0,8},{8,16},{16,24},{24,0},{1,9},{9,17},{17,25},{25,1},{2,10},{10... | collective-permute-start | bytes 1572872 | tf_op jit(solution)/shard_map/ppermute | solution.py:23
  50.7 24.8 %collective-permute-start.9 = (bf16[2,64,2048]{2,1,0:T(8,128)(2,1)S(1)}, bf16[2,64,2048]{2,1,0:T(8,128)(2,1)S(1)}, u32[]{:S(2)}, u32[]{:S(2)}) collective-permute-start(bf16[2,64,2048]{2,1,0:T(8,128)(2,1)S(1)} %get-tuple-element.44), channel_id=1, source_target_pairs={{0,16},{8,24},{16,0},{24,8},{1,17},{9,25},{17,1},{25,9},{2,18},{10... | collective-permute-start | bytes 1572872 | tf_op jit(solution)/shard_map/ppermute | solution.py:23
  53.3 22.2 %collective-permute-start.10 = (bf16[2,64,2048]{2,1,0:T(8,128)(2,1)S(1)}, bf16[2,64,2048]{2,1,0:T(8,128)(2,1)S(1)}, u32[]{:S(2)}, u32[]{:S(2)}) collective-permute-start(bf16[2,64,2048]{2,1,0:T(8,128)(2,1)S(1)} %get-tuple-element.45), channel_id=1, source_target_pairs={{0,24},{8,0},{16,8},{24,16},{1,25},{9,1},{17,9},{25,17},{2,26},{10... | collective-permute-start | bytes 1572872 | tf_op jit(solution)/shard_map/ppermute | solution.py:23
  68.1 34.8 %collective-permute-start.13 = (bf16[2,3,2,32,2048]{4,3,2,1,0:T(8,128)(2,1)}, bf16[2,3,2,32,2048]{4,3,2,1,0:T(8,128)(2,1)}, u32[]{:S(2)}, u32[]{:S(2)}) collective-permute-start(bf16[2,3,2,32,2048]{4,3,2,1,0:T(8,128)(2,1)} %pad_maximum_fusion.refs_4_), channel_id=1, source_target_pairs={{0,3},{1,0},{2,1},{3,2},{4,7},{5,4},{6,5},{7,6},{8,11},{9,8},{10,9... | collective-permute-start | bytes 4718600 | tf_op jit(solution)/shard_map/ppermute | solution.py:29
  68.1 37.5 %collective-permute-start.11 = (bf16[2,3,2,32,2048]{4,3,2,1,0:T(8,128)(2,1)}, bf16[2,3,2,32,2048]{4,3,2,1,0:T(8,128)(2,1)}, u32[]{:S(2)}, u32[]{:S(2)}) collective-permute-start(bf16[2,3,2,32,2048]{4,3,2,1,0:T(8,128)(2,1)} %pad_maximum_fusion.refs_4_), channel_id=1, source_target_pairs={{0,1},{1,2},{2,3},{3,0},{4,5},{5,6},{6,7},{7,4},{8,9},{9,10},{10,1... | collective-permute-start | bytes 4718600 | tf_op jit(solution)/shard_map/ppermute | solution.py:29
  78.1 34.4 %all-to-all-start = ((bf16[4,2,64,2048]{3,2,1,0:T(8,128)(2,1)}), bf16[4,2,64,2048]{3,2,1,0:T(8,128)(2,1)S(1)}, u32[]{:S(2)}, u32[]{:S(2)}) async-start(bf16[4,2,64,2048]{3,2,1,0:T(8,128)(2,1)} %get-tuple-element.46), calls=%async_computation | async-start | bytes 4194304 | tf_op jit(solution)/shard_map/all_to_all | solution.py:319
  82.7 25.1 %collective-permute-start.15 = (bf16[2,64,512]{2,1,0:T(8,128)(2,1)S(1)}, bf16[2,64,512]{2,1,0:T(8,128)(2,1)S(1)}, u32[]{:S(2)}, u32[]{:S(2)}) collective-permute-start(bf16[2,64,512]{2,1,0:T(8,128)(2,1)S(1)} %get-tuple-element.56), channel_id=1, source_target_pairs={{0,64},{32,96},{64,128},{96,160},{128,192},{160,224},{192,0},{224,... | collective-permute-start | bytes 393224 | tf_op jit(solution)/shard_map/ppermute | solution.py:23
  85.7 22.1 %collective-permute-start.16 = (bf16[2,64,512]{2,1,0:T(8,128)(2,1)S(1)}, bf16[2,64,512]{2,1,0:T(8,128)(2,1)S(1)}, u32[]{:S(2)}, u32[]{:S(2)}) collective-permute-start(bf16[2,64,512]{2,1,0:T(8,128)(2,1)S(1)} %get-tuple-element.57), channel_id=1, source_target_pairs={{0,128},{32,160},{64,192},{96,224},{128,0},{160,32},{192,64},{224,... | collective-permute-start | bytes 393224 | tf_op jit(solution)/shard_map/ppermute | solution.py:23
  89.9 17.9 %collective-permute-start.17 = (bf16[2,64,512]{2,1,0:T(8,128)(2,1)S(1)}, bf16[2,64,512]{2,1,0:T(8,128)(2,1)S(1)}, u32[]{:S(2)}, u32[]{:S(2)}) collective-permute-start(bf16[2,64,512]{2,1,0:T(8,128)(2,1)S(1)} %get-tuple-element.58), channel_id=1, source_target_pairs={{0,192},{32,224},{64,0},{96,32},{128,64},{160,96},{192,128},{224,1... | collective-permute-start | bytes 393224 | tf_op jit(solution)/shard_map/ppermute | solution.py:23
  104.1 34.2 %collective-permute-start.14 = (bf16[1,3,2,32,2048]{4,3,2,1,0:T(8,128)(2,1)S(1)}, bf16[1,3,2,32,2048]{4,3,2,1,0:T(8,128)(2,1)}, u32[]{:S(2)}, u32[]{:S(2)}) collective-permute-start(bf16[1,3,2,32,2048]{4,3,2,1,0:T(8,128)(2,1)S(1)} %slice.9), channel_id=1, source_target_pairs={{0,3},{1,0},{2,1},{3,2},{4,7},{5,4},{6,5},{7,6},{8,11},{9,8},{10,9... | collective-permute-start | bytes 2359304 | tf_op jit(solution)/shard_map/ppermute | solution.py:29
  107.6 30.7 %collective-permute-start.12 = (bf16[1,3,2,32,2048]{4,3,2,1,0:T(8,128)(2,1)}, bf16[1,3,2,32,2048]{4,3,2,1,0:T(8,128)(2,1)}, u32[]{:S(2)}, u32[]{:S(2)}) collective-permute-start(bf16[1,3,2,32,2048]{4,3,2,1,0:T(8,128)(2,1)} %slice.8), channel_id=1, source_target_pairs={{0,1},{1,2},{2,3},{3,0},{4,5},{5,6},{6,7},{7,4},{8,9},{9,10},{10,1... | collective-permute-start | bytes 2359304 | tf_op jit(solution)/shard_map/ppermute | solution.py:29
  108.6 18.0 %collective-permute-start.20 = (bf16[4,2,64,512]{3,2,1,0:T(8,128)(2,1)}, bf16[4,2,64,512]{3,2,1,0:T(8,128)(2,1)S(1)}, u32[]{:S(2)}, u32[]{:S(2)}) collective-permute-start(bf16[4,2,64,512]{3,2,1,0:T(8,128)(2,1)} %pad_maximum_fusion.3.refs_9_), channel_id=1, source_target_pairs={{0,24},{8,0},{16,8},{24,16},{1,25},{9,1},{17,9},{25,17},{2,26},{10... | collective-permute-start | bytes 1572872 | tf_op jit(solution)/shard_map/ppermute | solution.py:23
  111.4 15.3 %collective-permute-start.19 = (bf16[4,2,64,512]{3,2,1,0:T(8,128)(2,1)}, bf16[4,2,64,512]{3,2,1,0:T(8,128)(2,1)}, u32[]{:S(2)}, u32[]{:S(2)}) collective-permute-start(bf16[4,2,64,512]{3,2,1,0:T(8,128)(2,1)} %pad_maximum_fusion.3.refs_9_), channel_id=1, source_target_pairs={{0,16},{8,24},{16,0},{24,8},{1,17},{9,25},{17,1},{25,9},{2,18},{10... | collective-permute-start | bytes 1572872 | tf_op jit(solution)/shard_map/ppermute | solution.py:23
  111.8 26.6 %collective-permute-start.18 = (bf16[4,2,64,512]{3,2,1,0:T(8,128)(2,1)}, bf16[4,2,64,512]{3,2,1,0:T(8,128)(2,1)}, u32[]{:S(2)}, u32[]{:S(2)}) collective-permute-start(bf16[4,2,64,512]{3,2,1,0:T(8,128)(2,1)} %pad_maximum_fusion.3.refs_9_), channel_id=1, source_target_pairs={{0,8},{8,16},{16,24},{24,0},{1,9},{9,17},{17,25},{25,1},{2,10},{10... | collective-permute-start | bytes 1572872 | tf_op jit(solution)/shard_map/ppermute | solution.py:23
  112.5 1.3 copy-start.11
  122.8 33.6 %all-to-all-start.1 = ((bf16[8,2,32,2048]{3,2,1,0:T(8,128)(2,1)}), bf16[8,2,32,2048]{3,2,1,0:T(8,128)(2,1)S(1)}, u32[]{:S(2)}, u32[]{:S(2)}) async-start(bf16[8,2,32,2048]{3,2,1,0:T(8,128)(2,1)} %down.1), calls=%async_computation.1 | async-start | bytes 4194304 | tf_op jit(solution)/shard_map/all_to_all | solution.py:328
  126.7 26.0 %copy-start.8 = (s32[8,8]{1,0:T(8,128)S(1)}, s32[8,8]{1,0:T(8,128)}, u32[]{:S(2)}) copy-start(s32[8,8]{1,0:T(8,128)} %mask_ref.5) | copy-start | bytes 772
  126.7 26.0 %copy-start.10 = (s32[6]{0:T(128)S(1)}, s32[6]{0:T(128)}, u32[]{:S(2)}) copy-start(s32[6]{0:T(128)} %copy-done.9) | copy-start | bytes 76
  126.7 11.6 %copy-start.12 = (bf16[4,2,64,512]{3,2,1,0:T(8,128)(2,1)}, bf16[4,2,64,512]{3,2,1,0:T(8,128)(2,1)S(1)}, u32[]{:S(2)}) copy-start(bf16[4,2,64,512]{3,2,1,0:T(8,128)(2,1)S(1)} %collective-permute-done.20.refs_12_) | copy-start | bytes 1572868
  148.1 4.6 %collective-permute-start.21 = (f32[2048,256]{1,0:T(8,128)}, f32[2048,256]{1,0:T(8,128)S(1)}, u32[]{:S(2)}, u32[]{:S(2)}) collective-permute-start(f32[2048,256]{1,0:T(8,128)} %get-tuple-element.60), channel_id=1, source_target_pairs={{0,32},{32,0},{64,96},{96,64},{128,160},{160,128},{192,224},{224,1... | collective-permute-start | bytes 6291464 | tf_op jit(solution)/shard_map/ppermute | solution.py:331
  152.7 1.6 %copy-start.1 = (f32[2048,256]{1,0:T(8,128)S(1)}, f32[2048,256]{1,0:T(8,128)}, u32[]{:S(2)}) copy-start(f32[2048,256]{1,0:T(8,128)} %get-tuple-element.59.a_ref) | copy-start | bytes 6291460
  154.3 2.1 %copy-start.5 = (bf16[32,2048]{1,0:T(8,128)(2,1)S(1)}, bf16[32,2048]{1,0:T(8,128)(2,1)}, u32[]{:S(2)}) copy-start(bf16[32,2048]{1,0:T(8,128)(2,1)} %cot_ref.1) | copy-start | bytes 393220
  154.3 2.1 %copy-start.6 = (bf16[32,2048]{1,0:T(8,128)(2,1)S(1)}, bf16[32,2048]{1,0:T(8,128)(2,1)}, u32[]{:S(2)}) copy-start(bf16[32,2048]{1,0:T(8,128)(2,1)} %tok_ref.1) | copy-start | bytes 393220

commit v6 on v5

--- a/solution.py
+++ b/solution.py
@@ -218,7 +218,7 @@
     other_ref[...] = sum_ref[:, pl.ds(BLOCK - mine, BLOCK)]
 
 
-def grad(pos, near, far, hidden, width=512):
+def grad(pos, near, far, hidden, width=1024):
     n_col, n_row = len(near), len(hidden)
     _, _, rows, feats = near[0].shape
     n_z, _, share, cols = hidden[0].shape

time: 158 us -> 158 us (level)
  no operation moved by 1% of the time
where the time goes in v6:
time: 158 us; the launch traced here: 157 us
  waiting for transfers between devices  65.9 us (42%)
  starting transfers between devices  48 us (30%)
  Pallas kernels  32.4 us (21%)
  local copies, waits for them, and re-layouts  7.02 us (4%)
  other arithmetic  3.35 us (2%)
    ppermute x9, waiting for transfers between devices, shift_col(): return lax.ppermute(value, 'col', pairs)  44.3 us
    ppermute x12, starting transfers between devices, shift(): lax.ppermute(value, axis, [(i, (i + by) % size) for i in range(size)])  27.4 us
    ppermute x12, waiting for transfers between devices, shift(): lax.ppermute(value, axis, [(i, (i + by) % size) for i in range(size)])  17.6 us
    ppermute x9, starting transfers between devices, shift_col(): return lax.ppermute(value, 'col', pairs)  11.5 us
    pallas_call x1, Pallas kernels, grad(): pl.pallas_call(functools.partial(grad_kernel, n_col, n_row, n_z), grid=(f...  9.91 us
    pallas_call x1, Pallas kernels, down(): pl.pallas_call(functools.partial(down_kernel, n_col, n_row), grid=(feats...  9.03 us
    pallas_call x1, Pallas kernels, up(): pl.pallas_call(functools.partial(up_kernel, n_col, n_row), grid=(cols //...  7.86 us
    all_to_all x1, starting transfers between devices, on_device(): acts = lax.all_to_all(acts, 'row', 0, 0)  4.6 us
  transfers between devices with their start and end apart: 24, of which 8 were waited for; matrix products, arithmetic and copies ran while one was open for 4% of the time, Pallas kernels for 20%

profile of v6, /device:TPU:1, one launch (start us, length us, event | category | flops | bytes accessed | tf_op | source)
XLA Modules:
  0.0 157.5 jit_solution(7848677465459517042)
XLA Ops:
  0.6 1.0 pad_maximum_fusion.4
  1.6 2.6 %collective-permute-start = (bf16[2,32,2048]{2,1,0:T(8,128)(2,1)S(1)}, bf16[2,32,2048]{2,1,0:T(8,128)(2,1)S(1)}, u32[]{:S(2)}, u32[]{:S(2)}) collective-permute-start(bf16[2,32,2048]{2,1,0:T(8,128)(2,1)S(1)} %pad_maximum_fusion.4), channel_id=1, source_target_pairs={{0,4},{1,5},{2,6},{3,7},{4,0},{5,1},{6,2},{7,3},{8,12},{9,13},{10,... | collective-permute-start | bytes 786440 | tf_op jit(solution)/shard_map/ppermute | solution.py:29
  4.2 5.0 %collective-permute-done = bf16[2,32,2048]{2,1,0:T(8,128)(2,1)S(1)} collective-permute-done((bf16[2,32,2048]{2,1,0:T(8,128)(2,1)S(1)}, bf16[2,32,2048]{2,1,0:T(8,128)(2,1)S(1)}, u32[]{:S(2)}, u32[]{:S(2)}) %collective-permute-start) | collective-permute-done | bytes 262176 | tf_op jit(solution)/shard_map/ppermute | solution.py:29
  9.2 0.1 pad_maximum_fusion.2.refs_0_
  9.2 3.5 %collective-permute-start.3 = (bf16[2,2,32,2048]{3,2,1,0:T(8,128)(2,1)S(1)}, bf16[2,2,32,2048]{3,2,1,0:T(8,128)(2,1)S(1)}, u32[]{:S(2)}, u32[]{:S(2)}) collective-permute-start(bf16[2,2,32,2048]{3,2,1,0:T(8,128)(2,1)S(1)} %pad_maximum_fusion.2.refs_0_), channel_id=1, source_target_pairs={{0,3},{1,0},{2,1},{3,2},{4,7},{5,4},{6,5},{7,6},{8,11},{9,8},{10,9... | collective-permute-start | bytes 1572872 | tf_op jit(solution)/shard_map/ppermute | solution.py:29
  12.7 0.5 collective-permute-start.2
  13.2 0.6 collective-permute-start.1
  13.8 5.6 %collective-permute-start.6 = (bf16[2,32,2048]{2,1,0:T(8,128)(2,1)S(1)}, bf16[2,32,2048]{2,1,0:T(8,128)(2,1)S(1)}, u32[]{:S(2)}, u32[]{:S(2)}) collective-permute-start(bf16[2,32,2048]{2,1,0:T(8,128)(2,1)S(1)} %pad_maximum_fusion.4), channel_id=1, source_target_pairs={{0,192},{32,224},{64,0},{96,32},{128,64},{160,96},{192,128},{224,1... | collective-permute-start | bytes 786440 | tf_op jit(solution)/shard_map/ppermute | solution.py:23
  19.5 0.9 collective-permute-start.5
  20.4 3.5 %collective-permute-done.3.refs_3_ = bf16[2,2,32,2048]{3,2,1,0:T(8,128)(2,1)S(1)} collective-permute-done((bf16[2,2,32,2048]{3,2,1,0:T(8,128)(2,1)S(1)}, bf16[2,2,32,2048]{3,2,1,0:T(8,128)(2,1)S(1)}, u32[]{:S(2)}, u32[]{:S(2)}) %collective-permute-start.3) | collective-permute-done | bytes 524320 | tf_op jit(solution)/shard_map/ppermute | solution.py:29
  23.9 2.5 %collective-permute-start.4 = (bf16[2,32,2048]{2,1,0:T(8,128)(2,1)S(1)}, bf16[2,32,2048]{2,1,0:T(8,128)(2,1)S(1)}, u32[]{:S(2)}, u32[]{:S(2)}) collective-permute-start(bf16[2,32,2048]{2,1,0:T(8,128)(2,1)S(1)} %pad_maximum_fusion.4), channel_id=1, source_target_pairs={{0,64},{32,96},{64,128},{96,160},{128,192},{160,224},{192,0},{224,... | collective-permute-start | bytes 786440 | tf_op jit(solution)/shard_map/ppermute | solution.py:23
  26.4 0.1 stack.81.pos_ref
  26.5 12.8 %collective-permute-done.1.refs_1_ = bf16[2,2,32,2048]{3,2,1,0:T(8,128)(2,1)S(1)} collective-permute-done((bf16[2,2,32,2048]{3,2,1,0:T(8,128)(2,1)S(1)}, bf16[2,2,32,2048]{3,2,1,0:T(8,128)(2,1)S(1)}, u32[]{:S(2)}, u32[]{:S(2)}) %collective-permute-start.1) | collective-permute-done | bytes 524320 | tf_op jit(solution)/shard_map/ppermute | solution.py:29
  39.3 0.7 copy-done.7
  40.0 7.9 %up.1 = (f32[2,64,2048]{2,1,0:T(8,128)S(1)}, bf16[2,64,2048]{2,1,0:T(8,128)(2,1)S(1)}, bf16[2,64,2048]{2,1,0:T(8,128)(2,1)S(1)}, bf16[2,64,2048]{2,1,0:T(8,128)(2,1)S(1)}) custom-call(s32[6]{0:T(128)S(1)} %stack.81.pos_ref, s32[8,8]{1,0:T(8,128)S(1)} %copy-done.7, bf16[2,2,32,2048]{3,2,1,0:T(8,128)(2,1)S(1)} %pad_maximum_fusion.2.refs_0_, ...), custom_call_target="tpu_custom_call" | custom-call | flops 1 | bytes 1 | tf_op jit(solution)/shard_map/up/pallas_call | solution.py:80
  47.9 0.1 fusion
  48.1 1.3 collective-permute-start.7
  49.4 1.3 collective-permute-start.8
  50.7 2.6 %collective-permute-start.9 = (bf16[2,64,2048]{2,1,0:T(8,128)(2,1)S(1)}, bf16[2,64,2048]{2,1,0:T(8,128)(2,1)S(1)}, u32[]{:S(2)}, u32[]{:S(2)}) collective-permute-start(bf16[2,64,2048]{2,1,0:T(8,128)(2,1)S(1)} %get-tuple-element.44), channel_id=1, source_target_pairs={{0,16},{8,24},{16,0},{24,8},{1,17},{9,25},{17,1},{25,9},{2,18},{10... | collective-permute-start | bytes 1572872 | tf_op jit(solution)/shard_map/ppermute | solution.py:23
  53.3 1.1 collective-permute-start.10
  54.4 12.3 %collective-permute-done.7 = bf16[3,2,32,2048]{3,2,1,0:T(8,128)(2,1)S(1)} collective-permute-done((bf16[3,2,32,2048]{3,2,1,0:T(8,128)(2,1)S(1)}, bf16[3,2,32,2048]{3,2,1,0:T(8,128)(2,1)S(1)}, u32[]{:S(2)}, u32[]{:S(2)}) %collective-permute-start.7) | collective-permute-done | bytes 786464 | tf_op jit(solution)/shard_map/ppermute | solution.py:29
  66.7 1.3 pad_maximum_fusion.refs_4_
  68.1 1.5 collective-permute-start.11
  69.5 6.0 %collective-permute-done.9.refs_2_ = bf16[2,64,2048]{2,1,0:T(8,128)(2,1)S(1)} collective-permute-done((bf16[2,64,2048]{2,1,0:T(8,128)(2,1)S(1)}, bf16[2,64,2048]{2,1,0:T(8,128)(2,1)S(1)}, u32[]{:S(2)}, u32[]{:S(2)}) %collective-permute-start.9) | collective-permute-done | bytes 524320 | tf_op jit(solution)/shard_map/ppermute | solution.py:23
  75.5 2.6 %act.1 = (bf16[4,2,64,2048]{3,2,1,0:T(8,128)(2,1)}, bf16[2,64,512]{2,1,0:T(8,128)(2,1)S(1)}, bf16[2,64,512]{2,1,0:T(8,128)(2,1)S(1)}, bf16[2,64,512]{2,1,0:T(8,128)(2,1)S(1)}, bf16[2,64,512]{2,1,0:T(8,128)(2,1)S(1)}) custom-call(s32[6]{0:T(128)S(1)} %stack.81.pos_ref, f32[2,64,2048]{2,1,0:T(8,128)S(1)} %get-tuple-element.42.refs_0_, ...), custom_call_target="tpu_custom_call" | custom-call | flops 1 | bytes 1 | tf_op jit(solution)/shard_map/act/pallas_call | solution.py:122
  78.1 4.6 %all-to-all-start = ((bf16[4,2,64,2048]{3,2,1,0:T(8,128)(2,1)}), bf16[4,2,64,2048]{3,2,1,0:T(8,128)(2,1)S(1)}, u32[]{:S(2)}, u32[]{:S(2)}) async-start(bf16[4,2,64,2048]{3,2,1,0:T(8,128)(2,1)} %get-tuple-element.46), calls=%async_computation | async-start | bytes 4194304 | tf_op jit(solution)/shard_map/all_to_all | solution.py:319
  82.7 3.0 %collective-permute-start.15 = (bf16[2,64,512]{2,1,0:T(8,128)(2,1)S(1)}, bf16[2,64,512]{2,1,0:T(8,128)(2,1)S(1)}, u32[]{:S(2)}, u32[]{:S(2)}) collective-permute-start(bf16[2,64,512]{2,1,0:T(8,128)(2,1)S(1)} %get-tuple-element.56), channel_id=1, source_target_pairs={{0,64},{32,96},{64,128},{96,160},{128,192},{160,224},{192,0},{224,... | collective-permute-start | bytes 393224 | tf_op jit(solution)/shard_map/ppermute | solution.py:23
  85.7 4.2 %collective-permute-start.16 = (bf16[2,64,512]{2,1,0:T(8,128)(2,1)S(1)}, bf16[2,64,512]{2,1,0:T(8,128)(2,1)S(1)}, u32[]{:S(2)}, u32[]{:S(2)}) collective-permute-start(bf16[2,64,512]{2,1,0:T(8,128)(2,1)S(1)} %get-tuple-element.57), channel_id=1, source_target_pairs={{0,128},{32,160},{64,192},{96,224},{128,0},{160,32},{192,64},{224,... | collective-permute-start | bytes 393224 | tf_op jit(solution)/shard_map/ppermute | solution.py:23
  89.9 2.4 %collective-permute-start.17 = (bf16[2,64,512]{2,1,0:T(8,128)(2,1)S(1)}, bf16[2,64,512]{2,1,0:T(8,128)(2,1)S(1)}, u32[]{:S(2)}, u32[]{:S(2)}) collective-permute-start(bf16[2,64,512]{2,1,0:T(8,128)(2,1)S(1)} %get-tuple-element.58), channel_id=1, source_target_pairs={{0,192},{32,224},{64,0},{96,32},{128,64},{160,96},{192,128},{224,1... | collective-permute-start | bytes 393224 | tf_op jit(solution)/shard_map/ppermute | solution.py:23
  92.3 10.6 %collective-permute-done.13.refs_7_ = bf16[2,3,2,32,2048]{4,3,2,1,0:T(8,128)(2,1)} collective-permute-done((bf16[2,3,2,32,2048]{4,3,2,1,0:T(8,128)(2,1)}, bf16[2,3,2,32,2048]{4,3,2,1,0:T(8,128)(2,1)}, u32[]{:S(2)}, u32[]{:S(2)}) %collective-permute-start.13) | collective-permute-done | bytes 1572896 | tf_op jit(solution)/shard_map/ppermute | solution.py:29
  102.9 1.2 slice.9
  104.1 1.4 collective-permute-start.14
  105.5 2.1 %slice.8 = bf16[1,3,2,32,2048]{4,3,2,1,0:T(8,128)(2,1)} slice(bf16[2,3,2,32,2048]{4,3,2,1,0:T(8,128)(2,1)} %collective-permute-done.11.refs_5_), slice={[0:1], [0:3], [0:2], [0:32], [0:2048]} | slice | bytes 1572864 | tf_op jit(solution)/shard_map/slice | solution.py:321
  107.6 0.1 collective-permute-start.12
  107.8 0.9 pad_maximum_fusion.3.refs_9_
  108.6 2.8 %collective-permute-start.20 = (bf16[4,2,64,512]{3,2,1,0:T(8,128)(2,1)}, bf16[4,2,64,512]{3,2,1,0:T(8,128)(2,1)S(1)}, u32[]{:S(2)}, u32[]{:S(2)}) collective-permute-start(bf16[4,2,64,512]{3,2,1,0:T(8,128)(2,1)} %pad_maximum_fusion.3.refs_9_), channel_id=1, source_target_pairs={{0,24},{8,0},{16,8},{24,16},{1,25},{9,1},{17,9},{25,17},{2,26},{10... | collective-permute-start | bytes 1572872 | tf_op jit(solution)/shard_map/ppermute | solution.py:23
  111.4 0.3 collective-permute-start.19
  111.8 0.7 collective-permute-start.18
  112.5 1.3 copy-done.11
  113.8 9.0 %down.1 = bf16[8,2,32,2048]{3,2,1,0:T(8,128)(2,1)} custom-call(s32[6]{0:T(128)} %copy-done.9, s32[8,8]{1,0:T(8,128)} %mask_ref.5, bf16[4,2,64,2048]{3,2,1,0:T(8,128)(2,1)} %copy-done.11, bf16[2048,2048]{1,0:T(8,128)(2,1)} %refs_1_.1), custom_call_target="tpu_custom_call" | custom-call | flops 6000000000 | bytes 1 | tf_op jit(solution)/shard_map/down/pallas_call | solution.py:167
  122.8 3.8 %all-to-all-start.1 = ((bf16[8,2,32,2048]{3,2,1,0:T(8,128)(2,1)}), bf16[8,2,32,2048]{3,2,1,0:T(8,128)(2,1)S(1)}, u32[]{:S(2)}, u32[]{:S(2)}) async-start(bf16[8,2,32,2048]{3,2,1,0:T(8,128)(2,1)} %down.1), calls=%async_computation.1 | async-start | bytes 4194304 | tf_op jit(solution)/shard_map/all_to_all | solution.py:328
  126.7 11.6 %collective-permute-done.18.refs_10_ = bf16[4,2,64,512]{3,2,1,0:T(8,128)(2,1)} collective-permute-done((bf16[4,2,64,512]{3,2,1,0:T(8,128)(2,1)}, bf16[4,2,64,512]{3,2,1,0:T(8,128)(2,1)}, u32[]{:S(2)}, u32[]{:S(2)}) %collective-permute-start.18) | collective-permute-done | bytes 524320 | tf_op jit(solution)/shard_map/ppermute | solution.py:23
  138.3 9.9 %grad.1 = (f32[2048,256]{1,0:T(8,128)}, f32[2048,256]{1,0:T(8,128)}) custom-call(s32[6]{0:T(128)} %copy-done.9, bf16[2,2,32,2048]{3,2,1,0:T(8,128)(2,1)} %copy-done, bf16[2,2,32,2048]{3,2,1,0:T(8,128)(2,1)} %copy-done.4, bf16[2,2,32,2048]{3,2,1,0:T(8,128)(2,1)} %copy-done.3, bf16[2,2,32,2048]{3,2,1,0:T(8,128)(2,1)} %copy-done.2, ...), custom_call_target="tpu_custom_call" | custom-call | flops 99999997952 | bytes 1000000000 | tf_op jit(solution)/shard_map/grad/pallas_call | solution.py:226
  148.3 0.6 collective-permute-start.21
  148.8 4.0 %collective-permute-done.21.b_ref = f32[2048,256]{1,0:T(8,128)S(1)} collective-permute-done((f32[2048,256]{1,0:T(8,128)}, f32[2048,256]{1,0:T(8,128)S(1)}, u32[]{:S(2)}, u32[]{:S(2)}) %collective-permute-start.21) | collective-permute-done | bytes 2097184 | tf_op jit(solution)/shard_map/ppermute | solution.py:331
  152.8 1.6 %copy-done.1 = f32[2048,256]{1,0:T(8,128)S(1)} copy-done((f32[2048,256]{1,0:T(8,128)S(1)}, f32[2048,256]{1,0:T(8,128)}, u32[]{:S(2)}) %copy-start.1) | copy-done | bytes 2097176
  154.4 2.1 %finish.1 = f32[4096,128]{1,0:T(8,128)} custom-call(s32[6]{0:T(128)S(1)} %copy-done.10, s32[8,8]{1,0:T(8,128)S(1)} %copy-done.8, f32[2048,256]{1,0:T(8,128)S(1)} %copy-done.1, f32[2048,256]{1,0:T(8,128)S(1)} %collective-permute-done.21.b_ref), custom_call_target="tpu_custom_call" | custom-call | flops 1 | bytes 1 | tf_op jit(solution)/shard_map/finish/pallas_call | solution.py:263
  156.5 1.0 add.12
  (40 shorter events, 0.1 us)
Async XLA Ops:
  1.6 7.5 %collective-permute-start = (bf16[2,32,2048]{2,1,0:T(8,128)(2,1)S(1)}, bf16[2,32,2048]{2,1,0:T(8,128)(2,1)S(1)}, u32[]{:S(2)}, u32[]{:S(2)}) collective-permute-start(bf16[2,32,2048]{2,1,0:T(8,128)(2,1)S(1)} %pad_maximum_fusion.4), channel_id=1, source_target_pairs={{0,4},{1,5},{2,6},{3,7},{4,0},{5,1},{6,2},{7,3},{8,12},{9,13},{10,... | collective-permute-start | bytes 786440 | tf_op jit(solution)/shard_map/ppermute | solution.py:29
  9.2 38.7 %copy-start = (bf16[2,2,32,2048]{3,2,1,0:T(8,128)(2,1)}, bf16[2,2,32,2048]{3,2,1,0:T(8,128)(2,1)S(1)}, u32[]{:S(2)}) copy-start(bf16[2,2,32,2048]{3,2,1,0:T(8,128)(2,1)S(1)} %pad_maximum_fusion.2.refs_0_) | copy-start | bytes 1572868
  9.2 14.7 %collective-permute-start.3 = (bf16[2,2,32,2048]{3,2,1,0:T(8,128)(2,1)S(1)}, bf16[2,2,32,2048]{3,2,1,0:T(8,128)(2,1)S(1)}, u32[]{:S(2)}, u32[]{:S(2)}) collective-permute-start(bf16[2,2,32,2048]{3,2,1,0:T(8,128)(2,1)S(1)} %pad_maximum_fusion.2.refs_0_), channel_id=1, source_target_pairs={{0,3},{1,0},{2,1},{3,2},{4,7},{5,4},{6,5},{7,6},{8,11},{9,8},{10,9... | collective-permute-start | bytes 1572872 | tf_op jit(solution)/shard_map/ppermute | solution.py:29
  12.7 13.7 %collective-permute-start.2 = (bf16[2,2,32,2048]{3,2,1,0:T(8,128)(2,1)S(1)}, bf16[2,2,32,2048]{3,2,1,0:T(8,128)(2,1)S(1)}, u32[]{:S(2)}, u32[]{:S(2)}) collective-permute-start(bf16[2,2,32,2048]{3,2,1,0:T(8,128)(2,1)S(1)} %pad_maximum_fusion.2.refs_0_), channel_id=1, source_target_pairs={{0,2},{1,3},{2,0},{3,1},{4,6},{5,7},{6,4},{7,5},{8,10},{9,11},{10,... | collective-permute-start | bytes 1572872 | tf_op jit(solution)/shard_map/ppermute | solution.py:29
  13.2 26.1 %collective-permute-start.1 = (bf16[2,2,32,2048]{3,2,1,0:T(8,128)(2,1)S(1)}, bf16[2,2,32,2048]{3,2,1,0:T(8,128)(2,1)S(1)}, u32[]{:S(2)}, u32[]{:S(2)}) collective-permute-start(bf16[2,2,32,2048]{3,2,1,0:T(8,128)(2,1)S(1)} %pad_maximum_fusion.2.refs_0_), channel_id=1, source_target_pairs={{0,1},{1,2},{2,3},{3,0},{4,5},{5,6},{6,7},{7,4},{8,9},{9,10},{10,1... | collective-permute-start | bytes 1572872 | tf_op jit(solution)/shard_map/ppermute | solution.py:29
  13.8 34.1 %collective-permute-start.6 = (bf16[2,32,2048]{2,1,0:T(8,128)(2,1)S(1)}, bf16[2,32,2048]{2,1,0:T(8,128)(2,1)S(1)}, u32[]{:S(2)}, u32[]{:S(2)}) collective-permute-start(bf16[2,32,2048]{2,1,0:T(8,128)(2,1)S(1)} %pad_maximum_fusion.4), channel_id=1, source_target_pairs={{0,192},{32,224},{64,0},{96,32},{128,64},{160,96},{192,128},{224,1... | collective-permute-start | bytes 786440 | tf_op jit(solution)/shard_map/ppermute | solution.py:23
  19.5 28.4 %collective-permute-start.5 = (bf16[2,32,2048]{2,1,0:T(8,128)(2,1)S(1)}, bf16[2,32,2048]{2,1,0:T(8,128)(2,1)S(1)}, u32[]{:S(2)}, u32[]{:S(2)}) collective-permute-start(bf16[2,32,2048]{2,1,0:T(8,128)(2,1)S(1)} %pad_maximum_fusion.4), channel_id=1, source_target_pairs={{0,128},{32,160},{64,192},{96,224},{128,0},{160,32},{192,64},{224,... | collective-permute-start | bytes 786440 | tf_op jit(solution)/shard_map/ppermute | solution.py:23
  23.9 24.0 %copy-start.2 = (bf16[2,2,32,2048]{3,2,1,0:T(8,128)(2,1)}, bf16[2,2,32,2048]{3,2,1,0:T(8,128)(2,1)S(1)}, u32[]{:S(2)}) copy-start(bf16[2,2,32,2048]{3,2,1,0:T(8,128)(2,1)S(1)} %collective-permute-done.3.refs_3_) | copy-start | bytes 1572868
  23.9 24.0 %collective-permute-start.4 = (bf16[2,32,2048]{2,1,0:T(8,128)(2,1)S(1)}, bf16[2,32,2048]{2,1,0:T(8,128)(2,1)S(1)}, u32[]{:S(2)}, u32[]{:S(2)}) collective-permute-start(bf16[2,32,2048]{2,1,0:T(8,128)(2,1)S(1)} %pad_maximum_fusion.4), channel_id=1, source_target_pairs={{0,64},{32,96},{64,128},{96,160},{128,192},{160,224},{192,0},{224,... | collective-permute-start | bytes 786440 | tf_op jit(solution)/shard_map/ppermute | solution.py:23
  26.5 49.1 %copy-start.9 = (s32[6]{0:T(128)}, s32[6]{0:T(128)S(1)}, u32[]{:S(2)}) copy-start(s32[6]{0:T(128)S(1)} %stack.81.pos_ref) | copy-start | bytes 76
  26.5 21.4 %copy-start.3 = (bf16[2,2,32,2048]{3,2,1,0:T(8,128)(2,1)}, bf16[2,2,32,2048]{3,2,1,0:T(8,128)(2,1)S(1)}, u32[]{:S(2)}) copy-start(bf16[2,2,32,2048]{3,2,1,0:T(8,128)(2,1)S(1)} %collective-permute-done.2.refs_2_) | copy-start | bytes 1572868
  39.3 0.7 copy-start.7
  40.0 7.9 %copy-start.4 = (bf16[2,2,32,2048]{3,2,1,0:T(8,128)(2,1)}, bf16[2,2,32,2048]{3,2,1,0:T(8,128)(2,1)S(1)}, u32[]{:S(2)}) copy-start(bf16[2,2,32,2048]{3,2,1,0:T(8,128)(2,1)S(1)} %collective-permute-done.1.refs_1_) | copy-start | bytes 1572868
  48.1 18.7 %collective-permute-start.7 = (bf16[3,2,32,2048]{3,2,1,0:T(8,128)(2,1)S(1)}, bf16[3,2,32,2048]{3,2,1,0:T(8,128)(2,1)S(1)}, u32[]{:S(2)}, u32[]{:S(2)}) collective-permute-start(bf16[3,2,32,2048]{3,2,1,0:T(8,128)(2,1)S(1)} %get-tuple-element.65), channel_id=1, source_target_pairs={{0,4},{1,5},{2,6},{3,7},{4,0},{5,1},{6,2},{7,3},{8,12},{9,13},{10,... | collective-permute-start | bytes 2359304 | tf_op jit(solution)/shard_map/ppermute | solution.py:29
  49.4 20.1 %collective-permute-start.8 = (bf16[2,64,2048]{2,1,0:T(8,128)(2,1)S(1)}, bf16[2,64,2048]{2,1,0:T(8,128)(2,1)S(1)}, u32[]{:S(2)}, u32[]{:S(2)}) collective-permute-start(bf16[2,64,2048]{2,1,0:T(8,128)(2,1)S(1)} %get-tuple-element.43), channel_id=1, source_target_pairs={{0,8},{8,16},{16,24},{24,0},{1,9},{9,17},{17,25},{25,1},{2,10},{10... | collective-permute-start | bytes 1572872 | tf_op jit(solution)/shard_map/ppermute | solution.py:23
  50.7 24.8 %collective-permute-start.9 = (bf16[2,64,2048]{2,1,0:T(8,128)(2,1)S(1)}, bf16[2,64,2048]{2,1,0:T(8,128)(2,1)S(1)}, u32[]{:S(2)}, u32[]{:S(2)}) collective-permute-start(bf16[2,64,2048]{2,1,0:T(8,128)(2,1)S(1)} %get-tuple-element.44), channel_id=1, source_target_pairs={{0,16},{8,24},{16,0},{24,8},{1,17},{9,25},{17,1},{25,9},{2,18},{10... | collective-permute-start | bytes 1572872 | tf_op jit(solution)/shard_map/ppermute | solution.py:23
  53.3 22.2 %collective-permute-start.10 = (bf16[2,64,2048]{2,1,0:T(8,128)(2,1)S(1)}, bf16[2,64,2048]{2,1,0:T(8,128)(2,1)S(1)}, u32[]{:S(2)}, u32[]{:S(2)}) collective-permute-start(bf16[2,64,2048]{2,1,0:T(8,128)(2,1)S(1)} %get-tuple-element.45), channel_id=1, source_target_pairs={{0,24},{8,0},{16,8},{24,16},{1,25},{9,1},{17,9},{25,17},{2,26},{10... | collective-permute-start | bytes 1572872 | tf_op jit(solution)/shard_map/ppermute | solution.py:23
  68.1 34.8 %collective-permute-start.13 = (bf16[2,3,2,32,2048]{4,3,2,1,0:T(8,128)(2,1)}, bf16[2,3,2,32,2048]{4,3,2,1,0:T(8,128)(2,1)}, u32[]{:S(2)}, u32[]{:S(2)}) collective-permute-start(bf16[2,3,2,32,2048]{4,3,2,1,0:T(8,128)(2,1)} %pad_maximum_fusion.refs_4_), channel_id=1, source_target_pairs={{0,3},{1,0},{2,1},{3,2},{4,7},{5,4},{6,5},{7,6},{8,11},{9,8},{10,9... | collective-permute-start | bytes 4718600 | tf_op jit(solution)/shard_map/ppermute | solution.py:29
  68.1 37.5 %collective-permute-start.11 = (bf16[2,3,2,32,2048]{4,3,2,1,0:T(8,128)(2,1)}, bf16[2,3,2,32,2048]{4,3,2,1,0:T(8,128)(2,1)}, u32[]{:S(2)}, u32[]{:S(2)}) collective-permute-start(bf16[2,3,2,32,2048]{4,3,2,1,0:T(8,128)(2,1)} %pad_maximum_fusion.refs_4_), channel_id=1, source_target_pairs={{0,1},{1,2},{2,3},{3,0},{4,5},{5,6},{6,7},{7,4},{8,9},{9,10},{10,1... | collective-permute-start | bytes 4718600 | tf_op jit(solution)/shard_map/ppermute | solution.py:29
  78.1 34.4 %all-to-all-start = ((bf16[4,2,64,2048]{3,2,1,0:T(8,128)(2,1)}), bf16[4,2,64,2048]{3,2,1,0:T(8,128)(2,1)S(1)}, u32[]{:S(2)}, u32[]{:S(2)}) async-start(bf16[4,2,64,2048]{3,2,1,0:T(8,128)(2,1)} %get-tuple-element.46), calls=%async_computation | async-start | bytes 4194304 | tf_op jit(solution)/shard_map/all_to_all | solution.py:319
  82.7 25.1 %collective-permute-start.15 = (bf16[2,64,512]{2,1,0:T(8,128)(2,1)S(1)}, bf16[2,64,512]{2,1,0:T(8,128)(2,1)S(1)}, u32[]{:S(2)}, u32[]{:S(2)}) collective-permute-start(bf16[2,64,512]{2,1,0:T(8,128)(2,1)S(1)} %get-tuple-element.56), channel_id=1, source_target_pairs={{0,64},{32,96},{64,128},{96,160},{128,192},{160,224},{192,0},{224,... | collective-permute-start | bytes 393224 | tf_op jit(solution)/shard_map/ppermute | solution.py:23
  85.7 22.1 %collective-permute-start.16 = (bf16[2,64,512]{2,1,0:T(8,128)(2,1)S(1)}, bf16[2,64,512]{2,1,0:T(8,128)(2,1)S(1)}, u32[]{:S(2)}, u32[]{:S(2)}) collective-permute-start(bf16[2,64,512]{2,1,0:T(8,128)(2,1)S(1)} %get-tuple-element.57), channel_id=1, source_target_pairs={{0,128},{32,160},{64,192},{96,224},{128,0},{160,32},{192,64},{224,... | collective-permute-start | bytes 393224 | tf_op jit(solution)/shard_map/ppermute | solution.py:23
  89.9 17.9 %collective-permute-start.17 = (bf16[2,64,512]{2,1,0:T(8,128)(2,1)S(1)}, bf16[2,64,512]{2,1,0:T(8,128)(2,1)S(1)}, u32[]{:S(2)}, u32[]{:S(2)}) collective-permute-start(bf16[2,64,512]{2,1,0:T(8,128)(2,1)S(1)} %get-tuple-element.58), channel_id=1, source_target_pairs={{0,192},{32,224},{64,0},{96,32},{128,64},{160,96},{192,128},{224,1... | collective-permute-start | bytes 393224 | tf_op jit(solution)/shard_map/ppermute | solution.py:23
  104.1 34.2 %collective-permute-start.14 = (bf16[1,3,2,32,2048]{4,3,2,1,0:T(8,128)(2,1)S(1)}, bf16[1,3,2,32,2048]{4,3,2,1,0:T(8,128)(2,1)}, u32[]{:S(2)}, u32[]{:S(2)}) collective-permute-start(bf16[1,3,2,32,2048]{4,3,2,1,0:T(8,128)(2,1)S(1)} %slice.9), channel_id=1, source_target_pairs={{0,3},{1,0},{2,1},{3,2},{4,7},{5,4},{6,5},{7,6},{8,11},{9,8},{10,9... | collective-permute-start | bytes 2359304 | tf_op jit(solution)/shard_map/ppermute | solution.py:29
  107.6 30.7 %collective-permute-start.12 = (bf16[1,3,2,32,2048]{4,3,2,1,0:T(8,128)(2,1)}, bf16[1,3,2,32,2048]{4,3,2,1,0:T(8,128)(2,1)}, u32[]{:S(2)}, u32[]{:S(2)}) collective-permute-start(bf16[1,3,2,32,2048]{4,3,2,1,0:T(8,128)(2,1)} %slice.8), channel_id=1, source_target_pairs={{0,1},{1,2},{2,3},{3,0},{4,5},{5,6},{6,7},{7,4},{8,9},{9,10},{10,1... | collective-permute-start | bytes 2359304 | tf_op jit(solution)/shard_map/ppermute | solution.py:29
  108.6 18.0 %collective-permute-start.20 = (bf16[4,2,64,512]{3,2,1,0:T(8,128)(2,1)}, bf16[4,2,64,512]{3,2,1,0:T(8,128)(2,1)S(1)}, u32[]{:S(2)}, u32[]{:S(2)}) collective-permute-start(bf16[4,2,64,512]{3,2,1,0:T(8,128)(2,1)} %pad_maximum_fusion.3.refs_9_), channel_id=1, source_target_pairs={{0,24},{8,0},{16,8},{24,16},{1,25},{9,1},{17,9},{25,17},{2,26},{10... | collective-permute-start | bytes 1572872 | tf_op jit(solution)/shard_map/ppermute | solution.py:23
  111.4 15.3 %collective-permute-start.19 = (bf16[4,2,64,512]{3,2,1,0:T(8,128)(2,1)}, bf16[4,2,64,512]{3,2,1,0:T(8,128)(2,1)}, u32[]{:S(2)}, u32[]{:S(2)}) collective-permute-start(bf16[4,2,64,512]{3,2,1,0:T(8,128)(2,1)} %pad_maximum_fusion.3.refs_9_), channel_id=1, source_target_pairs={{0,16},{8,24},{16,0},{24,8},{1,17},{9,25},{17,1},{25,9},{2,18},{10... | collective-permute-start | bytes 1572872 | tf_op jit(solution)/shard_map/ppermute | solution.py:23
  111.8 26.6 %collective-permute-start.18 = (bf16[4,2,64,512]{3,2,1,0:T(8,128)(2,1)}, bf16[4,2,64,512]{3,2,1,0:T(8,128)(2,1)}, u32[]{:S(2)}, u32[]{:S(2)}) collective-permute-start(bf16[4,2,64,512]{3,2,1,0:T(8,128)(2,1)} %pad_maximum_fusion.3.refs_9_), channel_id=1, source_target_pairs={{0,8},{8,16},{16,24},{24,0},{1,9},{9,17},{17,25},{25,1},{2,10},{10... | collective-permute-start | bytes 1572872 | tf_op jit(solution)/shard_map/ppermute | solution.py:23
  112.5 1.3 copy-start.11
  122.8 33.7 %all-to-all-start.1 = ((bf16[8,2,32,2048]{3,2,1,0:T(8,128)(2,1)}), bf16[8,2,32,2048]{3,2,1,0:T(8,128)(2,1)S(1)}, u32[]{:S(2)}, u32[]{:S(2)}) async-start(bf16[8,2,32,2048]{3,2,1,0:T(8,128)(2,1)} %down.1), calls=%async_computation.1 | async-start | bytes 4194304 | tf_op jit(solution)/shard_map/all_to_all | solution.py:328
  126.7 26.2 %copy-start.8 = (s32[8,8]{1,0:T(8,128)S(1)}, s32[8,8]{1,0:T(8,128)}, u32[]{:S(2)}) copy-start(s32[8,8]{1,0:T(8,128)} %mask_ref.5) | copy-start | bytes 772
  126.7 26.2 %copy-start.10 = (s32[6]{0:T(128)S(1)}, s32[6]{0:T(128)}, u32[]{:S(2)}) copy-start(s32[6]{0:T(128)} %copy-done.9) | copy-start | bytes 76
  126.7 11.6 %copy-start.12 = (bf16[4,2,64,512]{3,2,1,0:T(8,128)(2,1)}, bf16[4,2,64,512]{3,2,1,0:T(8,128)(2,1)S(1)}, u32[]{:S(2)}) copy-start(bf16[4,2,64,512]{3,2,1,0:T(8,128)(2,1)S(1)} %collective-permute-done.20.refs_12_) | copy-start | bytes 1572868
  148.3 4.6 %collective-permute-start.21 = (f32[2048,256]{1,0:T(8,128)}, f32[2048,256]{1,0:T(8,128)S(1)}, u32[]{:S(2)}, u32[]{:S(2)}) collective-permute-start(f32[2048,256]{1,0:T(8,128)} %get-tuple-element.60), channel_id=1, source_target_pairs={{0,32},{32,0},{64,96},{96,64},{128,160},{160,128},{192,224},{224,1... | collective-permute-start | bytes 6291464 | tf_op jit(solution)/shard_map/ppermute | solution.py:331
  152.8 1.6 %copy-start.1 = (f32[2048,256]{1,0:T(8,128)S(1)}, f32[2048,256]{1,0:T(8,128)}, u32[]{:S(2)}) copy-start(f32[2048,256]{1,0:T(8,128)} %get-tuple-element.59.a_ref) | copy-start | bytes 6291460
  154.4 2.1 %copy-start.5 = (bf16[32,2048]{1,0:T(8,128)(2,1)S(1)}, bf16[32,2048]{1,0:T(8,128)(2,1)}, u32[]{:S(2)}) copy-start(bf16[32,2048]{1,0:T(8,128)(2,1)} %cot_ref.1) | copy-start | bytes 393220
  154.4 2.1 %copy-start.6 = (bf16[32,2048]{1,0:T(8,128)(2,1)S(1)}, bf16[32,2048]{1,0:T(8,128)(2,1)}, u32[]{:S(2)}) copy-start(bf16[32,2048]{1,0:T(8,128)(2,1)} %tok_ref.1) | copy-start | bytes 393220
